TPU v7x, 256 devices: a whole 4x4x8 slice. The times are simulated.
256 devices in a mesh: dp: 4 (over x_lo, core), uly: 4 (over y), blk: 16 (over z, x_hi).
Axes of the slice: x: 4 (x_hi: 2, x_lo: 2; x = x_hi * 2 + x_lo), y: 4, z: 8, core: 2. Of those that a mesh axis runs over, the one named last changes fastest.
Arguments:
- q_tok: bfloat16 [4, 8192, 1536], P('dp', ('blk', 'uly')), may hold values from -5 to 5
- k_tok: bfloat16 [4, 8192, 1536], P('dp', ('blk', 'uly')), may hold values from -5 to 5
- v_tok: bfloat16 [4, 8192, 1536], P('dp', ('blk', 'uly')), may hold values from -6 to 6
- d_y: bfloat16 [4, 8192, 3072], P('dp', ('blk', 'uly')), may hold values from -8 to 8
- gate: float32 [4, 3072], P('dp'), may hold values from 0.3 to 3
- w_out: bfloat16 [3072, 1536], P('blk', 'uly'), may hold values from -0.15625 to 0.15625
Outputs:
- grad_q: bfloat16 [4, 8192, 1536], P('dp', ('blk', 'uly'))
- grad_k: bfloat16 [4, 8192, 1536], P('dp', ('blk', 'uly'))
- grad_v: bfloat16 [4, 8192, 1536], P('dp', ('blk', 'uly'))
- grad_w: float32 [3072, 1536], P('blk', 'uly')
All inputs are finite; a program needn't handle non-finite values.
Results may differ from a plain program's by a relative error of at most 0.022.
Values may be sent and summed in bfloat16 or wider, within the bound.
No kernel may reach another device: no remote copies, remote signals or barrier semaphores. Data moves between devices by JAX's collectives and lax.ppermute only.
A program may use at most 64 MiB of HBM per device.

v0:
```python
import math

import jax
import jax.numpy as jnp
from jax import lax
from jax.sharding import PartitionSpec as P

HDIM = 128


def from_behind(block, axis, distance):
    devices = range(lax.axis_size(axis))
    route = [((i - distance) % len(devices), i) for i in devices]
    return lax.ppermute(block, axis, route)


def shortened(x):
    return jax.tree.map(lambda a: a.astype(jnp.bfloat16) if a.dtype == jnp.float32 else a, x)


def head_columns(array, head_index):
    return array[:, head_index * HDIM : (head_index + 1) * HDIM]


def shards(q_tok, k_tok, v_tok, d_y, gate, w_out):
    softmax_scale = HDIM ** (-0.5)
    head_width = w_out.shape[1]
    heads_here = head_width // HDIM
    scaled = (d_y.astype(jnp.float32) * gate[:, None, :]).astype(jnp.bfloat16)
    q_head, k_head, v_head = (
        lax.all_to_all(q_tok, "uly", split_axis=2, concat_axis=1, tiled=True),
        lax.all_to_all(k_tok, "uly", split_axis=2, concat_axis=1, tiled=True),
        lax.all_to_all(v_tok, "uly", split_axis=2, concat_axis=1, tiled=True),
    )
    everyone = lax.all_gather(scaled, "uly", axis=1, tiled=True)[0]
    block_tokens = everyone.shape[0]
    columns = everyone
    attn_grad = jnp.dot(
        columns,
        lax.all_gather(w_out, "blk", axis=0, tiled=True),
        preferred_element_type=jnp.float32,
    ).astype(jnp.bfloat16)
    key_prior, value_prior = from_behind((k_head[0], v_head[0]), "blk", 1)
    key_cat = jnp.concatenate([key_prior, k_head[0]], axis=0)
    value_cat = jnp.concatenate([value_prior, v_head[0]], axis=0)
    row_block = math.gcd(block_tokens, 512)
    row_count = block_tokens // row_block
    q_blocks = q_head[0].reshape(row_count, row_block, head_width)
    g_blocks = attn_grad.reshape(row_count, row_block, head_width)
    across = (((1,), (1,)), ((), ()))
    down = (((0,), (0,)), ((), ()))

    def row_step(carry, inputs):
        key_total, value_total = carry
        q_rows, g_rows = inputs
        grads, outputs, key_parts, value_parts = ([], [], [], [])
        for head_index in range(heads_here):
            q_part = head_columns(q_rows, head_index)
            k_part = head_columns(key_cat, head_index)
            v_part = head_columns(value_cat, head_index)
            g_part = head_columns(g_rows, head_index)
            scores = (
                lax.dot_general(q_part, k_part, across, preferred_element_type=jnp.float32)
                * softmax_scale
            )
            expo = jnp.exp(scores - jnp.max(scores, axis=1, keepdims=True))
            probs = expo / jnp.sum(expo, axis=1, keepdims=True)
            probs_half = probs.astype(jnp.bfloat16)
            attended = jnp.dot(probs_half, v_part, preferred_element_type=jnp.float32).astype(
                jnp.bfloat16
            )
            attended_wide = lax.optimization_barrier(attended).astype(jnp.float32)
            delta = jnp.sum(g_part.astype(jnp.float32) * attended_wide, axis=1, keepdims=True)
            prob_grad = lax.dot_general(g_part, v_part, across, preferred_element_type=jnp.float32)
            score_grad = (probs * (prob_grad - delta)).astype(jnp.bfloat16)
            grads.append(
                (
                    jnp.dot(score_grad, k_part, preferred_element_type=jnp.float32) * softmax_scale
                ).astype(jnp.bfloat16)
            )
            outputs.append(attended)
            key_parts.append(
                lax.dot_general(score_grad, q_part, down, preferred_element_type=jnp.float32)
                * softmax_scale
            )
            value_parts.append(
                lax.dot_general(probs_half, g_part, down, preferred_element_type=jnp.float32)
            )
        new_carry = (
            key_total + jnp.concatenate(key_parts, axis=1),
            value_total + jnp.concatenate(value_parts, axis=1),
        )
        return (new_carry, (jnp.concatenate(grads, axis=1), jnp.concatenate(outputs, axis=1)))

    empty = jnp.zeros((2 * block_tokens, head_width), jnp.float32)
    (key_total, value_total), (grad_rows, attended_rows) = lax.scan(
        row_step, (empty, empty), (q_blocks, g_blocks)
    )
    grad_q = grad_rows.reshape(block_tokens, head_width)
    attended_all = attended_rows.reshape(block_tokens, head_width)
    key_after, value_after = (
        from_behind(key_total[:block_tokens].astype(jnp.bfloat16), "blk", -1).astype(jnp.float32),
        from_behind(value_total[:block_tokens].astype(jnp.bfloat16), "blk", -1).astype(jnp.float32),
    )
    grad_k = (key_total[block_tokens:] + key_after).astype(jnp.bfloat16)
    grad_v = (value_total[block_tokens:] + value_after).astype(jnp.bfloat16)
    q_back, k_back, v_back = (
        lax.all_to_all(shortened(grad_q[None]), "uly", split_axis=1, concat_axis=2, tiled=True),
        lax.all_to_all(grad_k[None], "uly", split_axis=1, concat_axis=2, tiled=True),
        lax.all_to_all(grad_v[None], "uly", split_axis=1, concat_axis=2, tiled=True),
    )
    columns = everyone
    shard = lax.psum_scatter(
        lax.dot_general(columns, attended_all, down, preferred_element_type=jnp.float32).astype(
            jnp.bfloat16
        ),
        "blk",
        scatter_dimension=0,
        tiled=True,
    )
    grad_w = lax.psum(shard, "dp").astype(jnp.float32)
    return (q_back, k_back, v_back, grad_w)


def solution(mesh):
    return jax.shard_map(
        shards,
        mesh=mesh,
        in_specs=(
            P("dp", ("blk", "uly"), None),
            P("dp", ("blk", "uly"), None),
            P("dp", ("blk", "uly"), None),
            P("dp", ("blk", "uly"), None),
            P("dp", None),
            P("blk", "uly"),
        ),
        out_specs=(
            P("dp", ("blk", "uly"), None),
            P("dp", ("blk", "uly"), None),
            P("dp", ("blk", "uly"), None),
            P("blk", "uly"),
        ),
        check_vma=False,
    )
```

profile of v0, /device:TPU:1, one launch (start us, length us, event | category | flops | bytes accessed | tf_op | source)
XLA Modules:
  0.0 421.6 jit_solution(4970577312891578452)
XLA Ops:
  7.2 2.2 multiply_convert_fusion
  11.4 8.8 %reduce.8 = bf16[1536,128]{1,0:T(8,128)(2,1)S(1)} reduce(bf16[1536,1,128]{2,1,0:T(2,128)(2,1)S(1)} %bitcast.91, bf16[]{:T(256)} %broadcast.75), dimensions={1}, to_apply=%bitcast.63.reduce_sub_computation | reduce | bytes 786434
  21.0 5.0 %all-to-all-start = ((bf16[4,2,24576]{2,1,0:T(2,128)(2,1)}), bf16[4,2,24576]{2,1,0:T(2,128)(2,1)S(1)}, u32[]{:S(2)}, u32[]{:S(2)}) async-start(bf16[4,2,24576]{2,1,0:T(2,128)(2,1)} %reshape.32), calls=%async_computation | async-start | bytes 786432 | tf_op jit(solution)/shard_map/all_to_all | solution.py:32
  26.6 8.8 %reduce.7 = bf16[1536,128]{1,0:T(8,128)(2,1)S(1)} reduce(bf16[1536,1,128]{2,1,0:T(2,128)(2,1)S(1)} %bitcast.101, bf16[]{:T(256)} %broadcast.75), dimensions={1}, to_apply=%bitcast.61.reduce_sub_computation | reduce | bytes 786434
  37.6 3.5 all-to-all-start.1
  41.8 3.8 collective-permute-start
  46.1 8.8 %reduce.6 = bf16[1536,128]{1,0:T(8,128)(2,1)S(1)} reduce(bf16[1536,1,128]{2,1,0:T(2,128)(2,1)S(1)} %bitcast.102, bf16[]{:T(256)} %broadcast.75), dimensions={1}, to_apply=%bitcast.59.reduce_sub_computation | reduce | bytes 786434
  55.8 4.2 all-to-all-start.2
  60.6 5.5 %all-to-all-done.2 = bf16[4,2,24576]{2,1,0:T(2,128)(2,1)S(1)} async-done(((bf16[4,2,24576]{2,1,0:T(2,128)(2,1)}), bf16[4,2,24576]{2,1,0:T(2,128)(2,1)S(1)}, u32[]{:S(2)}, u32[]{:S(2)}) %all-to-all-start.2) | async-done | bytes 393248 | tf_op jit(solution)/shard_map/all_to_all | solution.py:33
  67.6 2.6 collective-permute-start.1
  71.0 8.3 %collective-permute-done.1 = bf16[512,384]{1,0:T(8,128)(2,1)S(1)} collective-permute-done((bf16[512,384]{1,0:T(8,128)(2,1)}, bf16[512,384]{1,0:T(8,128)(2,1)S(1)}, u32[]{:S(2)}, u32[]{:S(2)}) %collective-permute-start.1) | collective-permute-done | bytes 393248 | tf_op jit(solution)/shard_map/ppermute | solution.py:14
  79.3 1.6 convolution_convert_fusion.1
  86.4 2.1 convolution_convert_fusion.3
  88.5 5.2 %convolution_convert_fusion = bf16[3072,384]{1,0:T(8,128)(2,1)} fusion(bf16[1,512,3072]{2,1,0:T(8,128)(2,1)} %all-gather.3.cloned.1.call-done, bf16[512,128]{0,1:T(8,128)(2,1)S(1)} %convolution_convert_fusion.1, bf16[512,128]{0,1:T(8,128)(2,1)S(1)} %convolution_convert_fusion.2, bf16[512,128]{0,1:T(8,128)(2,1)} %convolution_convert_fusion.3), kind=kOutput, calls=%fused_computation | convolution fusion | flops 1210318848 | bytes 5898240 | tf_op jit(solution)/shard_map/dot_general | solution.py:114
  93.7 57.8 %all-gather.5.cloned.1.call-done = bf16[3072,384]{1,0:T(8,128)(2,1)} async-done(((bf16[192,384]{1,0:T(8,128)(2,1)}), bf16[3072,384]{1,0:T(8,128)(2,1)}) %all-gather.5.cloned.1.call-update) | async-done | bytes 2359312 | tf_op jit(solution)/shard_map/all_gather | solution.py:40
  151.6 4.2 fusion.12
  159.7 1.9 collective-permute-start.3
  161.8 1.5 fusion.5
  163.8 1.5 fusion.4
  168.8 2.7 collective-permute-start.2
  172.6 1.8 copy.70
  174.4 3.9 reduce.9
  179.2 4.0 all-to-all-start.3
  183.2 1.9 fusion.24
  185.1 2.5 copy.74
  187.6 3.0 reduce.11
  191.5 4.4 %all-to-all-start.5 = ((bf16[4,2,24576]{2,1,0:T(2,128)(2,1)}), bf16[4,2,24576]{2,1,0:T(2,128)(2,1)S(1)}, u32[]{:S(2)}, u32[]{:S(2)}) async-start(bf16[4,2,24576]{2,1,0:T(2,128)(2,1)} %reshape.38), calls=%async_computation.5 | async-start | bytes 786432 | tf_op jit(solution)/shard_map/all_to_all | solution.py:110
  198.1 3.0 reduce.10
  202.5 3.7 all-to-all-start.4
  206.2 161.0 %reduce-scatter.2.cloned.1.call-done = bf16[192,384]{1,0:T(8,128)(2,1)} async-done(((bf16[3072,384]{1,0:T(8,128)(2,1)}), bf16[192,384]{1,0:T(8,128)(2,1)}) %reduce-scatter.2.cloned.1.call-update) | async-done | bytes 147472 | tf_op jit(solution)/shard_map/reduce_scatter | solution.py:113
  372.3 40.9 %all-reduce.2.cloned.1.call-done = bf16[192,384]{1,0:T(8,128)(2,1)} async-done(((bf16[192,384]{1,0:T(8,128)(2,1)}), bf16[192,384]{1,0:T(8,128)(2,1)}) %all-reduce.2.cloned.1.call-update) | async-done | bytes 147472 | tf_op jit(solution)/shard_map/psum | solution.py:121
  413.2 1.6 convert_element_type.127
  (105 shorter events, 35.2 us)
Async XLA Ops:
  7.2 3.1 copy-start.6
  7.2 81.3 %all-gather.3.cloned.1.call-start = ((), (), s32[]{:S(2)}) async-start(), calls=%async_computation.7 | async-start | bytes 3932160 | tf_op jit(solution)/shard_map/all_gather | solution.py:35
  9.5 16.6 %copy-start.7 = (bf16[1,128,1536]{2,1,0:T(8,128)(2,1)S(1)}, bf16[1,128,1536]{2,1,0:T(8,128)(2,1)}, u32[]{:S(2)}) copy-start(bf16[1,128,1536]{2,1,0:T(8,128)(2,1)} %param.6) | copy-start | bytes 1179652
  9.5 142.1 %all-gather.5.cloned.1.call-start = ((), (), s32[]{:S(2)}) async-start(), calls=%async_computation.8 | async-start | bytes 2506752 | tf_op jit(solution)/shard_map/all_gather | solution.py:40
  21.0 16.6 %all-to-all-start = ((bf16[4,2,24576]{2,1,0:T(2,128)(2,1)}), bf16[4,2,24576]{2,1,0:T(2,128)(2,1)S(1)}, u32[]{:S(2)}, u32[]{:S(2)}) async-start(bf16[4,2,24576]{2,1,0:T(2,128)(2,1)} %reshape.32), calls=%async_computation | async-start | bytes 786432 | tf_op jit(solution)/shard_map/all_to_all | solution.py:32
  36.2 9.3 %copy-start.8 = (bf16[1,128,1536]{2,1,0:T(8,128)(2,1)S(1)}, bf16[1,128,1536]{2,1,0:T(8,128)(2,1)}, u32[]{:S(2)}) copy-start(bf16[1,128,1536]{2,1,0:T(8,128)(2,1)} %param.8) | copy-start | bytes 1179652
  37.6 18.1 %all-to-all-start.1 = ((bf16[4,2,24576]{2,1,0:T(2,128)(2,1)}), bf16[4,2,24576]{2,1,0:T(2,128)(2,1)S(1)}, u32[]{:S(2)}, u32[]{:S(2)}) async-start(bf16[4,2,24576]{2,1,0:T(2,128)(2,1)} %reshape.30), calls=%async_computation.1 | async-start | bytes 786432 | tf_op jit(solution)/shard_map/all_to_all | solution.py:31
  41.8 28.3 %collective-permute-start = (bf16[512,384]{1,0:T(8,128)(2,1)S(1)}, bf16[512,384]{1,0:T(8,128)(2,1)S(1)}, u32[]{:S(2)}, u32[]{:S(2)}) collective-permute-start(bf16[512,384]{1,0:T(8,128)(2,1)S(1)} %bitcast.78), channel_id=1, source_target_pairs={{15,0},{0,1},{1,2},{2,3},{3,4},{4,5},{5,6},{6,7},{7,8},{8,9},{9,10... | collective-permute-start | bytes 1179656 | tf_op jit(solution)/shard_map/ppermute | solution.py:14
  55.8 10.4 %all-to-all-start.2 = ((bf16[4,2,24576]{2,1,0:T(2,128)(2,1)}), bf16[4,2,24576]{2,1,0:T(2,128)(2,1)S(1)}, u32[]{:S(2)}, u32[]{:S(2)}) async-start(bf16[4,2,24576]{2,1,0:T(2,128)(2,1)} %reshape.28), calls=%async_computation.2 | async-start | bytes 786432 | tf_op jit(solution)/shard_map/all_to_all | solution.py:33
  59.9 307.3 %reduce-scatter.2.cloned.1.call-start = ((), (), s32[]{:S(2)}) async-start(), calls=%async_computation.9 | async-start | bytes 2506752 | tf_op jit(solution)/shard_map/reduce_scatter | solution.py:113
  67.6 11.7 %collective-permute-start.1 = (bf16[512,384]{1,0:T(8,128)(2,1)}, bf16[512,384]{1,0:T(8,128)(2,1)S(1)}, u32[]{:S(2)}, u32[]{:S(2)}) collective-permute-start(bf16[512,384]{1,0:T(8,128)(2,1)} %bitcast.8), channel_id=1, source_target_pairs={{15,0},{0,1},{1,2},{2,3},{3,4},{4,5},{5,6},{6,7},{7,8},{8,9},{9,10... | collective-permute-start | bytes 1179656 | tf_op jit(solution)/shard_map/ppermute | solution.py:14
  79.3 5.7 %copy-start.14 = (bf16[512,384]{1,0:T(8,128)(2,1)}, bf16[512,384]{1,0:T(8,128)(2,1)S(1)}, u32[]{:S(2)}) copy-start(bf16[512,384]{1,0:T(8,128)(2,1)S(1)} %collective-permute-done.1) | copy-start | bytes 1179652
  81.3 2.8 copy-start
  81.7 0.9 copy-start.10
  84.5 1.3 copy-start.2
  85.8 0.5 copy-start.12
  151.6 4.2 copy-start.3
  151.6 4.2 copy-start.13
  155.8 1.6 copy-start.1
  155.8 1.6 copy-start.11
  158.6 3.0 copy-start.9
  158.6 3.2 copy-start.15
  158.8 4.5 %copy-start.4 = (f32[1024,384]{0,1:T(8,128)}, f32[1024,384]{0,1:T(8,128)S(1)}, u32[]{:S(2)}) copy-start(f32[1024,384]{0,1:T(8,128)S(1)} %pad_maximum_fusion.1) | copy-start | bytes 4718596
  159.7 23.5 %collective-permute-start.3 = (bf16[512,384]{0,1:T(8,128)(2,1)}, bf16[512,384]{0,1:T(8,128)(2,1)}, u32[]{:S(2)}, u32[]{:S(2)}) collective-permute-start(bf16[512,384]{0,1:T(8,128)(2,1)} %slice.175), channel_id=1, source_target_pairs={{1,0},{2,1},{3,2},{4,3},{5,4},{6,5},{7,6},{8,7},{9,8},{10,9},{11,1... | collective-permute-start | bytes 1179656 | tf_op jit(solution)/shard_map/ppermute | solution.py:14
  168.8 27.1 %collective-permute-start.2 = (bf16[512,384]{0,1:T(8,128)(2,1)}, bf16[512,384]{0,1:T(8,128)(2,1)}, u32[]{:S(2)}, u32[]{:S(2)}) collective-permute-start(bf16[512,384]{0,1:T(8,128)(2,1)} %slice.176), channel_id=1, source_target_pairs={{1,0},{2,1},{3,2},{4,3},{5,4},{6,5},{7,6},{8,7},{9,8},{10,9},{11,1... | collective-permute-start | bytes 1179656 | tf_op jit(solution)/shard_map/ppermute | solution.py:14
  172.6 10.6 %copy-start.5 = (f32[1024,384]{0,1:T(8,128)S(1)}, f32[1024,384]{0,1:T(8,128)}, u32[]{:S(2)}) copy-start(f32[1024,384]{0,1:T(8,128)} %copy-done.4) | copy-start | bytes 4718596
  179.2 12.2 %all-to-all-start.3 = ((bf16[4,2,24576]{2,1,0:T(2,128)(2,1)}), bf16[4,2,24576]{2,1,0:T(2,128)(2,1)S(1)}, u32[]{:S(2)}, u32[]{:S(2)}) async-start(bf16[4,2,24576]{2,1,0:T(2,128)(2,1)} %reshape.34), calls=%async_computation.3 | async-start | bytes 786432 | tf_op jit(solution)/shard_map/all_to_all | solution.py:108
  191.5 11.1 %all-to-all-start.5 = ((bf16[4,2,24576]{2,1,0:T(2,128)(2,1)}), bf16[4,2,24576]{2,1,0:T(2,128)(2,1)S(1)}, u32[]{:S(2)}, u32[]{:S(2)}) async-start(bf16[4,2,24576]{2,1,0:T(2,128)(2,1)} %reshape.38), calls=%async_computation.5 | async-start | bytes 786432 | tf_op jit(solution)/shard_map/all_to_all | solution.py:110
  202.5 168.1 %all-to-all-start.4 = ((bf16[4,2,24576]{2,1,0:T(2,128)(2,1)}), bf16[4,2,24576]{2,1,0:T(2,128)(2,1)S(1)}, u32[]{:S(2)}, u32[]{:S(2)}) async-start(bf16[4,2,24576]{2,1,0:T(2,128)(2,1)} %reshape.36), calls=%async_computation.4 | async-start | bytes 786432 | tf_op jit(solution)/shard_map/all_to_all | solution.py:109
  206.2 206.9 %all-reduce.2.cloned.1.call-start = ((), (), s32[]{:S(2)}) async-start(), calls=%async_computation.10 | async-start | bytes 294912 | tf_op jit(solution)/shard_map/psum | solution.py:121
Sparse Core Ops, SparseCore 0:
  9.8 54.2 all-gather.2
  66.7 84.7 all-gather.4
  155.5 211.7 reduce-scatter.1
  369.8 43.3 all-reduce.1
where the time goes:
time: 429 us; the launch traced here: 422 us
  waiting for transfers between devices  276 us (64%)
  other arithmetic  44.8 us (10%)
  starting transfers between devices  35.9 us (8%)
  local copies, waits for them, and re-layouts  25.4 us (6%)
  matrix products  24.8 us (6%)
  between operations  14.5 us (3%)
    reduce_scatter x1, waiting for transfers between devices, shards(): lax.psum_scatter(lax.dot_general(columns, attended_all, down, preferred_e...  161 us
    all_gather x1, waiting for transfers between devices, shards(): lax.all_gather(w_out, 'blk', axis=0, tiled=True)  57.8 us
    psum x1, waiting for transfers between devices, shards(): grad_w = lax.psum(shard, 'dp').astype(jnp.float32)  40.9 us
    unnamed x6, other arithmetic  36.3 us
    unnamed x57, local copies, waits for them, and re-layouts  16.2 us
    ppermute x4, starting transfers between devices, from_behind(): return lax.ppermute(block, axis, route)  11 us
  transfers between devices with their start and end apart: 14, of which 7 were waited for; matrix products, arithmetic and copies ran while one was open for 21% of the time, Pallas kernels for 0%

commit v1 on v0

v1 whole, which is shorter than its diff:
```python
import functools
import itertools
import math

import jax
import jax.numpy as jnp
from jax import lax
from jax.experimental import pallas as pl
from jax.experimental.pallas import tpu as pltpu
from jax.sharding import PartitionSpec as P

HDIM = 128
BF16 = jnp.bfloat16
F32 = jnp.float32
VMEM_LIMIT = 48 * 1024 * 1024
ACROSS = (((1,), (1,)), ((), ()))
DOWN = (((0,), (0,)), ((), ()))
PLAIN = (((1,), (0,)), ((), ()))


def dot(a, b, dims):
    return lax.dot_general(a, b, dims, preferred_element_type=F32)


def params(**kw):
    return pltpu.CompilerParams(vmem_limit_bytes=VMEM_LIMIT, **kw)


def cost(flops, size, exps=0):
    return pl.CostEstimate(flops=flops, bytes_accessed=size, transcendentals=exps)


def shift(x, axis, distance):
    n = lax.axis_size(axis)
    return lax.ppermute(x, axis, [(i, (i + distance) % n) for i in range(n)])


def routed(x, axes, target):
    sizes = [lax.axis_size(a) for a in axes]

    def index(at):
        r = 0
        for a, n in zip(axes, sizes):
            r = r * n + at[a] % n
        return r

    pairs = []
    for t in itertools.product(*[range(n) for n in sizes]):
        at = dict(zip(axes, t))
        pairs.append((index(at), index({**at, **target(at)})))
    return lax.ppermute(x, tuple(axes), pairs)


def exchange(x, axis, split):
    return lax.all_to_all(x, axis, split_axis=split, concat_axis=split, tiled=True)


def forward_kernel(q_ref, k_ref, v_ref, kp_ref, vp_ref, p_ref, att_ref):
    rows = q_ref.shape[0] * q_ref.shape[1]
    flat = lambda r: r[...].reshape(rows, HDIM)
    q = flat(q_ref)
    factor = HDIM**-0.5 * math.log2(math.e)
    s_prior = dot(flat(kp_ref), q, ACROSS)
    s_own = dot(flat(k_ref), q, ACROSS)
    top = jnp.maximum(
        jnp.max(s_prior, axis=0, keepdims=True), jnp.max(s_own, axis=0, keepdims=True)
    )
    e_prior = jnp.exp2((s_prior - top) * factor)
    e_own = jnp.exp2((s_own - top) * factor)
    inv = 1.0 / (
        jnp.sum(e_prior, axis=0, keepdims=True) + jnp.sum(e_own, axis=0, keepdims=True)
    )
    p_prior = (e_prior * inv).astype(BF16)
    p_own = (e_own * inv).astype(BF16)
    p_ref[0, :rows, :] = p_prior
    p_ref[0, rows:, :] = p_own
    att_t = dot(flat(vp_ref), p_prior, DOWN) + dot(flat(v_ref), p_own, DOWN)
    att_ref[...] = att_t.T.astype(BF16)


def attention_forward(q, k, v, kp, vp):
    u, rows, width = q.shape
    heads = width // HDIM
    n = u * rows
    spec = pl.BlockSpec((u, rows, HDIM), lambda h: (0, 0, h))
    return pl.pallas_call(
        forward_kernel,
        grid=(heads,),
        in_specs=[spec] * 5,
        out_specs=[
            pl.BlockSpec((1, 2 * n, n), lambda h: (h, 0, 0)),
            pl.BlockSpec((n, HDIM), lambda h: (0, h)),
        ],
        out_shape=[
            jax.ShapeDtypeStruct((heads, 2 * n, n), BF16),
            jax.ShapeDtypeStruct((n, width), BF16),
        ],
        compiler_params=params(),
        cost_estimate=cost(8 * heads * n * n * HDIM, 12 * n * width + 4 * heads * n * n, 2 * heads * n * n),
        name="forward",
    )(q, k, v, kp, vp)


def backward_kernel(
    at_ref, q_ref, k_ref, v_ref, kp_ref, vp_ref, g_ref, p_ref, att_ref, own_ref, *rest
):
    halo_refs, (scr_k, scr_v) = rest[:4], rest[4:]
    u, part = q_ref.shape[0], q_ref.shape[1]
    rows = u * part
    flat = lambda r: r[...].reshape(rows, HDIM)
    scale = HDIM**-0.5
    q, g = flat(q_ref), g_ref[...]
    delta = jnp.sum(
        (g.astype(F32) * att_ref[...].astype(F32)).T, axis=0, keepdims=True
    )
    p_prior, p_own = p_ref[0, :rows, :], p_ref[0, rows:, :]
    ds_prior = (
        p_prior.astype(F32) * (dot(flat(vp_ref), g, ACROSS) - delta)
    ).astype(BF16)
    scr_k[...] = (dot(ds_prior, q, PLAIN) * scale).astype(BF16)
    scr_v[...] = dot(p_prior, g, PLAIN).astype(BF16)
    here = at_ref[0]
    for d in range(u):
        block = pl.ds(pl.multiple_of(lax.rem(here + d, u) * part, part), part)
        halo_refs[d][0, :, :] = scr_k[block, :]
        halo_refs[d][1, :, :] = scr_v[block, :]
    ds_own = (p_own.astype(F32) * (dot(flat(v_ref), g, ACROSS) - delta)).astype(BF16)
    dk = (dot(ds_own, q, PLAIN) * scale).astype(BF16)
    dv = dot(p_own, g, PLAIN).astype(BF16)
    dq_t = (dot(flat(kp_ref), ds_prior, DOWN) + dot(flat(k_ref), ds_own, DOWN)) * scale
    dq = dq_t.T.astype(BF16)
    for s in range(u):
        block = slice(s * part, (s + 1) * part)
        own_ref[s, 0, :, :] = dq[block, :]
        own_ref[s, 1, :, :] = dk[block, :]
        own_ref[s, 2, :, :] = dv[block, :]


def attention_backward(at, q, k, v, kp, vp, g, p, att):
    u, part, width = q.shape
    heads = width // HDIM
    n = u * part
    spec = pl.BlockSpec((u, part, HDIM), lambda h: (0, 0, h))
    flat = pl.BlockSpec((n, HDIM), lambda h: (0, h))
    return pl.pallas_call(
        backward_kernel,
        grid=(heads,),
        in_specs=[pl.BlockSpec(memory_space=pltpu.SMEM)]
        + [spec] * 5
        + [flat, pl.BlockSpec((1, 2 * n, n), lambda h: (h, 0, 0)), flat],
        out_specs=[pl.BlockSpec((u, 3, part, HDIM), lambda h: (0, 0, 0, h))]
        + [pl.BlockSpec((2, part, HDIM), lambda h: (0, 0, h))] * u,
        out_shape=[jax.ShapeDtypeStruct((u, 3, part, width), BF16)]
        + [jax.ShapeDtypeStruct((2, part, width), BF16)] * u,
        scratch_shapes=[pltpu.VMEM((n, HDIM), BF16)] * 2,
        compiler_params=params(),
        cost_estimate=cost(16 * heads * n * n * HDIM, 24 * n * width + 4 * heads * n * n),
        name="backward",
    )(at, q, k, v, kp, vp, g, p, att)


def weight_kernel(
    at_ref, own_ref, a1, a2, b1, b2, a3, b3, gate_ref, att_ref, scaled_ref, keep_ref, send_ref
):
    here, core = at_ref[0], at_ref[1]
    part = own_ref.shape[0]
    half = part // 2
    gate = gate_ref[...]

    def put(ref, distance, second):
        block = lax.rem(here + distance, 4) * part + second * half
        rows = pl.ds(pl.multiple_of(block, half), ref.shape[0])
        scaled_ref[rows, :] = (ref[...].astype(F32) * gate).astype(BF16)

    put(own_ref, 0, 0)
    put(a1, 3, 0)
    put(a2, 3, 1)
    put(b1, 1, 1)
    put(b2, 1, 0)
    put(a3, 2, 0)
    put(b3, 2, 1)
    term = dot(scaled_ref[...], att_ref[...], DOWN).astype(BF16)
    rows = term.shape[0] // 4
    first = jnp.concatenate([term[:rows], term[2 * rows : 3 * rows]], axis=0)
    second = jnp.concatenate([term[rows : 2 * rows], term[3 * rows :]], axis=0)
    keep_ref[0] = jnp.where(core == 0, first, second)
    send_ref[0] = jnp.where(core == 0, second, first)


def weight_term(at, pieces, gate, att, steps):
    part, depth = pieces[0].shape
    n, width = att.shape
    step = depth // steps
    spec = lambda r: pl.BlockSpec((r, step), lambda z: (0, z))
    out = pl.BlockSpec((1, step // 2, width), lambda z: (z, 0, 0))
    return pl.pallas_call(
        weight_kernel,
        grid=(steps,),
        in_specs=[pl.BlockSpec(memory_space=pltpu.SMEM)]
        + [spec(x.shape[0]) for x in pieces]
        + [spec(1), pl.BlockSpec((n, width), lambda z: (0, 0))],
        out_specs=[spec(n), out, out],
        out_shape=[jax.ShapeDtypeStruct((n, depth), BF16)]
        + [jax.ShapeDtypeStruct((steps, step // 2, width), BF16)] * 2,
        compiler_params=params(),
        cost_estimate=cost(2 * n * depth * width, 4 * n * depth + 2 * depth * width),
        name="weight_term",
    )(at, *pieces, gate, att)


def project_kernel(at_ref, scaled_ref, mine_ref, other_ref, g_ref, total):
    z = pl.program_id(0)
    core = at_ref[1]
    mine, other = mine_ref[0], other_ref[0]
    first = jnp.where(core == 0, mine, other)
    second = jnp.where(core == 0, other, mine)
    r = first.shape[0] // 2
    w = jnp.concatenate([first[:r], second[:r], first[r:], second[r:]], axis=0)
    term = dot(scaled_ref[...], w, PLAIN)

    @pl.when(z == 0)
    def _():
        total[...] = term

    @pl.when(z > 0)
    def _():
        total[...] += term

    @pl.when(z == pl.num_programs(0) - 1)
    def _():
        g_ref[...] = total[...].astype(BF16)


def project(at, scaled, mine, other):
    n, depth = scaled.shape
    steps, rows, width = mine.shape
    w_spec = pl.BlockSpec((1, rows, width), lambda z: (z, 0, 0))
    return pl.pallas_call(
        project_kernel,
        grid=(steps,),
        in_specs=[
            pl.BlockSpec(memory_space=pltpu.SMEM),
            pl.BlockSpec((n, depth // steps), lambda z: (0, z)),
            w_spec,
            w_spec,
        ],
        out_specs=pl.BlockSpec((n, width), lambda z: (0, 0)),
        out_shape=jax.ShapeDtypeStruct((n, width), BF16),
        scratch_shapes=[pltpu.VMEM((n, width), F32)],
        compiler_params=params(),
        cost_estimate=cost(2 * n * depth * width, 2 * n * depth + 2 * depth * width),
        name="project",
    )(at, scaled, mine, other)


def assemble_kernel(at_ref, own_ref, h0, h1, h2, h3, q_ref, k_ref, v_ref, scr):
    here = at_ref[0]
    width = own_ref.shape[3]
    for d, ref in enumerate((h0, h1, h2, h3)):
        scr[lax.rem(here + 4 - d, 4)] = ref[...]
    for s in range(4):
        cols = slice(s * width, (s + 1) * width)
        q_ref[0, :, cols] = own_ref[s, 0]
        for at, ref in ((0, k_ref), (1, v_ref)):
            ref[0, :, cols] = (
                own_ref[s, 1 + at].astype(F32) + scr[s, at].astype(F32)
            ).astype(BF16)


def assemble(at, own, halos):
    u, _, part, width = own.shape
    vmem = pl.BlockSpec(memory_space=pltpu.VMEM)
    return pl.pallas_call(
        assemble_kernel,
        in_specs=[pl.BlockSpec(memory_space=pltpu.SMEM)] + [vmem] * 5,
        out_specs=[vmem] * 3,
        out_shape=[jax.ShapeDtypeStruct((1, part, u * width), BF16)] * 3,
        scratch_shapes=[pltpu.VMEM((u, 2, part, width), BF16)],
        compiler_params=params(),
        cost_estimate=cost(2 * u * part * width, 16 * u * part * width),
        name="assemble",
    )(at, own, *halos)


def shards(q_tok, k_tok, v_tok, d_y, gate, w_out):
    uly = lax.axis_size("uly")
    n_blk = lax.axis_size("blk")
    here = lax.axis_index("uly")
    core = lax.axis_index("dp") % 2
    lower = lax.axis_index("dp") // 2
    upper = lax.axis_index("blk") % 2
    at = jnp.stack([here, core]).astype(jnp.int32)
    part = q_tok.shape[1]
    width = w_out.shape[1]
    rows = w_out.shape[0]
    along_z = [list(range(x, n_blk, 2)) for x in range(2)]
    z_size = n_blk // 2

    def to_heads(x):
        x = x[0].reshape(part, uly, width).transpose(1, 0, 2)
        return exchange(x, "uly", 0)

    w_half = lax.dynamic_slice_in_dim(w_out, core * (rows // 2), rows // 2, axis=0)
    w_far = routed(w_half, ["blk"], lambda c: dict(blk=c["blk"] ^ 1))
    w_pair = jnp.concatenate(
        [jnp.where(upper == 0, w_half, w_far), jnp.where(upper == 0, w_far, w_half)], axis=0
    )
    w_mine = lax.all_to_all(
        jnp.broadcast_to(w_pair[None], (z_size,) + w_pair.shape),
        "blk",
        split_axis=0,
        concat_axis=0,
        tiled=True,
        axis_index_groups=along_z,
    )
    swap_core = lambda x: routed(x, ["dp"], lambda c: dict(dp=c["dp"] ^ 1))
    w_other = swap_core(w_mine)

    k = to_heads(k_tok)
    v = to_heads(v_tok)
    kp = shift(k, "blk", 1)
    vp = shift(v, "blk", 1)

    dy = d_y[0]
    dy0, dy1 = dy[: part // 2], dy[part // 2 :]
    a1 = shift(dy0, "uly", 1)
    b1 = shift(dy1, "uly", -1)
    a2 = shift(dy1, "uly", 1)
    b2 = shift(dy0, "uly", -1)
    a3 = shift(a1, "uly", 1)
    b3 = shift(b1, "uly", -1)
    q = to_heads(q_tok)

    p, att = attention_forward(q, k, v, kp, vp)
    scaled, keep, send = weight_term(at, (dy, a1, a2, b1, b2, a3, b3), gate, att, z_size)

    both = (keep.astype(F32) + swap_core(send).astype(F32)).astype(BF16)
    terms = lax.all_to_all(
        both, "blk", split_axis=0, concat_axis=0, tiled=True, axis_index_groups=along_z
    )

    g = project(at, scaled, w_mine, w_other)
    own, *halos = attention_backward(at, q, k, v, kp, vp, g, p, att)
    halos = [
        routed(h, ["uly", "blk"], lambda c, d=d: dict(uly=c["uly"] + d, blk=c["blk"] - 1))
        for d, h in enumerate(halos)
    ]
    own = exchange(own, "uly", 0)
    grad_q, grad_k, grad_v = assemble(at, own, halos)

    column = jnp.sum(terms.astype(F32), axis=0).astype(BF16).reshape(2, 2, rows // 4, width)

    def x_piece(du, dl):
        piece = lax.dynamic_index_in_dim(column, upper ^ du, 0, keepdims=False)
        return lax.dynamic_index_in_dim(piece, lower ^ dl, 0, keepdims=False)

    share = x_piece(0, 0).astype(F32)
    for du, dl in ((0, 1), (1, 0), (1, 1)):
        share = share + routed(
            x_piece(du, dl),
            ["dp", "blk"],
            lambda c, du=du, dl=dl: dict(dp=c["dp"] ^ (2 * dl), blk=c["blk"] ^ du),
        ).astype(F32)
    shares = exchange(jnp.broadcast_to(share[None], (4,) + share.shape), "dp", 0)
    grad_w = (
        shares.reshape(2, 2, rows // 4, width).transpose(1, 0, 2, 3).reshape(rows, width)
    )
    return grad_q, grad_k, grad_v, grad_w


def solution(mesh):
    tokens = P("dp", ("blk", "uly"), None)
    return jax.shard_map(
        shards,
        mesh=mesh,
        in_specs=(tokens, tokens, tokens, tokens, P("dp", None), P("blk", "uly")),
        out_specs=(tokens, tokens, tokens, P("blk", "uly")),
        check_vma=False,
    )
```

time: 429 us -> 170 us (0.40); the launches traced: 422 us -> 169 us
  waiting for transfers between devices: 276 us -> 61.2 us
  other arithmetic: 44.8 us -> 2.92 us
  starting transfers between devices: 35.9 us -> 68.2 us
  matrix products: 24.8 us -> 0 us
  Pallas kernels: 0 us -> 24.5 us
  local copies, waits for them, and re-layouts: 25.4 us -> 11.6 us
  between operations: 14.5 us -> 0.81 us
    reduce_scatter x1 -> x0, waiting for transfers between devices: 161 us -> none  [shards(): lax.psum_scatter(lax.dot_general(columns, attended_all, down, preferred_e...]
    all_gather x2 -> x0, waiting for transfers between devices: 57.8 us -> none  [the longest x1 57.8 us: shards(): lax.all_gather(w_out, 'blk', axis=0, tiled=True)]
    psum x1 -> x0, waiting for transfers between devices: 40.9 us -> none  [shards(): grad_w = lax.psum(shard, 'dp').astype(jnp.float32)]
    unnamed x6 -> x0, other arithmetic: 36.3 us -> none
    dot_general x20 -> x0, matrix products: 24.8 us -> none  [the longest x3 5.21 us: row_step(): jnp.dot(probs_half, v_part, preferred_element_type=jnp.float32)]
    pallas_call x0 -> x5, Pallas kernels: none -> 24.5 us  [the longest x1 6.92 us: weight_term(): pl.pallas_call(weight_kernel, grid=(steps,), in_specs=[pl.BlockSpec(memor...]
    all_to_all x6 -> x7, waiting for transfers between devices: 7.41 us -> 31.5 us  [the longest x1 16.2 us: shards(): lax.all_to_all(both, 'blk', split_axis=0, concat_axis=0, tiled=True, axis...]
    ppermute x4 -> x18, waiting for transfers between devices: 8.28 us -> 29.6 us  [the longest x10 24.6 us: routed(): return lax.ppermute(x, tuple(axes), pairs)]
  transfers between devices with their start and end apart: 14 -> 25, of which waited for: 7 -> 13; matrix products, arithmetic and copies ran while one was open for 21% -> 4% of each run, Pallas kernels for 0% -> 14%
where the time goes in v1:
time: 170 us; the launch traced here: 169 us
  starting transfers between devices  68.2 us (40%)
  waiting for transfers between devices  61.2 us (36%)
  Pallas kernels  24.5 us (14%)
  local copies, waits for them, and re-layouts  11.6 us (7%)
  other arithmetic  2.92 us (2%)
    ppermute x10, waiting for transfers between devices, routed(): return lax.ppermute(x, tuple(axes), pairs)  24.6 us
    all_to_all x5, starting transfers between devices, exchange(): lax.all_to_all(x, axis, split_axis=split, concat_axis=split, tiled=True)  21.1 us
    ppermute x10, starting transfers between devices, routed(): return lax.ppermute(x, tuple(axes), pairs)  19.1 us
    all_to_all x1, waiting for transfers between devices, shards(): lax.all_to_all(both, 'blk', split_axis=0, concat_axis=0, tiled=True, axis...  16.2 us
    all_to_all x5, waiting for transfers between devices, exchange(): lax.all_to_all(x, axis, split_axis=split, concat_axis=split, tiled=True)  15.4 us
    ppermute x8, starting transfers between devices, shift(): return lax.ppermute(x, axis, [(i, (i + distance) % n) for i in range(n)])  12.8 us
    all_to_all x1, starting transfers between devices, shards(): lax.all_to_all(jnp.broadcast_to(w_pair[None], (z_size,) + w_pair.shape),...  8.53 us
    pallas_call x1, Pallas kernels, weight_term(): pl.pallas_call(weight_kernel, grid=(steps,), in_specs=[pl.BlockSpec(memor...  6.92 us
  transfers between devices with their start and end apart: 25, of which 13 were waited for; matrix products, arithmetic and copies ran while one was open for 4% of the time, Pallas kernels for 14%

profile of v1, /device:TPU:1, one launch (start us, length us, event | category | flops | bytes accessed | tf_op | source)
XLA Modules:
  0.0 169.2 jit_solution(12249023193073375747)
XLA Ops:
  2.9 5.0 %all-to-all-start.1 = ((bf16[4,128,384]{2,1,0:T(8,128)(2,1)}), bf16[4,128,384]{2,1,0:T(8,128)(2,1)S(1)}, u32[]{:S(2)}, u32[]{:S(2)}) async-start(bf16[4,128,384]{2,1,0:T(8,128)(2,1)} %bitcast.5), calls=%async_computation.1 | async-start | bytes 786432 | tf_op jit(solution)/shard_map/all_to_all | solution.py:55
  7.9 2.8 %collective-permute-start.8 = (bf16[96,384]{1,0:T(8,128)(2,1)S(1)}, bf16[96,384]{1,0:T(8,128)(2,1)S(1)}, u32[]{:S(2)}, u32[]{:S(2)}) collective-permute-start(bf16[96,384]{1,0:T(8,128)(2,1)S(1)} %constant_dynamic-slice_fusion), channel_id=1, source_target_pairs={{0,1},{1,0},{2,3},{3,2},{4,5},{5,4},{6,7},{7,6},{8,9},{9,8},{10,11... | collective-permute-start | bytes 221192 | tf_op jit(solution)/shard_map/ppermute | solution.py:51
  11.9 2.5 %all-to-all-done.1.k_ref = bf16[4,128,384]{2,1,0:T(8,128)(2,1)S(1)} async-done(((bf16[4,128,384]{2,1,0:T(8,128)(2,1)}), bf16[4,128,384]{2,1,0:T(8,128)(2,1)S(1)}, u32[]{:S(2)}, u32[]{:S(2)}) %all-to-all-start.1) | async-done | bytes 393248 | tf_op jit(solution)/shard_map/all_to_all | solution.py:55
  14.4 3.6 %all-to-all-start.2 = ((bf16[4,128,384]{2,1,0:T(8,128)(2,1)}), bf16[4,128,384]{2,1,0:T(8,128)(2,1)S(1)}, u32[]{:S(2)}, u32[]{:S(2)}) async-start(bf16[4,128,384]{2,1,0:T(8,128)(2,1)} %bitcast.7), calls=%async_computation.2 | async-start | bytes 786432 | tf_op jit(solution)/shard_map/all_to_all | solution.py:55
  22.8 3.1 %collective-permute-start = (bf16[4,128,384]{2,1,0:T(8,128)(2,1)S(1)}, bf16[4,128,384]{2,1,0:T(8,128)(2,1)S(1)}, u32[]{:S(2)}, u32[]{:S(2)}) collective-permute-start(bf16[4,128,384]{2,1,0:T(8,128)(2,1)S(1)} %all-to-all-done.1.k_ref), channel_id=1, source_target_pairs={{0,1},{1,2},{2,3},{3,4},{4,5},{5,6},{6,7},{7,8},{8,9},{9,10},{10,1... | collective-permute-start | bytes 1179656 | tf_op jit(solution)/shard_map/ppermute | solution.py:35
  25.9 3.5 %all-to-all-start = ((bf16[4,128,384]{2,1,0:T(8,128)(2,1)}), bf16[4,128,384]{2,1,0:T(8,128)(2,1)S(1)}, u32[]{:S(2)}, u32[]{:S(2)}) async-start(bf16[4,128,384]{2,1,0:T(8,128)(2,1)} %bitcast.3), calls=%async_computation | async-start | bytes 786432 | tf_op jit(solution)/shard_map/all_to_all | solution.py:55
  31.1 6.1 %all-to-all-done.q_ref = bf16[4,128,384]{2,1,0:T(8,128)(2,1)S(1)} async-done(((bf16[4,128,384]{2,1,0:T(8,128)(2,1)}), bf16[4,128,384]{2,1,0:T(8,128)(2,1)S(1)}, u32[]{:S(2)}, u32[]{:S(2)}) %all-to-all-start) | async-done | bytes 393248 | tf_op jit(solution)/shard_map/all_to_all | solution.py:55
  38.3 8.5 %all-to-all-start.3 = ((bf16[8,192,384]{2,1,0:T(8,128)(2,1)}), bf16[8,192,384]{2,1,0:T(8,128)(2,1)S(1)}, u32[]{:S(2)}, u32[]{:S(2)}) async-start(bf16[8,192,384]{2,1,0:T(8,128)(2,1)} %broadcast_in_dim.4), calls=%async_computation.3 | async-start | bytes 2359296 | tf_op jit(solution)/shard_map/all_to_all | solution.py:308
  47.4 2.1 %collective-permute-start.5 = (bf16[64,3072]{1,0:T(8,128)(2,1)}, bf16[64,3072]{1,0:T(8,128)(2,1)}, u32[]{:S(2)}, u32[]{:S(2)}) collective-permute-start(bf16[64,3072]{1,0:T(8,128)(2,1)} %get-tuple-element.31), channel_id=1, source_target_pairs={{0,48},{16,0},{32,16},{48,32},{1,49},{17,1},{33,17},{49,33},{2,50}... | collective-permute-start | bytes 1179656 | tf_op jit(solution)/shard_map/ppermute | solution.py:35
  49.5 2.7 %collective-permute-start.7 = (bf16[64,3072]{1,0:T(8,128)(2,1)}, bf16[64,3072]{1,0:T(8,128)(2,1)}, u32[]{:S(2)}, u32[]{:S(2)}) collective-permute-start(bf16[64,3072]{1,0:T(8,128)(2,1)} %collective-permute-done.4.b1), channel_id=1, source_target_pairs={{0,48},{16,0},{32,16},{48,32},{1,49},{17,1},{33,17},{49,33},{2,50}... | collective-permute-start | bytes 1179656 | tf_op jit(solution)/shard_map/ppermute | solution.py:35
  52.3 4.8 %forward.1 = (bf16[3,1024,512]{2,1,0:T(8,128)(2,1)S(1)}, bf16[512,384]{1,0:T(8,128)(2,1)S(1)}) custom-call(bf16[4,128,384]{2,1,0:T(8,128)(2,1)S(1)} %all-to-all-done.q_ref, bf16[4,128,384]{2,1,0:T(8,128)(2,1)S(1)} %all-to-all-done.1.k_ref, bf16[4,128,384]{2,1,0:T(8,128)(2,1)S(1)} %all-to-all-done.2.v_ref, ...), custom_call_target="tpu_custom_call" | custom-call | flops 805306368 | bytes 5505024 | tf_op jit(solution)/shard_map/forward/pallas_call | solution.py:86
  58.7 5.0 %collective-permute-done.6.a3 = bf16[64,3072]{1,0:T(8,128)(2,1)} collective-permute-done((bf16[64,3072]{1,0:T(8,128)(2,1)}, bf16[64,3072]{1,0:T(8,128)(2,1)}, u32[]{:S(2)}, u32[]{:S(2)}) %collective-permute-start.6) | collective-permute-done | bytes 393248 | tf_op jit(solution)/shard_map/ppermute | solution.py:35
  63.8 6.9 %weight_term.1 = (bf16[512,3072]{1,0:T(8,128)(2,1)}, bf16[8,192,384]{2,1,0:T(8,128)(2,1)S(1)}, bf16[8,192,384]{2,1,0:T(8,128)(2,1)S(1)}) custom-call(s32[2]{0:T(128)S(1)} %pad_add_fusion.at_ref, bf16[128,3072]{1,0:T(8,128)(2,1)S(1)} %bitcast.27, bf16[64,3072]{1,0:T(8,128)(2,1)} %collective-permute-done.2.a1, bf16[64,3072]{1,0:T(8,128)(2,1)} %collective-permute-done.3.a2, ...), custom_call_target="tpu_custom_call" | custom-call | flops 1207959552 | bytes 8650752 | tf_op jit(solution)/shard_map/weight_term/pallas_call | solution.py:196
  70.7 4.6 %collective-permute-start.14 = (bf16[8,192,384]{2,1,0:T(8,128)(2,1)S(1)}, bf16[8,192,384]{2,1,0:T(8,128)(2,1)S(1)}, u32[]{:S(2)}, u32[]{:S(2)}) collective-permute-start(bf16[8,192,384]{2,1,0:T(8,128)(2,1)S(1)} %get-tuple-element.29), channel_id=1, source_target_pairs={{0,64},{64,0},{128,192},{192,128},{1,65},{65,1},{129,193},{193,129... | collective-permute-start | bytes 3538952 | tf_op jit(solution)/shard_map/ppermute | solution.py:51
  75.3 2.5 %collective-permute-done.14 = bf16[8,192,384]{2,1,0:T(8,128)(2,1)S(1)} collective-permute-done((bf16[8,192,384]{2,1,0:T(8,128)(2,1)S(1)}, bf16[8,192,384]{2,1,0:T(8,128)(2,1)S(1)}, u32[]{:S(2)}, u32[]{:S(2)}) %collective-permute-start.14) | collective-permute-done | bytes 1179680 | tf_op jit(solution)/shard_map/ppermute | solution.py:51
  79.1 6.7 %all-to-all-start.5 = ((bf16[8,192,384]{2,1,0:T(8,128)(2,1)}), bf16[8,192,384]{2,1,0:T(8,128)(2,1)}, u32[]{:S(2)}, u32[]{:S(2)}) async-start(bf16[8,192,384]{2,1,0:T(8,128)(2,1)} %add_convert_fusion), calls=%async_computation.5 | async-start | bytes 2359296 | tf_op jit(solution)/shard_map/all_to_all | solution.py:338
  86.4 2.5 %collective-permute-done.9.other_ref = bf16[8,192,384]{2,1,0:T(8,128)(2,1)S(1)} collective-permute-done((bf16[8,192,384]{2,1,0:T(8,128)(2,1)S(1)}, bf16[8,192,384]{2,1,0:T(8,128)(2,1)S(1)}, u32[]{:S(2)}, u32[]{:S(2)}) %collective-permute-start.9) | collective-permute-done | bytes 1179680 | tf_op jit(solution)/shard_map/ppermute | solution.py:51
  88.9 1.9 %copy-done = bf16[512,3072]{1,0:T(8,128)(2,1)S(1)} copy-done((bf16[512,3072]{1,0:T(8,128)(2,1)S(1)}, bf16[512,3072]{1,0:T(8,128)(2,1)}, u32[]{:S(2)}) %copy-start) | copy-done | bytes 3145752
  90.8 4.8 %project.1.g_ref = bf16[512,384]{1,0:T(8,128)(2,1)S(1)} custom-call(s32[2]{0:T(128)S(1)} %pad_add_fusion.at_ref, bf16[512,3072]{1,0:T(8,128)(2,1)S(1)} %copy-done, bf16[8,192,384]{2,1,0:T(8,128)(2,1)S(1)} %all-to-all-done.3.mine_ref, bf16[8,192,384]{2,1,0:T(8,128)(2,1)S(1)} %collective-permute-done.9.other_ref), custom_call_target="tpu_custom_call" | custom-call | flops 1207959552 | bytes 5505024 | tf_op jit(solution)/shard_map/project/pallas_call | solution.py:238
  95.6 6.2 %backward.1 = (bf16[4,3,128,384]{3,2,1,0:T(8,128)(2,1)}, bf16[2,128,384]{2,1,0:T(8,128)(2,1)S(1)}, bf16[2,128,384]{2,1,0:T(8,128)(2,1)S(1)}, bf16[2,128,384]{2,1,0:T(8,128)(2,1)S(1)}, bf16[2,128,384]{2,1,0:T(8,128)(2,1)S(1)}) custom-call(s32[2]{0:T(128)S(1)} %pad_add_fusion.at_ref, bf16[4,128,384]{2,1,0:T(8,128)(2,1)S(1)} %all-to-all-done.q_ref, ...), custom_call_target="tpu_custom_call" | custom-call | flops 1610612736 | bytes 7864320 | tf_op jit(solution)/shard_map/backward/pallas_call | solution.py:145
  101.8 16.2 %all-to-all-done.5 = bf16[8,192,384]{2,1,0:T(8,128)(2,1)} async-done(((bf16[8,192,384]{2,1,0:T(8,128)(2,1)}), bf16[8,192,384]{2,1,0:T(8,128)(2,1)}, u32[]{:S(2)}, u32[]{:S(2)}) %all-to-all-start.5) | async-done | bytes 1179680 | tf_op jit(solution)/shard_map/all_to_all | solution.py:338
  118.0 3.9 %all-to-all-start.4 = ((bf16[4,3,128,384]{3,2,1,0:T(8,128)(2,1)}), bf16[4,3,128,384]{3,2,1,0:T(8,128)(2,1)S(1)}, u32[]{:S(2)}, u32[]{:S(2)}) async-start(bf16[4,3,128,384]{3,2,1,0:T(8,128)(2,1)} %get-tuple-element.20), calls=%async_computation.4 | async-start | bytes 2359296 | tf_op jit(solution)/shard_map/all_to_all | solution.py:55
  124.3 2.3 %collective-permute-start.16 = (bf16[48,384]{1,0:T(8,128)(2,1)S(1)}, bf16[48,384]{1,0:T(8,128)(2,1)S(1)}, u32[]{:S(2)}, u32[]{:S(2)}) collective-permute-start(bf16[48,384]{1,0:T(8,128)(2,1)S(1)} %get-tuple-element.34), channel_id=1, source_target_pairs={{0,1},{1,0},{2,3},{3,2},{4,5},{5,4},{6,7},{7,6},{8,9},{9,8},{10,11... | collective-permute-start | bytes 110600 | tf_op jit(solution)/shard_map/ppermute | solution.py:51
  128.6 2.3 %collective-permute-done.17 = bf16[48,384]{1,0:T(8,128)(2,1)S(1)} collective-permute-done((bf16[48,384]{1,0:T(8,128)(2,1)S(1)}, bf16[48,384]{1,0:T(8,128)(2,1)S(1)}, u32[]{:S(2)}, u32[]{:S(2)}) %collective-permute-start.17) | collective-permute-done | bytes 36896 | tf_op jit(solution)/shard_map/ppermute | solution.py:51
  130.9 6.8 %all-to-all-done.4.own_ref = bf16[4,3,128,384]{3,2,1,0:T(8,128)(2,1)S(1)} async-done(((bf16[4,3,128,384]{3,2,1,0:T(8,128)(2,1)}), bf16[4,3,128,384]{3,2,1,0:T(8,128)(2,1)S(1)}, u32[]{:S(2)}, u32[]{:S(2)}) %all-to-all-start.4) | async-done | bytes 1179680 | tf_op jit(solution)/shard_map/all_to_all | solution.py:55
  138.5 5.1 %all-to-all-start.6 = ((f32[4,48,384]{2,1,0:T(8,128)}), f32[4,48,384]{2,1,0:T(8,128)S(1)}, u32[]{:S(2)}, u32[]{:S(2)}) async-start(f32[4,48,384]{2,1,0:T(8,128)} %broadcast_in_dim.5), calls=%async_computation.6 | async-start | bytes 589824 | tf_op jit(solution)/shard_map/all_to_all | solution.py:55
  143.5 6.1 %collective-permute-start.12 = (bf16[2,128,384]{2,1,0:T(8,128)(2,1)S(1)}, bf16[2,128,384]{2,1,0:T(8,128)(2,1)S(1)}, u32[]{:S(2)}, u32[]{:S(2)}) collective-permute-start(bf16[2,128,384]{2,1,0:T(8,128)(2,1)S(1)} %get-tuple-element.23), channel_id=1, source_target_pairs={{0,47},{1,32},{2,33},{3,34},{4,35},{5,36},{6,37},{7,38},{8,39},{9,... | collective-permute-start | bytes 589832 | tf_op jit(solution)/shard_map/ppermute | solution.py:51
  150.7 3.4 %collective-permute-done.10.h0 = bf16[2,128,384]{2,1,0:T(8,128)(2,1)S(1)} collective-permute-done((bf16[2,128,384]{2,1,0:T(8,128)(2,1)S(1)}, bf16[2,128,384]{2,1,0:T(8,128)(2,1)S(1)}, u32[]{:S(2)}, u32[]{:S(2)}) %collective-permute-start.10) | collective-permute-done | bytes 196640 | tf_op jit(solution)/shard_map/ppermute | solution.py:51
  154.1 4.9 %collective-permute-done.11.h1 = bf16[2,128,384]{2,1,0:T(8,128)(2,1)S(1)} collective-permute-done((bf16[2,128,384]{2,1,0:T(8,128)(2,1)S(1)}, bf16[2,128,384]{2,1,0:T(8,128)(2,1)S(1)}, u32[]{:S(2)}, u32[]{:S(2)}) %collective-permute-start.11) | collective-permute-done | bytes 196640 | tf_op jit(solution)/shard_map/ppermute | solution.py:51
  159.0 3.8 %collective-permute-done.12.h2 = bf16[2,128,384]{2,1,0:T(8,128)(2,1)S(1)} collective-permute-done((bf16[2,128,384]{2,1,0:T(8,128)(2,1)S(1)}, bf16[2,128,384]{2,1,0:T(8,128)(2,1)S(1)}, u32[]{:S(2)}, u32[]{:S(2)}) %collective-permute-start.12) | collective-permute-done | bytes 196640 | tf_op jit(solution)/shard_map/ppermute | solution.py:51
  162.8 3.9 %collective-permute-done.13.h3 = bf16[2,128,384]{2,1,0:T(8,128)(2,1)S(1)} collective-permute-done((bf16[2,128,384]{2,1,0:T(8,128)(2,1)S(1)}, bf16[2,128,384]{2,1,0:T(8,128)(2,1)S(1)}, u32[]{:S(2)}, u32[]{:S(2)}) %collective-permute-start.13) | collective-permute-done | bytes 196640 | tf_op jit(solution)/shard_map/ppermute | solution.py:51
  166.7 1.8 %assemble.1 = (bf16[1,128,1536]{2,1,0:T(8,128)(2,1)}, bf16[1,128,1536]{2,1,0:T(8,128)(2,1)}, bf16[1,128,1536]{2,1,0:T(8,128)(2,1)}) custom-call(s32[2]{0:T(128)S(1)} %pad_add_fusion.at_ref, bf16[4,3,128,384]{3,2,1,0:T(8,128)(2,1)S(1)} %all-to-all-done.4.own_ref, bf16[2,128,384]{2,1,0:T(8,128)(2,1)S(1)} %collective-permute-done.10.h0, ...), custom_call_target="tpu_custom_call" | custom-call | flops 393216 | bytes 3145728 | tf_op jit(solution)/shard_map/assemble/pallas_call | solution.py:273
  (59 shorter events, 22.2 us)
Async XLA Ops:
  0.6 7.2 %copy-start.8 = (bf16[192,384]{1,0:T(8,128)(2,1)S(1)}, bf16[192,384]{1,0:T(8,128)(2,1)}, u32[]{:S(2)}) copy-start(bf16[192,384]{1,0:T(8,128)(2,1)} %param.11) | copy-start | bytes 442372
  0.6 10.1 %copy-start.6 = (bf16[1,128,1536]{2,1,0:T(8,128)(2,1)S(1)}, bf16[1,128,1536]{2,1,0:T(8,128)(2,1)}, u32[]{:S(2)}) copy-start(bf16[1,128,1536]{2,1,0:T(8,128)(2,1)} %param.8) | copy-start | bytes 1179652
  2.9 11.5 %all-to-all-start.1 = ((bf16[4,128,384]{2,1,0:T(8,128)(2,1)}), bf16[4,128,384]{2,1,0:T(8,128)(2,1)S(1)}, u32[]{:S(2)}, u32[]{:S(2)}) async-start(bf16[4,128,384]{2,1,0:T(8,128)(2,1)} %bitcast.5), calls=%async_computation.1 | async-start | bytes 786432 | tf_op jit(solution)/shard_map/all_to_all | solution.py:55
  7.9 10.1 %copy-start.1 = (bf16[1,128,3072]{2,1,0:T(8,128)(2,1)S(1)}, bf16[1,128,3072]{2,1,0:T(8,128)(2,1)}, u32[]{:S(2)}) copy-start(bf16[1,128,3072]{2,1,0:T(8,128)(2,1)} %param.9) | copy-start | bytes 2359300
  7.9 21.5 %collective-permute-start.8 = (bf16[96,384]{1,0:T(8,128)(2,1)S(1)}, bf16[96,384]{1,0:T(8,128)(2,1)S(1)}, u32[]{:S(2)}, u32[]{:S(2)}) collective-permute-start(bf16[96,384]{1,0:T(8,128)(2,1)S(1)} %constant_dynamic-slice_fusion), channel_id=1, source_target_pairs={{0,1},{1,0},{2,3},{3,2},{4,5},{5,4},{6,7},{7,6},{8,9},{9,8},{10,11... | collective-permute-start | bytes 221192 | tf_op jit(solution)/shard_map/ppermute | solution.py:51
  14.4 7.2 %copy-start.7 = (bf16[1,128,1536]{2,1,0:T(8,128)(2,1)S(1)}, bf16[1,128,1536]{2,1,0:T(8,128)(2,1)}, u32[]{:S(2)}) copy-start(bf16[1,128,1536]{2,1,0:T(8,128)(2,1)} %param.6) | copy-start | bytes 1179652
  14.4 11.5 %all-to-all-start.2 = ((bf16[4,128,384]{2,1,0:T(8,128)(2,1)}), bf16[4,128,384]{2,1,0:T(8,128)(2,1)S(1)}, u32[]{:S(2)}, u32[]{:S(2)}) async-start(bf16[4,128,384]{2,1,0:T(8,128)(2,1)} %bitcast.7), calls=%async_computation.2 | async-start | bytes 786432 | tf_op jit(solution)/shard_map/all_to_all | solution.py:55
  19.0 28.4 %collective-permute-start.2 = (bf16[64,3072]{1,0:T(8,128)(2,1)}, bf16[64,3072]{1,0:T(8,128)(2,1)}, u32[]{:S(2)}, u32[]{:S(2)}) collective-permute-start(bf16[64,3072]{1,0:T(8,128)(2,1)} %get-tuple-element.31), channel_id=1, source_target_pairs={{0,16},{16,32},{32,48},{48,0},{1,17},{17,33},{33,49},{49,1},{2,18}... | collective-permute-start | bytes 1179656 | tf_op jit(solution)/shard_map/ppermute | solution.py:35
  20.4 29.1 %collective-permute-start.4 = (bf16[64,3072]{1,0:T(8,128)(2,1)}, bf16[64,3072]{1,0:T(8,128)(2,1)}, u32[]{:S(2)}, u32[]{:S(2)}) collective-permute-start(bf16[64,3072]{1,0:T(8,128)(2,1)} %get-tuple-element.30), channel_id=1, source_target_pairs={{0,48},{16,0},{32,16},{48,32},{1,49},{17,1},{33,17},{49,33},{2,50}... | collective-permute-start | bytes 1179656 | tf_op jit(solution)/shard_map/ppermute | solution.py:35
  22.8 26.7 %collective-permute-start = (bf16[4,128,384]{2,1,0:T(8,128)(2,1)S(1)}, bf16[4,128,384]{2,1,0:T(8,128)(2,1)S(1)}, u32[]{:S(2)}, u32[]{:S(2)}) collective-permute-start(bf16[4,128,384]{2,1,0:T(8,128)(2,1)S(1)} %all-to-all-done.1.k_ref), channel_id=1, source_target_pairs={{0,1},{1,2},{2,3},{3,4},{4,5},{5,6},{6,7},{7,8},{8,9},{9,10},{10,1... | collective-permute-start | bytes 1179656 | tf_op jit(solution)/shard_map/ppermute | solution.py:35
  25.9 11.3 %all-to-all-start = ((bf16[4,128,384]{2,1,0:T(8,128)(2,1)}), bf16[4,128,384]{2,1,0:T(8,128)(2,1)S(1)}, u32[]{:S(2)}, u32[]{:S(2)}) async-start(bf16[4,128,384]{2,1,0:T(8,128)(2,1)} %bitcast.3), calls=%async_computation | async-start | bytes 786432 | tf_op jit(solution)/shard_map/all_to_all | solution.py:55
  29.4 22.8 %collective-permute-start.1 = (bf16[4,128,384]{2,1,0:T(8,128)(2,1)S(1)}, bf16[4,128,384]{2,1,0:T(8,128)(2,1)}, u32[]{:S(2)}, u32[]{:S(2)}) collective-permute-start(bf16[4,128,384]{2,1,0:T(8,128)(2,1)S(1)} %all-to-all-done.2.v_ref), channel_id=1, source_target_pairs={{0,1},{1,2},{2,3},{3,4},{4,5},{5,6},{6,7},{7,8},{8,9},{9,10},{10,1... | collective-permute-start | bytes 1179656 | tf_op jit(solution)/shard_map/ppermute | solution.py:35
  38.3 40.8 %all-to-all-start.3 = ((bf16[8,192,384]{2,1,0:T(8,128)(2,1)}), bf16[8,192,384]{2,1,0:T(8,128)(2,1)S(1)}, u32[]{:S(2)}, u32[]{:S(2)}) async-start(bf16[8,192,384]{2,1,0:T(8,128)(2,1)} %broadcast_in_dim.4), calls=%async_computation.3 | async-start | bytes 2359296 | tf_op jit(solution)/shard_map/all_to_all | solution.py:308
  46.8 11.9 %collective-permute-start.3 = (bf16[64,3072]{1,0:T(8,128)(2,1)}, bf16[64,3072]{1,0:T(8,128)(2,1)}, u32[]{:S(2)}, u32[]{:S(2)}) collective-permute-start(bf16[64,3072]{1,0:T(8,128)(2,1)} %get-tuple-element.30), channel_id=1, source_target_pairs={{0,16},{16,32},{32,48},{48,0},{1,17},{17,33},{33,49},{49,1},{2,18}... | collective-permute-start | bytes 1179656 | tf_op jit(solution)/shard_map/ppermute | solution.py:35
  47.4 11.4 %collective-permute-start.5 = (bf16[64,3072]{1,0:T(8,128)(2,1)}, bf16[64,3072]{1,0:T(8,128)(2,1)}, u32[]{:S(2)}, u32[]{:S(2)}) collective-permute-start(bf16[64,3072]{1,0:T(8,128)(2,1)} %get-tuple-element.31), channel_id=1, source_target_pairs={{0,48},{16,0},{32,16},{48,32},{1,49},{17,1},{33,17},{49,33},{2,50}... | collective-permute-start | bytes 1179656 | tf_op jit(solution)/shard_map/ppermute | solution.py:35
  49.5 14.3 %collective-permute-start.6 = (bf16[64,3072]{1,0:T(8,128)(2,1)}, bf16[64,3072]{1,0:T(8,128)(2,1)}, u32[]{:S(2)}, u32[]{:S(2)}) collective-permute-start(bf16[64,3072]{1,0:T(8,128)(2,1)} %collective-permute-done.2.a1), channel_id=1, source_target_pairs={{0,16},{16,32},{32,48},{48,0},{1,17},{17,33},{33,49},{49,1},{2,18}... | collective-permute-start | bytes 1179656 | tf_op jit(solution)/shard_map/ppermute | solution.py:35
  49.5 14.3 %collective-permute-start.7 = (bf16[64,3072]{1,0:T(8,128)(2,1)}, bf16[64,3072]{1,0:T(8,128)(2,1)}, u32[]{:S(2)}, u32[]{:S(2)}) collective-permute-start(bf16[64,3072]{1,0:T(8,128)(2,1)} %collective-permute-done.4.b1), channel_id=1, source_target_pairs={{0,48},{16,0},{32,16},{48,32},{1,49},{17,1},{33,17},{49,33},{2,50}... | collective-permute-start | bytes 1179656 | tf_op jit(solution)/shard_map/ppermute | solution.py:35
  52.3 11.5 %copy-start.2 = (f32[1,3072]{1,0:T(1,128)S(1)}, f32[1,3072]{1,0:T(1,128)}, u32[]{:S(2)}) copy-start(f32[1,3072]{1,0:T(1,128)} %gate_ref.1) | copy-start | bytes 36868
  58.7 12.0 %copy-start.4 = (bf16[512,384]{1,0:T(8,128)(2,1)}, bf16[512,384]{1,0:T(8,128)(2,1)S(1)}, u32[]{:S(2)}) copy-start(bf16[512,384]{1,0:T(8,128)(2,1)S(1)} %get-tuple-element.17.att_ref) | copy-start | bytes 1179652
  70.7 7.1 %collective-permute-start.14 = (bf16[8,192,384]{2,1,0:T(8,128)(2,1)S(1)}, bf16[8,192,384]{2,1,0:T(8,128)(2,1)S(1)}, u32[]{:S(2)}, u32[]{:S(2)}) collective-permute-start(bf16[8,192,384]{2,1,0:T(8,128)(2,1)S(1)} %get-tuple-element.29), channel_id=1, source_target_pairs={{0,64},{64,0},{128,192},{192,128},{1,65},{65,1},{129,193},{193,129... | collective-permute-start | bytes 3538952 | tf_op jit(solution)/shard_map/ppermute | solution.py:51
  79.1 38.8 %all-to-all-start.5 = ((bf16[8,192,384]{2,1,0:T(8,128)(2,1)}), bf16[8,192,384]{2,1,0:T(8,128)(2,1)}, u32[]{:S(2)}, u32[]{:S(2)}) async-start(bf16[8,192,384]{2,1,0:T(8,128)(2,1)} %add_convert_fusion), calls=%async_computation.5 | async-start | bytes 2359296 | tf_op jit(solution)/shard_map/all_to_all | solution.py:338
  85.8 3.1 %collective-permute-start.9 = (bf16[8,192,384]{2,1,0:T(8,128)(2,1)S(1)}, bf16[8,192,384]{2,1,0:T(8,128)(2,1)S(1)}, u32[]{:S(2)}, u32[]{:S(2)}) collective-permute-start(bf16[8,192,384]{2,1,0:T(8,128)(2,1)S(1)} %all-to-all-done.3.mine_ref), channel_id=1, source_target_pairs={{0,64},{64,0},{128,192},{192,128},{1,65},{65,1},{129,193},{193,129... | collective-permute-start | bytes 3538952 | tf_op jit(solution)/shard_map/ppermute | solution.py:51
  90.8 4.8 %copy-start.5 = (bf16[512,384]{1,0:T(8,128)(2,1)S(1)}, bf16[512,384]{1,0:T(8,128)(2,1)}, u32[]{:S(2)}) copy-start(bf16[512,384]{1,0:T(8,128)(2,1)} %copy-done.4) | copy-start | bytes 1179652
  118.0 19.7 %all-to-all-start.4 = ((bf16[4,3,128,384]{3,2,1,0:T(8,128)(2,1)}), bf16[4,3,128,384]{3,2,1,0:T(8,128)(2,1)S(1)}, u32[]{:S(2)}, u32[]{:S(2)}) async-start(bf16[4,3,128,384]{3,2,1,0:T(8,128)(2,1)} %get-tuple-element.20), calls=%async_computation.4 | async-start | bytes 2359296 | tf_op jit(solution)/shard_map/all_to_all | solution.py:55
  123.4 3.9 %collective-permute-start.15 = (bf16[48,384]{1,0:T(8,128)(2,1)S(1)}, bf16[48,384]{1,0:T(8,128)(2,1)S(1)}, u32[]{:S(2)}, u32[]{:S(2)}) collective-permute-start(bf16[48,384]{1,0:T(8,128)(2,1)S(1)} %get-tuple-element.32), channel_id=1, source_target_pairs={{0,128},{1,129},{2,130},{3,131},{4,132},{5,133},{6,134},{7,135},{8... | collective-permute-start | bytes 110600 | tf_op jit(solution)/shard_map/ppermute | solution.py:51
  124.3 4.3 %collective-permute-start.16 = (bf16[48,384]{1,0:T(8,128)(2,1)S(1)}, bf16[48,384]{1,0:T(8,128)(2,1)S(1)}, u32[]{:S(2)}, u32[]{:S(2)}) collective-permute-start(bf16[48,384]{1,0:T(8,128)(2,1)S(1)} %get-tuple-element.34), channel_id=1, source_target_pairs={{0,1},{1,0},{2,3},{3,2},{4,5},{5,4},{6,7},{7,6},{8,9},{9,8},{10,11... | collective-permute-start | bytes 110600 | tf_op jit(solution)/shard_map/ppermute | solution.py:51
  126.6 4.3 %collective-permute-start.17 = (bf16[48,384]{1,0:T(8,128)(2,1)S(1)}, bf16[48,384]{1,0:T(8,128)(2,1)S(1)}, u32[]{:S(2)}, u32[]{:S(2)}) collective-permute-start(bf16[48,384]{1,0:T(8,128)(2,1)S(1)} %get-tuple-element.33), channel_id=1, source_target_pairs={{0,129},{1,128},{2,131},{3,130},{4,133},{5,132},{6,135},{7,134},{8... | collective-permute-start | bytes 110600 | tf_op jit(solution)/shard_map/ppermute | solution.py:51
  138.5 30.0 %all-to-all-start.6 = ((f32[4,48,384]{2,1,0:T(8,128)}), f32[4,48,384]{2,1,0:T(8,128)S(1)}, u32[]{:S(2)}, u32[]{:S(2)}) async-start(f32[4,48,384]{2,1,0:T(8,128)} %broadcast_in_dim.5), calls=%async_computation.6 | async-start | bytes 589824 | tf_op jit(solution)/shard_map/all_to_all | solution.py:55
  143.5 10.5 %collective-permute-start.10 = (bf16[2,128,384]{2,1,0:T(8,128)(2,1)S(1)}, bf16[2,128,384]{2,1,0:T(8,128)(2,1)S(1)}, u32[]{:S(2)}, u32[]{:S(2)}) collective-permute-start(bf16[2,128,384]{2,1,0:T(8,128)(2,1)S(1)} %get-tuple-element.21), channel_id=1, source_target_pairs={{0,15},{1,0},{2,1},{3,2},{4,3},{5,4},{6,5},{7,6},{8,7},{9,8},{10,9... | collective-permute-start | bytes 589832 | tf_op jit(solution)/shard_map/ppermute | solution.py:51
  143.5 15.4 %collective-permute-start.11 = (bf16[2,128,384]{2,1,0:T(8,128)(2,1)S(1)}, bf16[2,128,384]{2,1,0:T(8,128)(2,1)S(1)}, u32[]{:S(2)}, u32[]{:S(2)}) collective-permute-start(bf16[2,128,384]{2,1,0:T(8,128)(2,1)S(1)} %get-tuple-element.22), channel_id=1, source_target_pairs={{0,31},{1,16},{2,17},{3,18},{4,19},{5,20},{6,21},{7,22},{8,23},{9,... | collective-permute-start | bytes 589832 | tf_op jit(solution)/shard_map/ppermute | solution.py:51
  143.5 19.3 %collective-permute-start.12 = (bf16[2,128,384]{2,1,0:T(8,128)(2,1)S(1)}, bf16[2,128,384]{2,1,0:T(8,128)(2,1)S(1)}, u32[]{:S(2)}, u32[]{:S(2)}) collective-permute-start(bf16[2,128,384]{2,1,0:T(8,128)(2,1)S(1)} %get-tuple-element.23), channel_id=1, source_target_pairs={{0,47},{1,32},{2,33},{3,34},{4,35},{5,36},{6,37},{7,38},{8,39},{9,... | collective-permute-start | bytes 589832 | tf_op jit(solution)/shard_map/ppermute | solution.py:51
  149.6 17.1 %collective-permute-start.13 = (bf16[2,128,384]{2,1,0:T(8,128)(2,1)S(1)}, bf16[2,128,384]{2,1,0:T(8,128)(2,1)S(1)}, u32[]{:S(2)}, u32[]{:S(2)}) collective-permute-start(bf16[2,128,384]{2,1,0:T(8,128)(2,1)S(1)} %get-tuple-element.24), channel_id=1, source_target_pairs={{0,63},{1,48},{2,49},{3,50},{4,51},{5,52},{6,53},{7,54},{8,55},{9,... | collective-permute-start | bytes 589832 | tf_op jit(solution)/shard_map/ppermute | solution.py:51
  (2 other events, 3.5 us)

commit v2 on v1

--- a/solution.py
+++ b/solution.py
@@ -282,6 +282,54 @@
     )(at, own, *halos)
 
 
+SMEM = pl.BlockSpec(memory_space=pltpu.SMEM)
+VMEM = pl.BlockSpec(memory_space=pltpu.VMEM)
+ANY = pl.BlockSpec(memory_space=pl.ANY)
+
+
+def after_those(arrays, after):
+    def kernel(*refs):
+        pass
+
+    return pl.pallas_call(
+        kernel,
+        in_specs=[ANY] * (len(arrays) + len(after)),
+        out_specs=[ANY] * len(arrays),
+        out_shape=[jax.ShapeDtypeStruct(x.shape, x.dtype) for x in arrays],
+        input_output_aliases={i: i for i in range(len(arrays))},
+        compiler_params=params(),
+        cost_estimate=cost(0, 0),
+        name="gate",
+    )(*arrays, *after)
+
+
+def sum_kernel(at_ref, terms_ref, *refs):
+    here_ref, there_ref, scr = refs[-3:]
+    total = terms_ref[0].astype(F32)
+    for i in range(1, terms_ref.shape[0]):
+        total = total + terms_ref[i].astype(F32)
+    half = here_ref.shape[0]
+    scr[0] = total[:half].astype(BF16)
+    scr[1] = total[half:].astype(BF16)
+    here_ref[...] = scr[at_ref[3]]
+    there_ref[...] = scr[1 - at_ref[3]]
+
+
+def sum_terms(at, terms, after):
+    steps, rows, width = terms.shape
+    out = jax.ShapeDtypeStruct((rows // 2, width), BF16)
+    return pl.pallas_call(
+        sum_kernel,
+        in_specs=[SMEM, VMEM] + [ANY] * len(after),
+        out_specs=[VMEM] * 2,
+        out_shape=[out, out],
+        scratch_shapes=[pltpu.VMEM((2, rows // 2, width), BF16)],
+        compiler_params=params(),
+        cost_estimate=cost(steps * rows * width, 2 * steps * rows * width),
+        name="sum_terms",
+    )(at, terms, *after)
+
+
 def shards(q_tok, k_tok, v_tok, d_y, gate, w_out):
     uly = lax.axis_size("uly")
     n_blk = lax.axis_size("blk")
@@ -289,7 +337,7 @@
     core = lax.axis_index("dp") % 2
     lower = lax.axis_index("dp") // 2
     upper = lax.axis_index("blk") % 2
-    at = jnp.stack([here, core]).astype(jnp.int32)
+    at = jnp.stack([here, core, lower, upper]).astype(jnp.int32)
     part = q_tok.shape[1]
     width = w_out.shape[1]
     rows = w_out.shape[0]
@@ -345,25 +393,22 @@
         routed(h, ["uly", "blk"], lambda c, d=d: dict(uly=c["uly"] + d, blk=c["blk"] - 1))
         for d, h in enumerate(halos)
     ]
+    (own,) = after_those([own], halos[:2])
     own = exchange(own, "uly", 0)
     grad_q, grad_k, grad_v = assemble(at, own, halos)
 
-    column = jnp.sum(terms.astype(F32), axis=0).astype(BF16).reshape(2, 2, rows // 4, width)
-
-    def x_piece(du, dl):
-        piece = lax.dynamic_index_in_dim(column, upper ^ du, 0, keepdims=False)
-        return lax.dynamic_index_in_dim(piece, lower ^ dl, 0, keepdims=False)
-
-    share = x_piece(0, 0).astype(F32)
-    for du, dl in ((0, 1), (1, 0), (1, 1)):
-        share = share + routed(
-            x_piece(du, dl),
-            ["dp", "blk"],
-            lambda c, du=du, dl=dl: dict(dp=c["dp"] ^ (2 * dl), blk=c["blk"] ^ du),
-        ).astype(F32)
-    shares = exchange(jnp.broadcast_to(share[None], (4,) + share.shape), "dp", 0)
-    grad_w = (
-        shares.reshape(2, 2, rows // 4, width).transpose(1, 0, 2, 3).reshape(rows, width)
+    here, there = sum_terms(at, terms, halos)
+    near_x = routed(here, ["dp"], lambda c: dict(dp=c["dp"] ^ 2))
+    far_x = [
+        routed(there, ["dp", "blk"], lambda c, i=i: dict(dp=c["dp"] ^ i, blk=c["blk"] ^ 1))
+        for i in (0, 2)
+    ]
+    mine = (here.astype(F32) + near_x.astype(F32)) + (
+        far_x[0].astype(F32) + far_x[1].astype(F32)
+    )
+    other = swap_core(mine)
+    grad_w = jnp.concatenate(
+        [jnp.where(core == 0, mine, other), jnp.where(core == 0, other, mine)], axis=0
     )
     return grad_q, grad_k, grad_v, grad_w
 

time: 170 us -> 148 us (0.87)
  waiting for transfers between devices: 61.2 us -> 36.7 us
  starting transfers between devices: 68.2 us -> 70.5 us
    all_to_all x1, waiting for transfers between devices: 16.2 us -> 0.01 us  [shards(): lax.all_to_all(both, 'blk', split_axis=0, concat_axis=0, tiled=True, axis...]
    ppermute x10 -> x11, starting transfers between devices: 19.1 us -> 26.5 us  [routed(): return lax.ppermute(x, tuple(axes), pairs)]
    all_to_all x5 -> x4, waiting for transfers between devices: 15.4 us -> 8.59 us  [exchange(): lax.all_to_all(x, axis, split_axis=split, concat_axis=split, tiled=True)]
    all_to_all x5 -> x4, starting transfers between devices: 21.1 us -> 16 us  [exchange(): lax.all_to_all(x, axis, split_axis=split, concat_axis=split, tiled=True)]
    ppermute x10 -> x11, waiting for transfers between devices: 24.6 us -> 23.1 us  [routed(): return lax.ppermute(x, tuple(axes), pairs)]
    unnamed x21 -> x25, local copies, waits for them, and re-layouts: 5.25 us -> 5.26 us
  transfers between devices with their start and end apart: 25 -> 25, of which waited for: 13 -> 12; matrix products, arithmetic and copies ran while one was open for 4% -> 5% of each run, Pallas kernels for 14% -> 16%
where the time goes in v2:
time: 148 us; the launch traced here: 146 us
  starting transfers between devices  70.5 us (48%)
  waiting for transfers between devices  36.7 us (25%)
  Pallas kernels  25.2 us (17%)
  local copies, waits for them, and re-layouts  10.1 us (7%)
  other arithmetic  2.32 us (2%)
    ppermute x11, starting transfers between devices, routed(): return lax.ppermute(x, tuple(axes), pairs)  26.5 us
    ppermute x11, waiting for transfers between devices, routed(): return lax.ppermute(x, tuple(axes), pairs)  23.1 us
    all_to_all x4, starting transfers between devices, exchange(): lax.all_to_all(x, axis, split_axis=split, concat_axis=split, tiled=True)  16 us
    ppermute x8, starting transfers between devices, shift(): return lax.ppermute(x, axis, [(i, (i + distance) % n) for i in range(n)])  12.8 us
    all_to_all x4, waiting for transfers between devices, exchange(): lax.all_to_all(x, axis, split_axis=split, concat_axis=split, tiled=True)  8.59 us
    all_to_all x1, starting transfers between devices, shards(): lax.all_to_all(jnp.broadcast_to(w_pair[None], (z_size,) + w_pair.shape),...  8.53 us
    pallas_call x1, Pallas kernels, weight_term(): pl.pallas_call(weight_kernel, grid=(steps,), in_specs=[pl.BlockSpec(memor...  6.89 us
    all_to_all x1, starting transfers between devices, shards(): lax.all_to_all(both, 'blk', split_axis=0, concat_axis=0, tiled=True, axis...  6.65 us
  transfers between devices with their start and end apart: 25, of which 12 were waited for; matrix products, arithmetic and copies ran while one was open for 5% of the time, Pallas kernels for 16%

profile of v2, /device:TPU:1, one launch (start us, length us, event | category | flops | bytes accessed | tf_op | source)
XLA Modules:
  0.0 145.7 jit_solution(5348084276964289049)
XLA Ops:
  2.9 5.0 %all-to-all-start.1 = ((bf16[4,128,384]{2,1,0:T(8,128)(2,1)}), bf16[4,128,384]{2,1,0:T(8,128)(2,1)S(1)}, u32[]{:S(2)}, u32[]{:S(2)}) async-start(bf16[4,128,384]{2,1,0:T(8,128)(2,1)} %bitcast.7), calls=%async_computation.1 | async-start | bytes 786432 | tf_op jit(solution)/shard_map/all_to_all | solution.py:55
  7.9 2.8 %collective-permute-start.8 = (bf16[96,384]{1,0:T(8,128)(2,1)S(1)}, bf16[96,384]{1,0:T(8,128)(2,1)S(1)}, u32[]{:S(2)}, u32[]{:S(2)}) collective-permute-start(bf16[96,384]{1,0:T(8,128)(2,1)S(1)} %constant_dynamic-slice_fusion), channel_id=1, source_target_pairs={{0,1},{1,0},{2,3},{3,2},{4,5},{5,4},{6,7},{7,6},{8,9},{9,8},{10,11... | collective-permute-start | bytes 221192 | tf_op jit(solution)/shard_map/ppermute | solution.py:51
  11.9 2.5 %all-to-all-done.1.k_ref = bf16[4,128,384]{2,1,0:T(8,128)(2,1)S(1)} async-done(((bf16[4,128,384]{2,1,0:T(8,128)(2,1)}), bf16[4,128,384]{2,1,0:T(8,128)(2,1)S(1)}, u32[]{:S(2)}, u32[]{:S(2)}) %all-to-all-start.1) | async-done | bytes 393248 | tf_op jit(solution)/shard_map/all_to_all | solution.py:55
  14.4 3.6 %all-to-all-start.2 = ((bf16[4,128,384]{2,1,0:T(8,128)(2,1)}), bf16[4,128,384]{2,1,0:T(8,128)(2,1)S(1)}, u32[]{:S(2)}, u32[]{:S(2)}) async-start(bf16[4,128,384]{2,1,0:T(8,128)(2,1)} %bitcast.9), calls=%async_computation.2 | async-start | bytes 786432 | tf_op jit(solution)/shard_map/all_to_all | solution.py:55
  22.8 3.1 %collective-permute-start = (bf16[4,128,384]{2,1,0:T(8,128)(2,1)S(1)}, bf16[4,128,384]{2,1,0:T(8,128)(2,1)S(1)}, u32[]{:S(2)}, u32[]{:S(2)}) collective-permute-start(bf16[4,128,384]{2,1,0:T(8,128)(2,1)S(1)} %all-to-all-done.1.k_ref), channel_id=1, source_target_pairs={{0,1},{1,2},{2,3},{3,4},{4,5},{5,6},{6,7},{7,8},{8,9},{9,10},{10,1... | collective-permute-start | bytes 1179656 | tf_op jit(solution)/shard_map/ppermute | solution.py:35
  25.9 3.5 %all-to-all-start = ((bf16[4,128,384]{2,1,0:T(8,128)(2,1)}), bf16[4,128,384]{2,1,0:T(8,128)(2,1)S(1)}, u32[]{:S(2)}, u32[]{:S(2)}) async-start(bf16[4,128,384]{2,1,0:T(8,128)(2,1)} %bitcast.5), calls=%async_computation | async-start | bytes 786432 | tf_op jit(solution)/shard_map/all_to_all | solution.py:55
  29.4 1.7 %collective-permute-start.1 = (bf16[4,128,384]{2,1,0:T(8,128)(2,1)S(1)}, bf16[4,128,384]{2,1,0:T(8,128)(2,1)}, u32[]{:S(2)}, u32[]{:S(2)}) collective-permute-start(bf16[4,128,384]{2,1,0:T(8,128)(2,1)S(1)} %all-to-all-done.2.v_ref), channel_id=1, source_target_pairs={{0,1},{1,2},{2,3},{3,4},{4,5},{5,6},{6,7},{7,8},{8,9},{9,10},{10,1... | collective-permute-start | bytes 1179656 | tf_op jit(solution)/shard_map/ppermute | solution.py:35
  31.1 6.1 %all-to-all-done.q_ref = bf16[4,128,384]{2,1,0:T(8,128)(2,1)S(1)} async-done(((bf16[4,128,384]{2,1,0:T(8,128)(2,1)}), bf16[4,128,384]{2,1,0:T(8,128)(2,1)S(1)}, u32[]{:S(2)}, u32[]{:S(2)}) %all-to-all-start) | async-done | bytes 393248 | tf_op jit(solution)/shard_map/all_to_all | solution.py:55
  38.3 8.5 %all-to-all-start.3 = ((bf16[8,192,384]{2,1,0:T(8,128)(2,1)}), bf16[8,192,384]{2,1,0:T(8,128)(2,1)S(1)}, u32[]{:S(2)}, u32[]{:S(2)}) async-start(bf16[8,192,384]{2,1,0:T(8,128)(2,1)} %broadcast_in_dim.2), calls=%async_computation.3 | async-start | bytes 2359296 | tf_op jit(solution)/shard_map/all_to_all | solution.py:356
  47.4 2.1 %collective-permute-start.5 = (bf16[64,3072]{1,0:T(8,128)(2,1)}, bf16[64,3072]{1,0:T(8,128)(2,1)}, u32[]{:S(2)}, u32[]{:S(2)}) collective-permute-start(bf16[64,3072]{1,0:T(8,128)(2,1)} %get-tuple-element.35), channel_id=1, source_target_pairs={{0,48},{16,0},{32,16},{48,32},{1,49},{17,1},{33,17},{49,33},{2,50}... | collective-permute-start | bytes 1179656 | tf_op jit(solution)/shard_map/ppermute | solution.py:35
  49.5 2.7 %collective-permute-start.7 = (bf16[64,3072]{1,0:T(8,128)(2,1)}, bf16[64,3072]{1,0:T(8,128)(2,1)}, u32[]{:S(2)}, u32[]{:S(2)}) collective-permute-start(bf16[64,3072]{1,0:T(8,128)(2,1)} %collective-permute-done.4.b1), channel_id=1, source_target_pairs={{0,48},{16,0},{32,16},{48,32},{1,49},{17,1},{33,17},{49,33},{2,50}... | collective-permute-start | bytes 1179656 | tf_op jit(solution)/shard_map/ppermute | solution.py:35
  52.3 4.9 %forward.1 = (bf16[3,1024,512]{2,1,0:T(8,128)(2,1)S(1)}, bf16[512,384]{1,0:T(8,128)(2,1)S(1)}) custom-call(bf16[4,128,384]{2,1,0:T(8,128)(2,1)S(1)} %all-to-all-done.q_ref, bf16[4,128,384]{2,1,0:T(8,128)(2,1)S(1)} %all-to-all-done.1.k_ref, bf16[4,128,384]{2,1,0:T(8,128)(2,1)S(1)} %all-to-all-done.2.v_ref, ...), custom_call_target="tpu_custom_call" | custom-call | flops 805306368 | bytes 5505024 | tf_op jit(solution)/shard_map/forward/pallas_call | solution.py:86
  58.8 5.0 %collective-permute-done.6.a3 = bf16[64,3072]{1,0:T(8,128)(2,1)} collective-permute-done((bf16[64,3072]{1,0:T(8,128)(2,1)}, bf16[64,3072]{1,0:T(8,128)(2,1)}, u32[]{:S(2)}, u32[]{:S(2)}) %collective-permute-start.6) | collective-permute-done | bytes 393248 | tf_op jit(solution)/shard_map/ppermute | solution.py:35
  63.8 6.9 %weight_term.1 = (bf16[512,3072]{1,0:T(8,128)(2,1)}, bf16[8,192,384]{2,1,0:T(8,128)(2,1)S(1)}, bf16[8,192,384]{2,1,0:T(8,128)(2,1)S(1)}) custom-call(s32[4]{0:T(128)S(1)} %pad_add_fusion.at_ref, bf16[128,3072]{1,0:T(8,128)(2,1)S(1)} %bitcast.15, bf16[64,3072]{1,0:T(8,128)(2,1)} %collective-permute-done.2.a1, bf16[64,3072]{1,0:T(8,128)(2,1)} %collective-permute-done.3.a2, ...), custom_call_target="tpu_custom_call" | custom-call | flops 1207959552 | bytes 8650752 | tf_op jit(solution)/shard_map/weight_term/pallas_call | solution.py:196
  70.7 4.6 %collective-permute-start.14 = (bf16[8,192,384]{2,1,0:T(8,128)(2,1)S(1)}, bf16[8,192,384]{2,1,0:T(8,128)(2,1)S(1)}, u32[]{:S(2)}, u32[]{:S(2)}) collective-permute-start(bf16[8,192,384]{2,1,0:T(8,128)(2,1)S(1)} %get-tuple-element.31), channel_id=1, source_target_pairs={{0,64},{64,0},{128,192},{192,128},{1,65},{65,1},{129,193},{193,129... | collective-permute-start | bytes 3538952 | tf_op jit(solution)/shard_map/ppermute | solution.py:51
  75.3 2.5 %collective-permute-done.14 = bf16[8,192,384]{2,1,0:T(8,128)(2,1)S(1)} collective-permute-done((bf16[8,192,384]{2,1,0:T(8,128)(2,1)S(1)}, bf16[8,192,384]{2,1,0:T(8,128)(2,1)S(1)}, u32[]{:S(2)}, u32[]{:S(2)}) %collective-permute-start.14) | collective-permute-done | bytes 1179680 | tf_op jit(solution)/shard_map/ppermute | solution.py:51
  79.2 6.7 %all-to-all-start.5 = ((bf16[8,192,384]{2,1,0:T(8,128)(2,1)}), bf16[8,192,384]{2,1,0:T(8,128)(2,1)S(1)}, u32[]{:S(2)}, u32[]{:S(2)}) async-start(bf16[8,192,384]{2,1,0:T(8,128)(2,1)} %add_convert_fusion), calls=%async_computation.5 | async-start | bytes 2359296 | tf_op jit(solution)/shard_map/all_to_all | solution.py:386
  86.5 2.5 %collective-permute-done.9.other_ref = bf16[8,192,384]{2,1,0:T(8,128)(2,1)S(1)} collective-permute-done((bf16[8,192,384]{2,1,0:T(8,128)(2,1)S(1)}, bf16[8,192,384]{2,1,0:T(8,128)(2,1)S(1)}, u32[]{:S(2)}, u32[]{:S(2)}) %collective-permute-start.9) | collective-permute-done | bytes 1179680 | tf_op jit(solution)/shard_map/ppermute | solution.py:51
  88.9 1.9 %copy-done = bf16[512,3072]{1,0:T(8,128)(2,1)S(1)} copy-done((bf16[512,3072]{1,0:T(8,128)(2,1)S(1)}, bf16[512,3072]{1,0:T(8,128)(2,1)}, u32[]{:S(2)}) %copy-start) | copy-done | bytes 3145752
  90.8 4.8 %project.1.g_ref = bf16[512,384]{1,0:T(8,128)(2,1)S(1)} custom-call(s32[4]{0:T(128)S(1)} %pad_add_fusion.at_ref, bf16[512,3072]{1,0:T(8,128)(2,1)S(1)} %copy-done, bf16[8,192,384]{2,1,0:T(8,128)(2,1)S(1)} %all-to-all-done.3.mine_ref, bf16[8,192,384]{2,1,0:T(8,128)(2,1)S(1)} %collective-permute-done.9.other_ref), custom_call_target="tpu_custom_call" | custom-call | flops 1207959552 | bytes 5505024 | tf_op jit(solution)/shard_map/project/pallas_call | solution.py:238
  95.6 6.2 %backward.1 = (bf16[4,3,128,384]{3,2,1,0:T(8,128)(2,1)}, bf16[2,128,384]{2,1,0:T(8,128)(2,1)S(1)}, bf16[2,128,384]{2,1,0:T(8,128)(2,1)S(1)}, bf16[2,128,384]{2,1,0:T(8,128)(2,1)}, bf16[2,128,384]{2,1,0:T(8,128)(2,1)}) custom-call(s32[4]{0:T(128)S(1)} %pad_add_fusion.at_ref, bf16[4,128,384]{2,1,0:T(8,128)(2,1)S(1)} %all-to-all-done.q_ref, ...), custom_call_target="tpu_custom_call" | custom-call | flops 1610612736 | bytes 7864320 | tf_op jit(solution)/shard_map/backward/pallas_call | solution.py:145
  101.8 4.6 %collective-permute-start.10 = (bf16[2,128,384]{2,1,0:T(8,128)(2,1)S(1)}, bf16[2,128,384]{2,1,0:T(8,128)(2,1)S(1)}, u32[]{:S(2)}, u32[]{:S(2)}) collective-permute-start(bf16[2,128,384]{2,1,0:T(8,128)(2,1)S(1)} %get-tuple-element.23), channel_id=1, source_target_pairs={{0,15},{1,0},{2,1},{3,2},{4,3},{5,4},{6,5},{7,6},{8,7},{9,8},{10,9... | collective-permute-start | bytes 589832 | tf_op jit(solution)/shard_map/ppermute | solution.py:51
  106.6 7.0 %collective-permute-start.12 = (bf16[2,128,384]{2,1,0:T(8,128)(2,1)}, bf16[2,128,384]{2,1,0:T(8,128)(2,1)S(1)}, u32[]{:S(2)}, u32[]{:S(2)}) collective-permute-start(bf16[2,128,384]{2,1,0:T(8,128)(2,1)} %get-tuple-element.25), channel_id=1, source_target_pairs={{0,47},{1,32},{2,33},{3,34},{4,35},{5,36},{6,37},{7,38},{8,39},{9,... | collective-permute-start | bytes 589832 | tf_op jit(solution)/shard_map/ppermute | solution.py:51
  113.8 3.1 %collective-permute-done.10.refs_1_.h0.refs_0_ = bf16[2,128,384]{2,1,0:T(8,128)(2,1)S(1)} collective-permute-done((bf16[2,128,384]{2,1,0:T(8,128)(2,1)S(1)}, bf16[2,128,384]{2,1,0:T(8,128)(2,1)S(1)}, u32[]{:S(2)}, u32[]{:S(2)}) %collective-permute-start.10) | collective-permute-done | bytes 196640 | tf_op jit(solution)/shard_map/ppermute | solution.py:51
  116.8 4.2 %collective-permute-done.11.refs_2_.h1.refs_1_ = bf16[2,128,384]{2,1,0:T(8,128)(2,1)S(1)} collective-permute-done((bf16[2,128,384]{2,1,0:T(8,128)(2,1)S(1)}, bf16[2,128,384]{2,1,0:T(8,128)(2,1)S(1)}, u32[]{:S(2)}, u32[]{:S(2)}) %collective-permute-start.11) | collective-permute-done | bytes 196640 | tf_op jit(solution)/shard_map/ppermute | solution.py:51
  121.0 3.9 %all-to-all-start.4 = ((bf16[4,3,128,384]{3,2,1,0:T(8,128)(2,1)}), bf16[4,3,128,384]{3,2,1,0:T(8,128)(2,1)S(1)}, u32[]{:S(2)}, u32[]{:S(2)}) async-start(bf16[4,3,128,384]{3,2,1,0:T(8,128)(2,1)} %gate.1), calls=%async_computation.4 | async-start | bytes 2359296 | tf_op jit(solution)/shard_map/all_to_all | solution.py:55
  125.4 4.2 %collective-permute-done.13.h3.refs_3_ = bf16[2,128,384]{2,1,0:T(8,128)(2,1)S(1)} collective-permute-done((bf16[2,128,384]{2,1,0:T(8,128)(2,1)}, bf16[2,128,384]{2,1,0:T(8,128)(2,1)S(1)}, u32[]{:S(2)}, u32[]{:S(2)}) %collective-permute-start.13) | collective-permute-done | bytes 196640 | tf_op jit(solution)/shard_map/ppermute | solution.py:51
  131.2 2.8 %collective-permute-start.16 = (bf16[96,384]{1,0:T(8,128)(2,1)S(1)}, bf16[96,384]{1,0:T(8,128)(2,1)S(1)}, u32[]{:S(2)}, u32[]{:S(2)}) collective-permute-start(bf16[96,384]{1,0:T(8,128)(2,1)S(1)} %get-tuple-element.33), channel_id=1, source_target_pairs={{0,1},{1,0},{2,3},{3,2},{4,5},{5,4},{6,7},{7,6},{8,9},{9,8},{10,11... | collective-permute-start | bytes 221192 | tf_op jit(solution)/shard_map/ppermute | solution.py:51
  134.3 2.3 %collective-permute-done.16 = bf16[96,384]{1,0:T(8,128)(2,1)S(1)} collective-permute-done((bf16[96,384]{1,0:T(8,128)(2,1)S(1)}, bf16[96,384]{1,0:T(8,128)(2,1)S(1)}, u32[]{:S(2)}, u32[]{:S(2)}) %collective-permute-start.16) | collective-permute-done | bytes 73760 | tf_op jit(solution)/shard_map/ppermute | solution.py:51
  136.6 3.0 %collective-permute-done.17 = bf16[96,384]{1,0:T(8,128)(2,1)S(1)} collective-permute-done((bf16[96,384]{1,0:T(8,128)(2,1)S(1)}, bf16[96,384]{1,0:T(8,128)(2,1)S(1)}, u32[]{:S(2)}, u32[]{:S(2)}) %collective-permute-start.17) | collective-permute-done | bytes 73760 | tf_op jit(solution)/shard_map/ppermute | solution.py:51
  139.6 2.6 %collective-permute-start.18 = (f32[96,384]{1,0:T(8,128)S(1)}, f32[96,384]{1,0:T(8,128)S(1)}, u32[]{:S(2)}, u32[]{:S(2)}) collective-permute-start(f32[96,384]{1,0:T(8,128)S(1)} %add_add_fusion), channel_id=1, source_target_pairs={{0,64},{64,0},{128,192},{192,128},{1,65},{65,1},{129,193},{193,129... | collective-permute-start | bytes 442376 | tf_op jit(solution)/shard_map/ppermute | solution.py:51
  143.9 1.8 %assemble.1 = (bf16[1,128,1536]{2,1,0:T(8,128)(2,1)}, bf16[1,128,1536]{2,1,0:T(8,128)(2,1)}, bf16[1,128,1536]{2,1,0:T(8,128)(2,1)}) custom-call(s32[4]{0:T(128)S(1)} %pad_add_fusion.at_ref, bf16[4,3,128,384]{3,2,1,0:T(8,128)(2,1)S(1)} %all-to-all-done.4.own_ref, bf16[2,128,384]{2,1,0:T(8,128)(2,1)S(1)} %collective-permute-done.10.refs_1_.h0.refs_0_, ...), custom_call_target="tpu_custom_call" | custom-call | flops 393216 | bytes 3145728 | tf_op jit(solution)/shard_map/assemble/pallas_call | solution.py:273
  (63 shorter events, 18.1 us)
Async XLA Ops:
  0.6 7.2 %copy-start.10 = (bf16[192,384]{1,0:T(8,128)(2,1)S(1)}, bf16[192,384]{1,0:T(8,128)(2,1)}, u32[]{:S(2)}) copy-start(bf16[192,384]{1,0:T(8,128)(2,1)} %param.11) | copy-start | bytes 442372
  0.6 10.1 %copy-start.8 = (bf16[1,128,1536]{2,1,0:T(8,128)(2,1)S(1)}, bf16[1,128,1536]{2,1,0:T(8,128)(2,1)}, u32[]{:S(2)}) copy-start(bf16[1,128,1536]{2,1,0:T(8,128)(2,1)} %param.8) | copy-start | bytes 1179652
  2.9 11.5 %all-to-all-start.1 = ((bf16[4,128,384]{2,1,0:T(8,128)(2,1)}), bf16[4,128,384]{2,1,0:T(8,128)(2,1)S(1)}, u32[]{:S(2)}, u32[]{:S(2)}) async-start(bf16[4,128,384]{2,1,0:T(8,128)(2,1)} %bitcast.7), calls=%async_computation.1 | async-start | bytes 786432 | tf_op jit(solution)/shard_map/all_to_all | solution.py:55
  7.9 10.1 %copy-start.1 = (bf16[1,128,3072]{2,1,0:T(8,128)(2,1)S(1)}, bf16[1,128,3072]{2,1,0:T(8,128)(2,1)}, u32[]{:S(2)}) copy-start(bf16[1,128,3072]{2,1,0:T(8,128)(2,1)} %param.9) | copy-start | bytes 2359300
  7.9 21.5 %collective-permute-start.8 = (bf16[96,384]{1,0:T(8,128)(2,1)S(1)}, bf16[96,384]{1,0:T(8,128)(2,1)S(1)}, u32[]{:S(2)}, u32[]{:S(2)}) collective-permute-start(bf16[96,384]{1,0:T(8,128)(2,1)S(1)} %constant_dynamic-slice_fusion), channel_id=1, source_target_pairs={{0,1},{1,0},{2,3},{3,2},{4,5},{5,4},{6,7},{7,6},{8,9},{9,8},{10,11... | collective-permute-start | bytes 221192 | tf_op jit(solution)/shard_map/ppermute | solution.py:51
  14.4 7.3 %copy-start.9 = (bf16[1,128,1536]{2,1,0:T(8,128)(2,1)S(1)}, bf16[1,128,1536]{2,1,0:T(8,128)(2,1)}, u32[]{:S(2)}) copy-start(bf16[1,128,1536]{2,1,0:T(8,128)(2,1)} %param.6) | copy-start | bytes 1179652
  14.4 11.5 %all-to-all-start.2 = ((bf16[4,128,384]{2,1,0:T(8,128)(2,1)}), bf16[4,128,384]{2,1,0:T(8,128)(2,1)S(1)}, u32[]{:S(2)}, u32[]{:S(2)}) async-start(bf16[4,128,384]{2,1,0:T(8,128)(2,1)} %bitcast.9), calls=%async_computation.2 | async-start | bytes 786432 | tf_op jit(solution)/shard_map/all_to_all | solution.py:55
  19.0 28.4 %collective-permute-start.2 = (bf16[64,3072]{1,0:T(8,128)(2,1)}, bf16[64,3072]{1,0:T(8,128)(2,1)}, u32[]{:S(2)}, u32[]{:S(2)}) collective-permute-start(bf16[64,3072]{1,0:T(8,128)(2,1)} %get-tuple-element.35), channel_id=1, source_target_pairs={{0,16},{16,32},{32,48},{48,0},{1,17},{17,33},{33,49},{49,1},{2,18}... | collective-permute-start | bytes 1179656 | tf_op jit(solution)/shard_map/ppermute | solution.py:35
  20.4 29.1 %collective-permute-start.4 = (bf16[64,3072]{1,0:T(8,128)(2,1)}, bf16[64,3072]{1,0:T(8,128)(2,1)}, u32[]{:S(2)}, u32[]{:S(2)}) collective-permute-start(bf16[64,3072]{1,0:T(8,128)(2,1)} %get-tuple-element.34), channel_id=1, source_target_pairs={{0,48},{16,0},{32,16},{48,32},{1,49},{17,1},{33,17},{49,33},{2,50}... | collective-permute-start | bytes 1179656 | tf_op jit(solution)/shard_map/ppermute | solution.py:35
  22.8 26.7 %collective-permute-start = (bf16[4,128,384]{2,1,0:T(8,128)(2,1)S(1)}, bf16[4,128,384]{2,1,0:T(8,128)(2,1)S(1)}, u32[]{:S(2)}, u32[]{:S(2)}) collective-permute-start(bf16[4,128,384]{2,1,0:T(8,128)(2,1)S(1)} %all-to-all-done.1.k_ref), channel_id=1, source_target_pairs={{0,1},{1,2},{2,3},{3,4},{4,5},{5,6},{6,7},{7,8},{8,9},{9,10},{10,1... | collective-permute-start | bytes 1179656 | tf_op jit(solution)/shard_map/ppermute | solution.py:35
  25.9 11.3 %all-to-all-start = ((bf16[4,128,384]{2,1,0:T(8,128)(2,1)}), bf16[4,128,384]{2,1,0:T(8,128)(2,1)S(1)}, u32[]{:S(2)}, u32[]{:S(2)}) async-start(bf16[4,128,384]{2,1,0:T(8,128)(2,1)} %bitcast.5), calls=%async_computation | async-start | bytes 786432 | tf_op jit(solution)/shard_map/all_to_all | solution.py:55
  29.4 22.9 %collective-permute-start.1 = (bf16[4,128,384]{2,1,0:T(8,128)(2,1)S(1)}, bf16[4,128,384]{2,1,0:T(8,128)(2,1)}, u32[]{:S(2)}, u32[]{:S(2)}) collective-permute-start(bf16[4,128,384]{2,1,0:T(8,128)(2,1)S(1)} %all-to-all-done.2.v_ref), channel_id=1, source_target_pairs={{0,1},{1,2},{2,3},{3,4},{4,5},{5,6},{6,7},{7,8},{8,9},{9,10},{10,1... | collective-permute-start | bytes 1179656 | tf_op jit(solution)/shard_map/ppermute | solution.py:35
  38.3 40.9 %all-to-all-start.3 = ((bf16[8,192,384]{2,1,0:T(8,128)(2,1)}), bf16[8,192,384]{2,1,0:T(8,128)(2,1)S(1)}, u32[]{:S(2)}, u32[]{:S(2)}) async-start(bf16[8,192,384]{2,1,0:T(8,128)(2,1)} %broadcast_in_dim.2), calls=%async_computation.3 | async-start | bytes 2359296 | tf_op jit(solution)/shard_map/all_to_all | solution.py:356
  46.8 12.0 %collective-permute-start.3 = (bf16[64,3072]{1,0:T(8,128)(2,1)}, bf16[64,3072]{1,0:T(8,128)(2,1)}, u32[]{:S(2)}, u32[]{:S(2)}) collective-permute-start(bf16[64,3072]{1,0:T(8,128)(2,1)} %get-tuple-element.34), channel_id=1, source_target_pairs={{0,16},{16,32},{32,48},{48,0},{1,17},{17,33},{33,49},{49,1},{2,18}... | collective-permute-start | bytes 1179656 | tf_op jit(solution)/shard_map/ppermute | solution.py:35
  47.4 11.4 %collective-permute-start.5 = (bf16[64,3072]{1,0:T(8,128)(2,1)}, bf16[64,3072]{1,0:T(8,128)(2,1)}, u32[]{:S(2)}, u32[]{:S(2)}) collective-permute-start(bf16[64,3072]{1,0:T(8,128)(2,1)} %get-tuple-element.35), channel_id=1, source_target_pairs={{0,48},{16,0},{32,16},{48,32},{1,49},{17,1},{33,17},{49,33},{2,50}... | collective-permute-start | bytes 1179656 | tf_op jit(solution)/shard_map/ppermute | solution.py:35
  49.5 14.3 %collective-permute-start.6 = (bf16[64,3072]{1,0:T(8,128)(2,1)}, bf16[64,3072]{1,0:T(8,128)(2,1)}, u32[]{:S(2)}, u32[]{:S(2)}) collective-permute-start(bf16[64,3072]{1,0:T(8,128)(2,1)} %collective-permute-done.2.a1), channel_id=1, source_target_pairs={{0,16},{16,32},{32,48},{48,0},{1,17},{17,33},{33,49},{49,1},{2,18}... | collective-permute-start | bytes 1179656 | tf_op jit(solution)/shard_map/ppermute | solution.py:35
  49.5 7.6 %copy-start.2 = (bf16[4,128,384]{2,1,0:T(8,128)(2,1)}, bf16[4,128,384]{2,1,0:T(8,128)(2,1)S(1)}, u32[]{:S(2)}) copy-start(bf16[4,128,384]{2,1,0:T(8,128)(2,1)S(1)} %collective-permute-done.kp_ref) | copy-start | bytes 1179652
  49.5 14.3 %collective-permute-start.7 = (bf16[64,3072]{1,0:T(8,128)(2,1)}, bf16[64,3072]{1,0:T(8,128)(2,1)}, u32[]{:S(2)}, u32[]{:S(2)}) collective-permute-start(bf16[64,3072]{1,0:T(8,128)(2,1)} %collective-permute-done.4.b1), channel_id=1, source_target_pairs={{0,48},{16,0},{32,16},{48,32},{1,49},{17,1},{33,17},{49,33},{2,50}... | collective-permute-start | bytes 1179656 | tf_op jit(solution)/shard_map/ppermute | solution.py:35
  52.3 11.5 %copy-start.4 = (f32[1,3072]{1,0:T(1,128)S(1)}, f32[1,3072]{1,0:T(1,128)}, u32[]{:S(2)}) copy-start(f32[1,3072]{1,0:T(1,128)} %gate_ref.1) | copy-start | bytes 36868
  58.8 11.9 %copy-start.6 = (bf16[512,384]{1,0:T(8,128)(2,1)}, bf16[512,384]{1,0:T(8,128)(2,1)S(1)}, u32[]{:S(2)}) copy-start(bf16[512,384]{1,0:T(8,128)(2,1)S(1)} %get-tuple-element.19.att_ref) | copy-start | bytes 1179652
  70.7 7.1 %collective-permute-start.14 = (bf16[8,192,384]{2,1,0:T(8,128)(2,1)S(1)}, bf16[8,192,384]{2,1,0:T(8,128)(2,1)S(1)}, u32[]{:S(2)}, u32[]{:S(2)}) collective-permute-start(bf16[8,192,384]{2,1,0:T(8,128)(2,1)S(1)} %get-tuple-element.31), channel_id=1, source_target_pairs={{0,64},{64,0},{128,192},{192,128},{1,65},{65,1},{129,193},{193,129... | collective-permute-start | bytes 3538952 | tf_op jit(solution)/shard_map/ppermute | solution.py:51
  79.2 41.9 %all-to-all-start.5 = ((bf16[8,192,384]{2,1,0:T(8,128)(2,1)}), bf16[8,192,384]{2,1,0:T(8,128)(2,1)S(1)}, u32[]{:S(2)}, u32[]{:S(2)}) async-start(bf16[8,192,384]{2,1,0:T(8,128)(2,1)} %add_convert_fusion), calls=%async_computation.5 | async-start | bytes 2359296 | tf_op jit(solution)/shard_map/all_to_all | solution.py:386
  85.8 3.1 %collective-permute-start.9 = (bf16[8,192,384]{2,1,0:T(8,128)(2,1)S(1)}, bf16[8,192,384]{2,1,0:T(8,128)(2,1)S(1)}, u32[]{:S(2)}, u32[]{:S(2)}) collective-permute-start(bf16[8,192,384]{2,1,0:T(8,128)(2,1)S(1)} %all-to-all-done.3.mine_ref), channel_id=1, source_target_pairs={{0,64},{64,0},{128,192},{192,128},{1,65},{65,1},{129,193},{193,129... | collective-permute-start | bytes 3538952 | tf_op jit(solution)/shard_map/ppermute | solution.py:51
  101.8 15.0 %collective-permute-start.10 = (bf16[2,128,384]{2,1,0:T(8,128)(2,1)S(1)}, bf16[2,128,384]{2,1,0:T(8,128)(2,1)S(1)}, u32[]{:S(2)}, u32[]{:S(2)}) collective-permute-start(bf16[2,128,384]{2,1,0:T(8,128)(2,1)S(1)} %get-tuple-element.23), channel_id=1, source_target_pairs={{0,15},{1,0},{2,1},{3,2},{4,3},{5,4},{6,5},{7,6},{8,7},{9,8},{10,9... | collective-permute-start | bytes 589832 | tf_op jit(solution)/shard_map/ppermute | solution.py:51
  106.4 14.6 %collective-permute-start.11 = (bf16[2,128,384]{2,1,0:T(8,128)(2,1)S(1)}, bf16[2,128,384]{2,1,0:T(8,128)(2,1)S(1)}, u32[]{:S(2)}, u32[]{:S(2)}) collective-permute-start(bf16[2,128,384]{2,1,0:T(8,128)(2,1)S(1)} %get-tuple-element.24), channel_id=1, source_target_pairs={{0,31},{1,16},{2,17},{3,18},{4,19},{5,20},{6,21},{7,22},{8,23},{9,... | collective-permute-start | bytes 589832 | tf_op jit(solution)/shard_map/ppermute | solution.py:51
  106.6 18.7 %collective-permute-start.12 = (bf16[2,128,384]{2,1,0:T(8,128)(2,1)}, bf16[2,128,384]{2,1,0:T(8,128)(2,1)S(1)}, u32[]{:S(2)}, u32[]{:S(2)}) collective-permute-start(bf16[2,128,384]{2,1,0:T(8,128)(2,1)} %get-tuple-element.25), channel_id=1, source_target_pairs={{0,47},{1,32},{2,33},{3,34},{4,35},{5,36},{6,37},{7,38},{8,39},{9,... | collective-permute-start | bytes 589832 | tf_op jit(solution)/shard_map/ppermute | solution.py:51
  113.6 15.9 %collective-permute-start.13 = (bf16[2,128,384]{2,1,0:T(8,128)(2,1)}, bf16[2,128,384]{2,1,0:T(8,128)(2,1)S(1)}, u32[]{:S(2)}, u32[]{:S(2)}) collective-permute-start(bf16[2,128,384]{2,1,0:T(8,128)(2,1)} %get-tuple-element.26), channel_id=1, source_target_pairs={{0,63},{1,48},{2,49},{3,50},{4,51},{5,52},{6,53},{7,54},{8,55},{9,... | collective-permute-start | bytes 589832 | tf_op jit(solution)/shard_map/ppermute | solution.py:51
  121.0 22.9 %all-to-all-start.4 = ((bf16[4,3,128,384]{3,2,1,0:T(8,128)(2,1)}), bf16[4,3,128,384]{3,2,1,0:T(8,128)(2,1)S(1)}, u32[]{:S(2)}, u32[]{:S(2)}) async-start(bf16[4,3,128,384]{3,2,1,0:T(8,128)(2,1)} %gate.1), calls=%async_computation.4 | async-start | bytes 2359296 | tf_op jit(solution)/shard_map/all_to_all | solution.py:55
  130.3 3.9 %collective-permute-start.15 = (bf16[96,384]{1,0:T(8,128)(2,1)S(1)}, bf16[96,384]{1,0:T(8,128)(2,1)S(1)}, u32[]{:S(2)}, u32[]{:S(2)}) collective-permute-start(bf16[96,384]{1,0:T(8,128)(2,1)S(1)} %get-tuple-element.32), channel_id=1, source_target_pairs={{0,128},{64,192},{128,0},{192,64},{1,129},{65,193},{129,1},{193,65... | collective-permute-start | bytes 221192 | tf_op jit(solution)/shard_map/ppermute | solution.py:51
  131.2 5.4 %collective-permute-start.16 = (bf16[96,384]{1,0:T(8,128)(2,1)S(1)}, bf16[96,384]{1,0:T(8,128)(2,1)S(1)}, u32[]{:S(2)}, u32[]{:S(2)}) collective-permute-start(bf16[96,384]{1,0:T(8,128)(2,1)S(1)} %get-tuple-element.33), channel_id=1, source_target_pairs={{0,1},{1,0},{2,3},{3,2},{4,5},{5,4},{6,7},{7,6},{8,9},{9,8},{10,11... | collective-permute-start | bytes 221192 | tf_op jit(solution)/shard_map/ppermute | solution.py:51
  134.1 5.5 %collective-permute-start.17 = (bf16[96,384]{1,0:T(8,128)(2,1)S(1)}, bf16[96,384]{1,0:T(8,128)(2,1)S(1)}, u32[]{:S(2)}, u32[]{:S(2)}) collective-permute-start(bf16[96,384]{1,0:T(8,128)(2,1)S(1)} %get-tuple-element.33), channel_id=1, source_target_pairs={{0,129},{1,128},{2,131},{3,130},{4,133},{5,132},{6,135},{7,134},{8... | collective-permute-start | bytes 221192 | tf_op jit(solution)/shard_map/ppermute | solution.py:51
  139.6 3.6 %collective-permute-start.18 = (f32[96,384]{1,0:T(8,128)S(1)}, f32[96,384]{1,0:T(8,128)S(1)}, u32[]{:S(2)}, u32[]{:S(2)}) collective-permute-start(f32[96,384]{1,0:T(8,128)S(1)} %add_add_fusion), channel_id=1, source_target_pairs={{0,64},{64,0},{128,192},{192,128},{1,65},{65,1},{129,193},{193,129... | collective-permute-start | bytes 442376 | tf_op jit(solution)/shard_map/ppermute | solution.py:51
  (4 other events, 13.1 us)

commit v3 on v1

v3 whole, which is shorter than its diff:
```python
import functools
import itertools
import math

import jax
import jax.numpy as jnp
from jax import lax
from jax.experimental import pallas as pl
from jax.experimental.pallas import tpu as pltpu
from jax.sharding import PartitionSpec as P

HDIM = 128
BF16 = jnp.bfloat16
F32 = jnp.float32
VMEM_LIMIT = 48 * 1024 * 1024
CHUNKS = 4
ACROSS = (((1,), (1,)), ((), ()))
DOWN = (((0,), (0,)), ((), ()))
PLAIN = (((1,), (0,)), ((), ()))


def dot(a, b, dims):
    return lax.dot_general(a, b, dims, preferred_element_type=F32)


def params(**kw):
    return pltpu.CompilerParams(vmem_limit_bytes=VMEM_LIMIT, **kw)


def cost(flops, size, exps=0):
    return pl.CostEstimate(flops=flops, bytes_accessed=size, transcendentals=exps)


def shift(x, axis, distance):
    n = lax.axis_size(axis)
    return lax.ppermute(x, axis, [(i, (i + distance) % n) for i in range(n)])


def routed(x, axes, target):
    sizes = [lax.axis_size(a) for a in axes]

    def index(at):
        r = 0
        for a, n in zip(axes, sizes):
            r = r * n + at[a] % n
        return r

    pairs = []
    for t in itertools.product(*[range(n) for n in sizes]):
        at = dict(zip(axes, t))
        pairs.append((index(at), index({**at, **target(at)})))
    return lax.ppermute(x, tuple(axes), pairs)


def exchange(x, axis, split):
    return lax.all_to_all(x, axis, split_axis=split, concat_axis=split, tiled=True)


SMEM = pl.BlockSpec(memory_space=pltpu.SMEM)
VMEM = pl.BlockSpec(memory_space=pltpu.VMEM)
ANY = pl.BlockSpec(memory_space=pl.ANY)


def after_those(arrays, after):
    def kernel(*refs):
        pass

    return pl.pallas_call(
        kernel,
        in_specs=[ANY] * (len(arrays) + len(after)),
        out_specs=[ANY] * len(arrays),
        out_shape=[jax.ShapeDtypeStruct(x.shape, x.dtype) for x in arrays],
        input_output_aliases={i: i for i in range(len(arrays))},
        compiler_params=params(),
        cost_estimate=cost(0, 0),
        name="gate",
    )(*arrays, *after)


def sum_kernel(at_ref, terms_ref, *refs):
    here_ref, there_ref, scr = refs[-3:]
    total = terms_ref[0].astype(F32)
    for i in range(1, terms_ref.shape[0]):
        total = total + terms_ref[i].astype(F32)
    half = here_ref.shape[0]
    scr[0] = total[:half].astype(BF16)
    scr[1] = total[half:].astype(BF16)
    here_ref[...] = scr[at_ref[3]]
    there_ref[...] = scr[1 - at_ref[3]]


def sum_terms(at, terms, after):
    steps, rows, width = terms.shape
    out = jax.ShapeDtypeStruct((rows // 2, width), BF16)
    return pl.pallas_call(
        sum_kernel,
        in_specs=[SMEM, VMEM] + [ANY] * len(after),
        out_specs=[VMEM] * 2,
        out_shape=[out, out],
        scratch_shapes=[pltpu.VMEM((2, rows // 2, width), BF16)],
        compiler_params=params(),
        cost_estimate=cost(steps * rows * width, 2 * steps * rows * width),
        name="sum_terms",
    )(at, terms, *after)


def cut_kernel(at_ref, k_ref, v_ref, q_ref, *rest):
    refs, scr = rest[:4], rest[4]
    part, width = refs[0].shape[1:]
    for s in range(4):
        cols = slice(s * width, (s + 1) * width)
        for i, ref in enumerate((k_ref, v_ref, q_ref)):
            scr[s, i] = ref[0, :, cols]
    for d in range(4):
        refs[d][...] = scr[lax.rem(at_ref[0] + d, 4)]


def cut(at, k, v, q):
    _, part, whole = q.shape
    width = whole // 4
    return pl.pallas_call(
        cut_kernel,
        in_specs=[SMEM] + [VMEM] * 3,
        out_specs=[VMEM] * 4,
        out_shape=[jax.ShapeDtypeStruct((3, part, width), BF16)] * 4,
        scratch_shapes=[pltpu.VMEM((4, 3, part, width), BF16)],
        compiler_params=params(),
        cost_estimate=cost(0, 12 * part * whole),
        name="cut",
    )(at, k, v, q)


def join_kernel(*refs):
    for d in range(4):
        refs[-2 + d // 2][d % 2] = refs[d][:2]


def join(kvq, after):
    _, part, width = kvq[0].shape
    return pl.pallas_call(
        join_kernel,
        in_specs=[VMEM] * 4 + [ANY] * len(after),
        out_specs=[VMEM] * 2,
        out_shape=[jax.ShapeDtypeStruct((2, 2, part, width), BF16)] * 2,
        compiler_params=params(),
        cost_estimate=cost(0, 32 * part * width),
        name="join",
    )(*kvq, *after)


def pieces_of(refs, plane):
    return jnp.concatenate([r[plane] for r in refs], axis=0)


def pairs_of(refs, plane):
    return jnp.concatenate([r[i, plane] for r in refs for i in range(2)], axis=0)


def piece_specs(part, planes):
    return [pl.BlockSpec((planes, part, HDIM), lambda h: (0, 0, h))] * 4


def pair_specs(part):
    return [pl.BlockSpec((2, 2, part, HDIM), lambda h: (0, 0, 0, h))] * 2


def flat_spec(n):
    return pl.BlockSpec((n, HDIM), lambda h: (0, h))


def head_spec(n):
    return pl.BlockSpec((1, n, n), lambda h: (h, 0, 0))


def forward_kernel(*refs):
    kvq, prior = refs[:4], refs[4:6]
    p_prior_ref, p_own_ref, att_ref = refs[-3:]
    q = pieces_of(kvq, 2)
    factor = HDIM**-0.5 * math.log2(math.e)
    s_prior = dot(pairs_of(prior, 0), q, ACROSS)
    s_own = dot(pieces_of(kvq, 0), q, ACROSS)
    top = jnp.maximum(
        jnp.max(s_prior, axis=0, keepdims=True), jnp.max(s_own, axis=0, keepdims=True)
    )
    e_prior = jnp.exp2((s_prior - top) * factor)
    e_own = jnp.exp2((s_own - top) * factor)
    inv = 1.0 / (
        jnp.sum(e_prior, axis=0, keepdims=True) + jnp.sum(e_own, axis=0, keepdims=True)
    )
    p_prior = (e_prior * inv).astype(BF16)
    p_own = (e_own * inv).astype(BF16)
    p_prior_ref[0] = p_prior
    p_own_ref[0] = p_own
    att_t = dot(pairs_of(prior, 1), p_prior, DOWN) + dot(pieces_of(kvq, 1), p_own, DOWN)
    att_ref[...] = att_t.T.astype(BF16)


def attention_forward(kvq, prior, after):
    _, part, width = kvq[0].shape
    heads, n = width // HDIM, 4 * part
    probs = jax.ShapeDtypeStruct((heads, n, n), BF16)
    return pl.pallas_call(
        forward_kernel,
        grid=(heads,),
        in_specs=piece_specs(part, 3) + pair_specs(part) + [ANY] * len(after),
        out_specs=[head_spec(n)] * 2 + [flat_spec(n)],
        out_shape=[probs, probs, jax.ShapeDtypeStruct((n, width), BF16)],
        compiler_params=params(),
        cost_estimate=cost(
            8 * heads * n * n * HDIM, 12 * n * width + 4 * heads * n * n, 2 * heads * n * n
        ),
        name="forward",
    )(*kvq, *prior, *after)


def backward_kernel(at_ref, *refs):
    kvq, prior, (g_ref, p_prior_ref, p_own_ref, att_ref) = refs[:4], refs[4:6], refs[6:10]
    own_ref, far = refs[-5], refs[-4:]
    q, g = pieces_of(kvq, 2), g_ref[...]
    part = kvq[0].shape[1]
    scale = HDIM**-0.5
    delta = jnp.sum((g.astype(F32) * att_ref[...].astype(F32)).T, axis=0, keepdims=True)
    dq_t = 0.0
    to = [lax.rem(at_ref[0] + 4 - d, 4) for d in range(4)]
    for side, keys, values, p_ref in (
        (0, pairs_of(prior, 0), pairs_of(prior, 1), p_prior_ref),
        (1, pieces_of(kvq, 0), pieces_of(kvq, 1), p_own_ref),
    ):
        p = p_ref[0]
        ds = (p.astype(F32) * (dot(values, g, ACROSS) - delta)).astype(BF16)
        dk = (dot(ds, q, PLAIN) * scale).astype(BF16)
        dv = dot(p, g, PLAIN).astype(BF16)
        for d in range(4):
            rows = slice(d * part, (d + 1) * part)
            for i, grad in enumerate((dk, dv)):
                if side:
                    own_ref[to[d], 1 + i] = grad[rows]
                else:
                    far[d][i] = grad[rows]
        dq_t = dq_t + dot(keys, ds, DOWN)
    dq = (dq_t * scale).T.astype(BF16)
    for d in range(4):
        own_ref[to[d], 0] = dq[d * part : (d + 1) * part]


def attention_backward(at, kvq, prior, g, p_prior, p_own, att):
    _, part, width = kvq[0].shape
    heads, n = width // HDIM, 4 * part
    out = pl.pallas_call(
        backward_kernel,
        grid=(heads,),
        in_specs=[SMEM]
        + piece_specs(part, 3)
        + pair_specs(part)
        + [flat_spec(n), head_spec(n), head_spec(n), flat_spec(n)],
        out_specs=[pl.BlockSpec((4, 3, part, HDIM), lambda h: (0, 0, 0, h))]
        + piece_specs(part, 2),
        out_shape=[jax.ShapeDtypeStruct((4, 3, part, width), BF16)]
        + [jax.ShapeDtypeStruct((2, part, width), BF16)] * 4,
        compiler_params=params(),
        cost_estimate=cost(16 * heads * n * n * HDIM, 24 * n * width + 4 * heads * n * n),
        name="backward",
    )(at, *kvq, *prior, g, p_prior, p_own, att)
    return out[0], out[1:]


def gated_kernel(dy_ref, gate_ref, *out_refs):
    half = out_refs[0].shape[0]
    for i, ref in enumerate(out_refs):
        rows = dy_ref[0, i * half : (i + 1) * half, :].astype(F32)
        ref[...] = (rows * gate_ref[...]).astype(BF16)


def gated(dy, gate):
    _, part, depth = dy.shape
    return pl.pallas_call(
        gated_kernel,
        out_shape=[jax.ShapeDtypeStruct((part // 2, depth), BF16)] * 2,
        compiler_params=params(),
        cost_estimate=cost(part * depth, 4 * part * depth),
        name="gated",
    )(dy, gate)


def weight_kernel(
    at_ref, o0, o1, a1, a2, b1, b2, a3, b3, att_ref, scaled_ref, keep_ref, send_ref
):
    core = at_ref[1]
    half = o0.shape[0]
    part = 2 * half

    def put(ref, distance, second):
        start = distance * part + second * half
        scaled_ref[start : start + ref.shape[0], :] = ref[...]

    put(o0, 0, 0)
    put(o1, 0, 1)
    put(a1, 1, 0)
    put(a2, 1, 1)
    put(b1, 3, 1)
    put(b2, 3, 0)
    put(a3, 2, 0)
    put(b3, 2, 1)
    step = 2 * keep_ref.shape[1]
    for z in range(keep_ref.shape[0]):
        columns = scaled_ref[:, z * step : (z + 1) * step]
        term = dot(columns, att_ref[...], DOWN).astype(BF16)
        rows = step // 4
        first = jnp.concatenate([term[:rows], term[2 * rows : 3 * rows]], axis=0)
        second = jnp.concatenate([term[rows : 2 * rows], term[3 * rows :]], axis=0)
        keep_ref[z] = jnp.where(core == 0, first, second)
        send_ref[z] = jnp.where(core == 0, second, first)


def weight_term(at, pieces, att, steps):
    _, depth = pieces[0].shape
    n, width = att.shape
    step = depth // steps
    per = CHUNKS
    spec = lambda r: pl.BlockSpec((r, per * step), lambda z: (0, z))
    out = pl.BlockSpec((per, step // 2, width), lambda z: (z, 0, 0))
    return pl.pallas_call(
        weight_kernel,
        grid=(steps // per,),
        in_specs=[pl.BlockSpec(memory_space=pltpu.SMEM)]
        + [spec(x.shape[0]) for x in pieces]
        + [pl.BlockSpec((n, width), lambda z: (0, 0))],
        out_specs=[spec(n), out, out],
        out_shape=[jax.ShapeDtypeStruct((n, depth), BF16)]
        + [jax.ShapeDtypeStruct((steps, step // 2, width), BF16)] * 2,
        compiler_params=params(),
        cost_estimate=cost(2 * n * depth * width, 4 * n * depth + 2 * depth * width),
        name="weight_term",
    )(at, *pieces, att)


def project_kernel(at_ref, scaled_ref, mine_ref, other_ref, g_ref, total):
    z = pl.program_id(0)
    core = at_ref[1]
    step = 2 * mine_ref.shape[1]
    term = 0.0
    for i in range(mine_ref.shape[0]):
        mine, other = mine_ref[i], other_ref[i]
        first = jnp.where(core == 0, mine, other)
        second = jnp.where(core == 0, other, mine)
        r = first.shape[0] // 2
        w = jnp.concatenate([first[:r], second[:r], first[r:], second[r:]], axis=0)
        term = term + dot(scaled_ref[:, i * step : (i + 1) * step], w, PLAIN)

    @pl.when(z == 0)
    def _():
        total[...] = term

    @pl.when(z > 0)
    def _():
        total[...] += term

    @pl.when(z == pl.num_programs(0) - 1)
    def _():
        g_ref[...] = total[...].astype(BF16)


def project(at, scaled, mine, other):
    n, depth = scaled.shape
    steps, rows, width = mine.shape
    per = CHUNKS
    w_spec = pl.BlockSpec((per, rows, width), lambda z: (z, 0, 0))
    return pl.pallas_call(
        project_kernel,
        grid=(steps // per,),
        in_specs=[
            pl.BlockSpec(memory_space=pltpu.SMEM),
            pl.BlockSpec((n, per * depth // steps), lambda z: (0, z)),
            w_spec,
            w_spec,
        ],
        out_specs=pl.BlockSpec((n, width), lambda z: (0, 0)),
        out_shape=jax.ShapeDtypeStruct((n, width), BF16),
        scratch_shapes=[pltpu.VMEM((n, width), F32)],
        compiler_params=params(),
        cost_estimate=cost(2 * n * depth * width, 2 * n * depth + 2 * depth * width),
        name="project",
    )(at, scaled, mine, other)


def assemble_kernel(at_ref, own_ref, h0, h1, h2, h3, q_ref, k_ref, v_ref, scr):
    here = at_ref[0]
    width = own_ref.shape[3]
    for d, ref in enumerate((h0, h1, h2, h3)):
        scr[lax.rem(here + d, 4)] = ref[...]
    for s in range(4):
        cols = slice(s * width, (s + 1) * width)
        q_ref[0, :, cols] = own_ref[s, 0]
        for at, ref in ((0, k_ref), (1, v_ref)):
            ref[0, :, cols] = (
                own_ref[s, 1 + at].astype(F32) + scr[s, at].astype(F32)
            ).astype(BF16)


def assemble(at, own, halos):
    u, _, part, width = own.shape
    vmem = pl.BlockSpec(memory_space=pltpu.VMEM)
    return pl.pallas_call(
        assemble_kernel,
        in_specs=[pl.BlockSpec(memory_space=pltpu.SMEM)] + [vmem] * 5,
        out_specs=[vmem] * 3,
        out_shape=[jax.ShapeDtypeStruct((1, part, u * width), BF16)] * 3,
        scratch_shapes=[pltpu.VMEM((u, 2, part, width), BF16)],
        compiler_params=params(),
        cost_estimate=cost(2 * u * part * width, 16 * u * part * width),
        name="assemble",
    )(at, own, *halos)


def shards(q_tok, k_tok, v_tok, d_y, gate, w_out):
    n_blk = lax.axis_size("blk")
    core, lower = lax.axis_index("dp") % 2, lax.axis_index("dp") // 2
    upper = lax.axis_index("blk") % 2
    at = jnp.stack([lax.axis_index("uly"), core, lower, upper]).astype(jnp.int32)
    rows = w_out.shape[0]
    z_size = n_blk // 2
    along_z = [list(range(x, n_blk, 2)) for x in range(2)]
    swap_core = lambda x: routed(x, ["dp"], lambda c: dict(dp=c["dp"] ^ 1))

    kvq = cut(at, k_tok, v_tok, q_tok)
    kvq = [kvq[0]] + [shift(kvq[d], "uly", d) for d in range(1, 4)]

    w_half = lax.dynamic_slice_in_dim(w_out, core * (rows // 2), rows // 2, axis=0)
    w_far = routed(w_half, ["blk"], lambda c: dict(blk=c["blk"] ^ 1))
    w_pair = jnp.concatenate(
        [jnp.where(upper == 0, w_half, w_far), jnp.where(upper == 0, w_far, w_half)], axis=0
    )
    (w_pair,) = after_those([w_pair], [kvq[1]])
    w_mine = lax.all_to_all(
        jnp.broadcast_to(w_pair[None], (z_size,) + w_pair.shape),
        "blk",
        split_axis=0,
        concat_axis=0,
        tiled=True,
        axis_index_groups=along_z,
    )
    dy0, dy1 = gated(d_y, gate)
    a1, b1 = shift(dy0, "uly", 1), shift(dy1, "uly", -1)

    prior = [shift(x, "blk", 1) for x in join(kvq, [])]
    a2, b2 = shift(dy1, "uly", 1), shift(dy0, "uly", -1)
    a3, b3 = shift(a1, "uly", 1), shift(b1, "uly", -1)
    w_other = swap_core(w_mine)

    p_prior, p_own, att = attention_forward(kvq, prior, [])
    scaled, keep, send = weight_term(at, (dy0, dy1, a1, a2, b1, b2, a3, b3), att, z_size)

    both = (keep.astype(F32) + swap_core(send).astype(F32)).astype(BF16)
    terms = lax.all_to_all(
        both, "blk", split_axis=0, concat_axis=0, tiled=True, axis_index_groups=along_z
    )

    g = project(at, scaled, w_mine, w_other)
    own, halos = attention_backward(at, kvq, prior, g, p_prior, p_own, att)
    halos = [
        routed(h, ["uly", "blk"], lambda c, d=d: dict(uly=c["uly"] - d, blk=c["blk"] - 1))
        for d, h in enumerate(halos)
    ]
    (own,) = after_those([own], halos[:1])
    own = exchange(own, "uly", 0)
    grad_q, grad_k, grad_v = assemble(at, own, halos)

    here, there = sum_terms(at, terms, halos)
    near_x = routed(here, ["dp"], lambda c: dict(dp=c["dp"] ^ 2))
    far_x = [
        routed(there, ["dp", "blk"], lambda c, i=i: dict(dp=c["dp"] ^ i, blk=c["blk"] ^ 1))
        for i in (0, 2)
    ]
    mine = (here.astype(F32) + near_x.astype(F32)) + (
        far_x[0].astype(F32) + far_x[1].astype(F32)
    )
    other = swap_core(mine)
    grad_w = jnp.concatenate(
        [jnp.where(core == 0, mine, other), jnp.where(core == 0, other, mine)], axis=0
    )
    return grad_q, grad_k, grad_v, grad_w


def solution(mesh):
    tokens = P("dp", ("blk", "uly"), None)
    return jax.shard_map(
        shards,
        mesh=mesh,
        in_specs=(tokens, tokens, tokens, tokens, P("dp", None), P("blk", "uly")),
        out_specs=(tokens, tokens, tokens, P("blk", "uly")),
        check_vma=False,
    )
```

time: 170 us -> 141 us (0.83)
  waiting for transfers between devices: 61.2 us -> 36.1 us
  local copies, waits for them, and re-layouts: 11.6 us -> 8.43 us
  Pallas kernels: 24.5 us -> 22.6 us
  starting transfers between devices: 68.2 us -> 70.1 us
    all_to_all x5 -> x1, starting transfers between devices: 21.1 us -> 4.28 us  [exchange(): lax.all_to_all(x, axis, split_axis=split, concat_axis=split, tiled=True)]
    ppermute x10 -> x11, starting transfers between devices: 19.1 us -> 35.6 us  [routed(): return lax.ppermute(x, tuple(axes), pairs)]
    all_to_all x5 -> x1, waiting for transfers between devices: 15.4 us -> 0.01 us  [exchange(): lax.all_to_all(x, axis, split_axis=split, concat_axis=split, tiled=True)]
    all_to_all x1, waiting for transfers between devices: 16.2 us -> 1.23 us  [shards(): lax.all_to_all(both, 'blk', split_axis=0, concat_axis=0, tiled=True, axis...]
    ppermute x8 -> x11, waiting for transfers between devices: 5.07 us -> 13 us  [shift(): return lax.ppermute(x, axis, [(i, (i + distance) % n) for i in range(n)])]
    ppermute x8 -> x11, starting transfers between devices: 12.8 us -> 16.2 us  [shift(): return lax.ppermute(x, axis, [(i, (i + distance) % n) for i in range(n)])]
    another operation x3 -> x0, local copies, waits for them, and re-layouts: 2.8 us -> none  [to_heads(): x = x[0].reshape(part, uly, width).transpose(1, 0, 2)]
    ppermute x10 -> x11, waiting for transfers between devices: 24.6 us -> 21.9 us  [routed(): return lax.ppermute(x, tuple(axes), pairs)]
  transfers between devices with their start and end apart: 25 -> 25, of which waited for: 13 -> 13; matrix products, arithmetic and copies ran while one was open for 4% -> 2% of each run, Pallas kernels for 14% -> 14%
where the time goes in v3:
time: 141 us; the launch traced here: 140 us
  starting transfers between devices  70.1 us (50%)
  waiting for transfers between devices  36.1 us (26%)
  Pallas kernels  22.6 us (16%)
  local copies, waits for them, and re-layouts  8.43 us (6%)
  other arithmetic  2.36 us (2%)
    ppermute x11, starting transfers between devices, routed(): return lax.ppermute(x, tuple(axes), pairs)  35.6 us
    ppermute x11, waiting for transfers between devices, routed(): return lax.ppermute(x, tuple(axes), pairs)  21.9 us
    ppermute x11, starting transfers between devices, shift(): return lax.ppermute(x, axis, [(i, (i + distance) % n) for i in range(n)])  16.2 us
    ppermute x11, waiting for transfers between devices, shift(): return lax.ppermute(x, axis, [(i, (i + distance) % n) for i in range(n)])  13 us
    unnamed x34, local copies, waits for them, and re-layouts  7.29 us
    all_to_all x1, starting transfers between devices, shards(): lax.all_to_all(jnp.broadcast_to(w_pair[None], (z_size,) + w_pair.shape),...  7.29 us
    all_to_all x1, starting transfers between devices, shards(): lax.all_to_all(both, 'blk', split_axis=0, concat_axis=0, tiled=True, axis...  6.67 us
    pallas_call x1, Pallas kernels, attention_backward(): pl.pallas_call(backward_kernel, grid=(heads,), in_specs=[SMEM] + piece_sp...  6.15 us
  transfers between devices with their start and end apart: 25, of which 13 were waited for; matrix products, arithmetic and copies ran while one was open for 2% of the time, Pallas kernels for 14%

profile of v3, /device:TPU:1, one launch (start us, length us, event | category | flops | bytes accessed | tf_op | source)
XLA Modules:
  0.0 140.5 jit_solution(11474921752361854565)
XLA Ops:
  4.6 2.2 %collective-permute-start = (bf16[3,128,384]{2,1,0:T(8,128)(2,1)S(1)}, bf16[3,128,384]{2,1,0:T(8,128)(2,1)S(1)}, u32[]{:S(2)}, u32[]{:S(2)}) collective-permute-start(bf16[3,128,384]{2,1,0:T(8,128)(2,1)S(1)} %get-tuple-element.29), channel_id=1, source_target_pairs={{0,16},{16,32},{32,48},{48,0},{1,17},{17,33},{33,49},{49,1},{2,18}... | collective-permute-start | bytes 884744 | tf_op jit(solution)/shard_map/ppermute | solution.py:36
  6.8 2.6 %collective-permute-start.1 = (bf16[3,128,384]{2,1,0:T(8,128)(2,1)S(1)}, bf16[3,128,384]{2,1,0:T(8,128)(2,1)S(1)}, u32[]{:S(2)}, u32[]{:S(2)}) collective-permute-start(bf16[3,128,384]{2,1,0:T(8,128)(2,1)S(1)} %get-tuple-element.30), channel_id=1, source_target_pairs={{0,32},{16,48},{32,0},{48,16},{1,33},{17,49},{33,1},{49,17},{2,34}... | collective-permute-start | bytes 884744 | tf_op jit(solution)/shard_map/ppermute | solution.py:36
  10.5 2.8 %collective-permute-start.11 = (bf16[96,384]{1,0:T(8,128)(2,1)S(1)}, bf16[96,384]{1,0:T(8,128)(2,1)S(1)}, u32[]{:S(2)}, u32[]{:S(2)}) collective-permute-start(bf16[96,384]{1,0:T(8,128)(2,1)S(1)} %constant_dynamic-slice_fusion), channel_id=1, source_target_pairs={{0,1},{1,0},{2,3},{3,2},{4,5},{5,4},{6,7},{7,6},{8,9},{9,8},{10,11... | collective-permute-start | bytes 221192 | tf_op jit(solution)/shard_map/ppermute | solution.py:52
  14.1 1.5 %collective-permute-start.5 = (bf16[64,3072]{1,0:T(8,128)(2,1)S(1)}, bf16[64,3072]{1,0:T(8,128)(2,1)}, u32[]{:S(2)}, u32[]{:S(2)}) collective-permute-start(bf16[64,3072]{1,0:T(8,128)(2,1)S(1)} %get-tuple-element.34.o0), channel_id=1, source_target_pairs={{0,16},{16,32},{32,48},{48,0},{1,17},{17,33},{33,49},{49,1},{2,18}... | collective-permute-start | bytes 1179656 | tf_op jit(solution)/shard_map/ppermute | solution.py:36
  15.6 6.6 %collective-permute-done.1.refs_2_ = bf16[3,128,384]{2,1,0:T(8,128)(2,1)S(1)} collective-permute-done((bf16[3,128,384]{2,1,0:T(8,128)(2,1)S(1)}, bf16[3,128,384]{2,1,0:T(8,128)(2,1)S(1)}, u32[]{:S(2)}, u32[]{:S(2)}) %collective-permute-start.1) | collective-permute-done | bytes 294944 | tf_op jit(solution)/shard_map/ppermute | solution.py:36
  23.1 2.7 %collective-permute-start.3 = (bf16[2,2,128,384]{3,2,1,0:T(8,128)(2,1)}, bf16[2,2,128,384]{3,2,1,0:T(8,128)(2,1)S(1)}, u32[]{:S(2)}, u32[]{:S(2)}) collective-permute-start(bf16[2,2,128,384]{3,2,1,0:T(8,128)(2,1)} %get-tuple-element.32), channel_id=1, source_target_pairs={{0,1},{1,2},{2,3},{3,4},{4,5},{5,6},{6,7},{7,8},{8,9},{9,10},{10,1... | collective-permute-start | bytes 1179656 | tf_op jit(solution)/shard_map/ppermute | solution.py:36
  25.9 1.7 %collective-permute-start.4 = (bf16[2,2,128,384]{3,2,1,0:T(8,128)(2,1)}, bf16[2,2,128,384]{3,2,1,0:T(8,128)(2,1)S(1)}, u32[]{:S(2)}, u32[]{:S(2)}) collective-permute-start(bf16[2,2,128,384]{3,2,1,0:T(8,128)(2,1)} %get-tuple-element.33), channel_id=1, source_target_pairs={{0,1},{1,2},{2,3},{3,4},{4,5},{5,6},{6,7},{7,8},{8,9},{9,10},{10,1... | collective-permute-start | bytes 1179656 | tf_op jit(solution)/shard_map/ppermute | solution.py:36
  28.7 7.3 %all-to-all-start = ((bf16[8,192,384]{2,1,0:T(8,128)(2,1)}), bf16[8,192,384]{2,1,0:T(8,128)(2,1)S(1)}, u32[]{:S(2)}, u32[]{:S(2)}) async-start(bf16[8,192,384]{2,1,0:T(8,128)(2,1)} %broadcast_in_dim.2), calls=%async_computation | async-start | bytes 2359296 | tf_op jit(solution)/shard_map/all_to_all | solution.py:434
  37.3 1.7 %collective-permute-start.8 = (bf16[64,3072]{1,0:T(8,128)(2,1)S(1)}, bf16[64,3072]{1,0:T(8,128)(2,1)S(1)}, u32[]{:S(2)}, u32[]{:S(2)}) collective-permute-start(bf16[64,3072]{1,0:T(8,128)(2,1)S(1)} %get-tuple-element.34.o0), channel_id=1, source_target_pairs={{0,48},{16,0},{32,16},{48,32},{1,49},{17,1},{33,17},{49,33},{2,50}... | collective-permute-start | bytes 1179656 | tf_op jit(solution)/shard_map/ppermute | solution.py:36
  40.5 6.0 %collective-permute-done.4.refs_5_ = bf16[2,2,128,384]{3,2,1,0:T(8,128)(2,1)S(1)} collective-permute-done((bf16[2,2,128,384]{3,2,1,0:T(8,128)(2,1)}, bf16[2,2,128,384]{3,2,1,0:T(8,128)(2,1)S(1)}, u32[]{:S(2)}, u32[]{:S(2)}) %collective-permute-start.4) | collective-permute-done | bytes 393248 | tf_op jit(solution)/shard_map/ppermute | solution.py:36
  46.5 4.1 %forward.1 = (bf16[3,512,512]{2,1,0:T(8,128)(2,1)S(1)}, bf16[3,512,512]{2,1,0:T(8,128)(2,1)S(1)}, bf16[512,384]{1,0:T(8,128)(2,1)S(1)}) custom-call(bf16[3,128,384]{2,1,0:T(8,128)(2,1)S(1)} %get-tuple-element.28.refs_0_, bf16[3,128,384]{2,1,0:T(8,128)(2,1)S(1)} %collective-permute-done.refs_1_, bf16[3,128,384]{2,1,0:T(8,128)(2,1)S(1)} %collective-permute-done.1.refs_2_, ...), custom_call_target="tpu_custom_call" | custom-call | flops 805306368 | bytes 5505024 | tf_op jit(solution)/shard_map/forward/pallas_call | solution.py:202
  53.4 4.2 %weight_term.1 = (bf16[512,3072]{1,0:T(8,128)(2,1)}, bf16[8,192,384]{2,1,0:T(8,128)(2,1)S(1)}, bf16[8,192,384]{2,1,0:T(8,128)(2,1)S(1)}) custom-call(s32[4]{0:T(128)S(1)} %pad_add_fusion.at_ref, bf16[64,3072]{1,0:T(8,128)(2,1)S(1)} %copy-done.11, bf16[64,3072]{1,0:T(8,128)(2,1)} %get-tuple-element.35.o1, bf16[64,3072]{1,0:T(8,128)(2,1)} %collective-permute-done.5.a1, ...), custom_call_target="tpu_custom_call" | custom-call | flops 1207959552 | bytes 8650752 | tf_op jit(solution)/shard_map/weight_term/pallas_call | solution.py:322
  57.5 10.3 %collective-permute-start.17 = (bf16[8,192,384]{2,1,0:T(8,128)(2,1)S(1)}, bf16[8,192,384]{2,1,0:T(8,128)(2,1)S(1)}, u32[]{:S(2)}, u32[]{:S(2)}) collective-permute-start(bf16[8,192,384]{2,1,0:T(8,128)(2,1)S(1)} %get-tuple-element.49), channel_id=1, source_target_pairs={{0,64},{64,0},{128,192},{192,128},{1,65},{65,1},{129,193},{193,129... | collective-permute-start | bytes 3538952 | tf_op jit(solution)/shard_map/ppermute | solution.py:52
  67.8 2.5 %collective-permute-done.17 = bf16[8,192,384]{2,1,0:T(8,128)(2,1)S(1)} collective-permute-done((bf16[8,192,384]{2,1,0:T(8,128)(2,1)S(1)}, bf16[8,192,384]{2,1,0:T(8,128)(2,1)S(1)}, u32[]{:S(2)}, u32[]{:S(2)}) %collective-permute-start.17) | collective-permute-done | bytes 1179680 | tf_op jit(solution)/shard_map/ppermute | solution.py:52
  71.7 6.7 %all-to-all-start.2 = ((bf16[8,192,384]{2,1,0:T(8,128)(2,1)}), bf16[8,192,384]{2,1,0:T(8,128)(2,1)S(1)}, u32[]{:S(2)}, u32[]{:S(2)}) async-start(bf16[8,192,384]{2,1,0:T(8,128)(2,1)} %add_convert_fusion), calls=%async_computation.2 | async-start | bytes 2359296 | tf_op jit(solution)/shard_map/all_to_all | solution.py:454
  79.1 2.5 %collective-permute-done.12.other_ref = bf16[8,192,384]{2,1,0:T(8,128)(2,1)S(1)} collective-permute-done((bf16[8,192,384]{2,1,0:T(8,128)(2,1)S(1)}, bf16[8,192,384]{2,1,0:T(8,128)(2,1)S(1)}, u32[]{:S(2)}, u32[]{:S(2)}) %collective-permute-start.12) | collective-permute-done | bytes 1179680 | tf_op jit(solution)/shard_map/ppermute | solution.py:52
  81.5 1.9 %copy-done = bf16[512,3072]{1,0:T(8,128)(2,1)S(1)} copy-done((bf16[512,3072]{1,0:T(8,128)(2,1)S(1)}, bf16[512,3072]{1,0:T(8,128)(2,1)}, u32[]{:S(2)}) %copy-start) | copy-done | bytes 3145752
  83.4 3.1 %project.1.refs_6_ = bf16[512,384]{1,0:T(8,128)(2,1)S(1)} custom-call(s32[4]{0:T(128)S(1)} %pad_add_fusion.at_ref, bf16[512,3072]{1,0:T(8,128)(2,1)S(1)} %copy-done, bf16[8,192,384]{2,1,0:T(8,128)(2,1)S(1)} %all-to-all-done.mine_ref, bf16[8,192,384]{2,1,0:T(8,128)(2,1)S(1)} %collective-permute-done.12.other_ref), custom_call_target="tpu_custom_call" | custom-call | flops 1207959552 | bytes 5505024 | tf_op jit(solution)/shard_map/project/pallas_call | solution.py:368
  86.6 6.2 %backward.1 = (bf16[4,3,128,384]{3,2,1,0:T(8,128)(2,1)}, bf16[2,128,384]{2,1,0:T(8,128)(2,1)S(1)}, bf16[2,128,384]{2,1,0:T(8,128)(2,1)}, bf16[2,128,384]{2,1,0:T(8,128)(2,1)}, bf16[2,128,384]{2,1,0:T(8,128)(2,1)}) custom-call(s32[4]{0:T(128)S(1)} %pad_add_fusion.at_ref, bf16[3,128,384]{2,1,0:T(8,128)(2,1)S(1)} %get-tuple-element.28.refs_0_, ...), custom_call_target="tpu_custom_call" | custom-call | flops 1610612736 | bytes 7864320 | tf_op jit(solution)/shard_map/backward/pallas_call | solution.py:249
  92.7 4.6 %collective-permute-start.13 = (bf16[2,128,384]{2,1,0:T(8,128)(2,1)S(1)}, bf16[2,128,384]{2,1,0:T(8,128)(2,1)S(1)}, u32[]{:S(2)}, u32[]{:S(2)}) collective-permute-start(bf16[2,128,384]{2,1,0:T(8,128)(2,1)S(1)} %get-tuple-element.41), channel_id=1, source_target_pairs={{0,15},{1,0},{2,1},{3,2},{4,3},{5,4},{6,5},{7,6},{8,7},{9,8},{10,9... | collective-permute-start | bytes 589832 | tf_op jit(solution)/shard_map/ppermute | solution.py:52
  97.3 2.7 %collective-permute-start.14 = (bf16[2,128,384]{2,1,0:T(8,128)(2,1)}, bf16[2,128,384]{2,1,0:T(8,128)(2,1)S(1)}, u32[]{:S(2)}, u32[]{:S(2)}) collective-permute-start(bf16[2,128,384]{2,1,0:T(8,128)(2,1)} %get-tuple-element.42), channel_id=1, source_target_pairs={{0,63},{1,48},{2,49},{3,50},{4,51},{5,52},{6,53},{7,54},{8,55},{9,... | collective-permute-start | bytes 589832 | tf_op jit(solution)/shard_map/ppermute | solution.py:52
  100.0 3.7 %collective-permute-start.15 = (bf16[2,128,384]{2,1,0:T(8,128)(2,1)}, bf16[2,128,384]{2,1,0:T(8,128)(2,1)S(1)}, u32[]{:S(2)}, u32[]{:S(2)}) collective-permute-start(bf16[2,128,384]{2,1,0:T(8,128)(2,1)} %get-tuple-element.43), channel_id=1, source_target_pairs={{0,47},{1,32},{2,33},{3,34},{4,35},{5,36},{6,37},{7,38},{8,39},{9,... | collective-permute-start | bytes 589832 | tf_op jit(solution)/shard_map/ppermute | solution.py:52
  103.8 1.6 %collective-permute-start.16 = (bf16[2,128,384]{2,1,0:T(8,128)(2,1)}, bf16[2,128,384]{2,1,0:T(8,128)(2,1)S(1)}, u32[]{:S(2)}, u32[]{:S(2)}) collective-permute-start(bf16[2,128,384]{2,1,0:T(8,128)(2,1)} %get-tuple-element.44), channel_id=1, source_target_pairs={{0,31},{1,16},{2,17},{3,18},{4,19},{5,20},{6,21},{7,22},{8,23},{9,... | collective-permute-start | bytes 589832 | tf_op jit(solution)/shard_map/ppermute | solution.py:52
  105.3 3.9 %collective-permute-done.13.refs_1_.h0.refs_0_ = bf16[2,128,384]{2,1,0:T(8,128)(2,1)S(1)} collective-permute-done((bf16[2,128,384]{2,1,0:T(8,128)(2,1)S(1)}, bf16[2,128,384]{2,1,0:T(8,128)(2,1)S(1)}, u32[]{:S(2)}, u32[]{:S(2)}) %collective-permute-start.13) | collective-permute-done | bytes 196640 | tf_op jit(solution)/shard_map/ppermute | solution.py:52
  110.5 4.3 %all-to-all-start.1 = ((bf16[4,3,128,384]{3,2,1,0:T(8,128)(2,1)}), bf16[4,3,128,384]{3,2,1,0:T(8,128)(2,1)S(1)}, u32[]{:S(2)}, u32[]{:S(2)}) async-start(bf16[4,3,128,384]{3,2,1,0:T(8,128)(2,1)} %gate.3), calls=%async_computation.1 | async-start | bytes 2359296 | tf_op jit(solution)/shard_map/all_to_all | solution.py:56
  114.8 3.0 %collective-permute-done.15.h2.refs_2_ = bf16[2,128,384]{2,1,0:T(8,128)(2,1)S(1)} collective-permute-done((bf16[2,128,384]{2,1,0:T(8,128)(2,1)}, bf16[2,128,384]{2,1,0:T(8,128)(2,1)S(1)}, u32[]{:S(2)}, u32[]{:S(2)}) %collective-permute-start.15) | collective-permute-done | bytes 196640 | tf_op jit(solution)/shard_map/ppermute | solution.py:52
  117.8 4.3 %collective-permute-done.16.h3.refs_3_ = bf16[2,128,384]{2,1,0:T(8,128)(2,1)S(1)} collective-permute-done((bf16[2,128,384]{2,1,0:T(8,128)(2,1)}, bf16[2,128,384]{2,1,0:T(8,128)(2,1)S(1)}, u32[]{:S(2)}, u32[]{:S(2)}) %collective-permute-start.16) | collective-permute-done | bytes 196640 | tf_op jit(solution)/shard_map/ppermute | solution.py:52
  124.2 4.3 %collective-permute-start.19 = (bf16[96,384]{1,0:T(8,128)(2,1)S(1)}, bf16[96,384]{1,0:T(8,128)(2,1)S(1)}, u32[]{:S(2)}, u32[]{:S(2)}) collective-permute-start(bf16[96,384]{1,0:T(8,128)(2,1)S(1)} %get-tuple-element.51), channel_id=1, source_target_pairs={{0,1},{1,0},{2,3},{3,2},{4,5},{5,4},{6,7},{7,6},{8,9},{9,8},{10,11... | collective-permute-start | bytes 221192 | tf_op jit(solution)/shard_map/ppermute | solution.py:52
  128.5 2.8 %collective-permute-done.19 = bf16[96,384]{1,0:T(8,128)(2,1)S(1)} collective-permute-done((bf16[96,384]{1,0:T(8,128)(2,1)S(1)}, bf16[96,384]{1,0:T(8,128)(2,1)S(1)}, u32[]{:S(2)}, u32[]{:S(2)}) %collective-permute-start.19) | collective-permute-done | bytes 73760 | tf_op jit(solution)/shard_map/ppermute | solution.py:52
  131.3 1.9 %collective-permute-done.20 = bf16[96,384]{1,0:T(8,128)(2,1)S(1)} collective-permute-done((bf16[96,384]{1,0:T(8,128)(2,1)S(1)}, bf16[96,384]{1,0:T(8,128)(2,1)S(1)}, u32[]{:S(2)}, u32[]{:S(2)}) %collective-permute-start.20) | collective-permute-done | bytes 73760 | tf_op jit(solution)/shard_map/ppermute | solution.py:52
  133.2 3.7 %collective-permute-start.21 = (f32[96,384]{1,0:T(8,128)S(1)}, f32[96,384]{1,0:T(8,128)S(1)}, u32[]{:S(2)}, u32[]{:S(2)}) collective-permute-start(f32[96,384]{1,0:T(8,128)S(1)} %add_add_fusion), channel_id=1, source_target_pairs={{0,64},{64,0},{128,192},{192,128},{1,65},{65,1},{129,193},{193,129... | collective-permute-start | bytes 442376 | tf_op jit(solution)/shard_map/ppermute | solution.py:52
  138.7 1.8 %assemble.1 = (bf16[1,128,1536]{2,1,0:T(8,128)(2,1)}, bf16[1,128,1536]{2,1,0:T(8,128)(2,1)}, bf16[1,128,1536]{2,1,0:T(8,128)(2,1)}) custom-call(s32[4]{0:T(128)S(1)} %pad_add_fusion.at_ref, bf16[4,3,128,384]{3,2,1,0:T(8,128)(2,1)S(1)} %all-to-all-done.1.own_ref, bf16[2,128,384]{2,1,0:T(8,128)(2,1)S(1)} %collective-permute-done.13.refs_1_.h0.refs_0_, ...), custom_call_target="tpu_custom_call" | custom-call | flops 393216 | bytes 3145728 | tf_op jit(solution)/shard_map/assemble/pallas_call | solution.py:403
  (72 shorter events, 20.6 us)
Async XLA Ops:
  0.6 12.7 %copy-start.1 = (bf16[1,128,3072]{2,1,0:T(8,128)(2,1)S(1)}, bf16[1,128,3072]{2,1,0:T(8,128)(2,1)}, u32[]{:S(2)}) copy-start(bf16[1,128,3072]{2,1,0:T(8,128)(2,1)} %dy_ref.1) | copy-start | bytes 2359300
  3.8 6.7 %copy-start.16 = (bf16[192,384]{1,0:T(8,128)(2,1)S(1)}, bf16[192,384]{1,0:T(8,128)(2,1)}, u32[]{:S(2)}) copy-start(bf16[192,384]{1,0:T(8,128)(2,1)} %param.11) | copy-start | bytes 442372
  3.8 9.5 %copy-start.5 = (f32[1,3072]{1,0:T(1,128)S(1)}, f32[1,3072]{1,0:T(1,128)}, u32[]{:S(2)}) copy-start(f32[1,3072]{1,0:T(1,128)} %gate_ref.1) | copy-start | bytes 36868
  4.6 9.6 %collective-permute-start = (bf16[3,128,384]{2,1,0:T(8,128)(2,1)S(1)}, bf16[3,128,384]{2,1,0:T(8,128)(2,1)S(1)}, u32[]{:S(2)}, u32[]{:S(2)}) collective-permute-start(bf16[3,128,384]{2,1,0:T(8,128)(2,1)S(1)} %get-tuple-element.29), channel_id=1, source_target_pairs={{0,16},{16,32},{32,48},{48,0},{1,17},{17,33},{33,49},{49,1},{2,18}... | collective-permute-start | bytes 884744 | tf_op jit(solution)/shard_map/ppermute | solution.py:36
  6.8 15.4 %collective-permute-start.1 = (bf16[3,128,384]{2,1,0:T(8,128)(2,1)S(1)}, bf16[3,128,384]{2,1,0:T(8,128)(2,1)S(1)}, u32[]{:S(2)}, u32[]{:S(2)}) collective-permute-start(bf16[3,128,384]{2,1,0:T(8,128)(2,1)S(1)} %get-tuple-element.30), channel_id=1, source_target_pairs={{0,32},{16,48},{32,0},{48,16},{1,33},{17,49},{33,1},{49,17},{2,34}... | collective-permute-start | bytes 884744 | tf_op jit(solution)/shard_map/ppermute | solution.py:36
  9.4 12.8 %collective-permute-start.2 = (bf16[3,128,384]{2,1,0:T(8,128)(2,1)S(1)}, bf16[3,128,384]{2,1,0:T(8,128)(2,1)S(1)}, u32[]{:S(2)}, u32[]{:S(2)}) collective-permute-start(bf16[3,128,384]{2,1,0:T(8,128)(2,1)S(1)} %get-tuple-element.31), channel_id=1, source_target_pairs={{0,48},{16,0},{32,16},{48,32},{1,49},{17,1},{33,17},{49,33},{2,50}... | collective-permute-start | bytes 884744 | tf_op jit(solution)/shard_map/ppermute | solution.py:36
  10.5 15.4 %collective-permute-start.11 = (bf16[96,384]{1,0:T(8,128)(2,1)S(1)}, bf16[96,384]{1,0:T(8,128)(2,1)S(1)}, u32[]{:S(2)}, u32[]{:S(2)}) collective-permute-start(bf16[96,384]{1,0:T(8,128)(2,1)S(1)} %constant_dynamic-slice_fusion), channel_id=1, source_target_pairs={{0,1},{1,0},{2,3},{3,2},{4,5},{5,4},{6,7},{7,6},{8,9},{9,8},{10,11... | collective-permute-start | bytes 221192 | tf_op jit(solution)/shard_map/ppermute | solution.py:52
  14.1 23.2 %copy-start.10 = (bf16[64,3072]{1,0:T(8,128)(2,1)}, bf16[64,3072]{1,0:T(8,128)(2,1)S(1)}, u32[]{:S(2)}) copy-start(bf16[64,3072]{1,0:T(8,128)(2,1)S(1)} %get-tuple-element.34.o0) | copy-start | bytes 1179652
  14.1 23.2 %collective-permute-start.7 = (bf16[64,3072]{1,0:T(8,128)(2,1)}, bf16[64,3072]{1,0:T(8,128)(2,1)}, u32[]{:S(2)}, u32[]{:S(2)}) collective-permute-start(bf16[64,3072]{1,0:T(8,128)(2,1)} %get-tuple-element.35.o1), channel_id=1, source_target_pairs={{0,48},{16,0},{32,16},{48,32},{1,49},{17,1},{33,17},{49,33},{2,50}... | collective-permute-start | bytes 1179656 | tf_op jit(solution)/shard_map/ppermute | solution.py:36
  14.1 24.9 %collective-permute-start.5 = (bf16[64,3072]{1,0:T(8,128)(2,1)S(1)}, bf16[64,3072]{1,0:T(8,128)(2,1)}, u32[]{:S(2)}, u32[]{:S(2)}) collective-permute-start(bf16[64,3072]{1,0:T(8,128)(2,1)S(1)} %get-tuple-element.34.o0), channel_id=1, source_target_pairs={{0,16},{16,32},{32,48},{48,0},{1,17},{17,33},{33,49},{49,1},{2,18}... | collective-permute-start | bytes 1179656 | tf_op jit(solution)/shard_map/ppermute | solution.py:36
  23.1 17.3 %collective-permute-start.3 = (bf16[2,2,128,384]{3,2,1,0:T(8,128)(2,1)}, bf16[2,2,128,384]{3,2,1,0:T(8,128)(2,1)S(1)}, u32[]{:S(2)}, u32[]{:S(2)}) collective-permute-start(bf16[2,2,128,384]{3,2,1,0:T(8,128)(2,1)} %get-tuple-element.32), channel_id=1, source_target_pairs={{0,1},{1,2},{2,3},{3,4},{4,5},{5,6},{6,7},{7,8},{8,9},{9,10},{10,1... | collective-permute-start | bytes 1179656 | tf_op jit(solution)/shard_map/ppermute | solution.py:36
  25.9 20.6 %collective-permute-start.4 = (bf16[2,2,128,384]{3,2,1,0:T(8,128)(2,1)}, bf16[2,2,128,384]{3,2,1,0:T(8,128)(2,1)S(1)}, u32[]{:S(2)}, u32[]{:S(2)}) collective-permute-start(bf16[2,2,128,384]{3,2,1,0:T(8,128)(2,1)} %get-tuple-element.33), channel_id=1, source_target_pairs={{0,1},{1,2},{2,3},{3,4},{4,5},{5,6},{6,7},{7,8},{8,9},{9,10},{10,1... | collective-permute-start | bytes 1179656 | tf_op jit(solution)/shard_map/ppermute | solution.py:36
  28.7 43.0 %all-to-all-start = ((bf16[8,192,384]{2,1,0:T(8,128)(2,1)}), bf16[8,192,384]{2,1,0:T(8,128)(2,1)S(1)}, u32[]{:S(2)}, u32[]{:S(2)}) async-start(bf16[8,192,384]{2,1,0:T(8,128)(2,1)} %broadcast_in_dim.2), calls=%async_computation | async-start | bytes 2359296 | tf_op jit(solution)/shard_map/all_to_all | solution.py:434
  36.0 17.0 %collective-permute-start.6 = (bf16[64,3072]{1,0:T(8,128)(2,1)}, bf16[64,3072]{1,0:T(8,128)(2,1)S(1)}, u32[]{:S(2)}, u32[]{:S(2)}) collective-permute-start(bf16[64,3072]{1,0:T(8,128)(2,1)} %get-tuple-element.35.o1), channel_id=1, source_target_pairs={{0,16},{16,32},{32,48},{48,0},{1,17},{17,33},{33,49},{49,1},{2,18}... | collective-permute-start | bytes 1179656 | tf_op jit(solution)/shard_map/ppermute | solution.py:36
  37.3 15.7 %collective-permute-start.8 = (bf16[64,3072]{1,0:T(8,128)(2,1)S(1)}, bf16[64,3072]{1,0:T(8,128)(2,1)S(1)}, u32[]{:S(2)}, u32[]{:S(2)}) collective-permute-start(bf16[64,3072]{1,0:T(8,128)(2,1)S(1)} %get-tuple-element.34.o0), channel_id=1, source_target_pairs={{0,48},{16,0},{32,16},{48,32},{1,49},{17,1},{33,17},{49,33},{2,50}... | collective-permute-start | bytes 1179656 | tf_op jit(solution)/shard_map/ppermute | solution.py:36
  39.0 14.4 %copy-start.11 = (bf16[64,3072]{1,0:T(8,128)(2,1)S(1)}, bf16[64,3072]{1,0:T(8,128)(2,1)}, u32[]{:S(2)}) copy-start(bf16[64,3072]{1,0:T(8,128)(2,1)} %copy-done.10) | copy-start | bytes 1179652
  39.0 14.3 %collective-permute-start.10 = (bf16[64,3072]{1,0:T(8,128)(2,1)}, bf16[64,3072]{1,0:T(8,128)(2,1)S(1)}, u32[]{:S(2)}, u32[]{:S(2)}) collective-permute-start(bf16[64,3072]{1,0:T(8,128)(2,1)} %collective-permute-done.7.b1), channel_id=1, source_target_pairs={{0,48},{16,0},{32,16},{48,32},{1,49},{17,1},{33,17},{49,33},{2,50}... | collective-permute-start | bytes 1179656 | tf_op jit(solution)/shard_map/ppermute | solution.py:36
  40.4 10.3 %copy-start.6 = (bf16[2,2,128,384]{3,2,1,0:T(8,128)(2,1)}, bf16[2,2,128,384]{3,2,1,0:T(8,128)(2,1)S(1)}, u32[]{:S(2)}) copy-start(bf16[2,2,128,384]{3,2,1,0:T(8,128)(2,1)S(1)} %collective-permute-done.3.refs_4_) | copy-start | bytes 1179652
  40.4 13.0 %collective-permute-start.9 = (bf16[64,3072]{1,0:T(8,128)(2,1)}, bf16[64,3072]{1,0:T(8,128)(2,1)S(1)}, u32[]{:S(2)}, u32[]{:S(2)}) collective-permute-start(bf16[64,3072]{1,0:T(8,128)(2,1)} %collective-permute-done.5.a1), channel_id=1, source_target_pairs={{0,16},{16,32},{32,48},{48,0},{1,17},{17,33},{33,49},{49,1},{2,18}... | collective-permute-start | bytes 1179656 | tf_op jit(solution)/shard_map/ppermute | solution.py:36
  53.0 4.6 %copy-start.14 = (bf16[512,384]{1,0:T(8,128)(2,1)}, bf16[512,384]{1,0:T(8,128)(2,1)S(1)}, u32[]{:S(2)}) copy-start(bf16[512,384]{1,0:T(8,128)(2,1)S(1)} %get-tuple-element.36.att_ref.refs_9_) | copy-start | bytes 1179652
  57.5 12.8 %collective-permute-start.17 = (bf16[8,192,384]{2,1,0:T(8,128)(2,1)S(1)}, bf16[8,192,384]{2,1,0:T(8,128)(2,1)S(1)}, u32[]{:S(2)}, u32[]{:S(2)}) collective-permute-start(bf16[8,192,384]{2,1,0:T(8,128)(2,1)S(1)} %get-tuple-element.49), channel_id=1, source_target_pairs={{0,64},{64,0},{128,192},{192,128},{1,65},{65,1},{129,193},{193,129... | collective-permute-start | bytes 3538952 | tf_op jit(solution)/shard_map/ppermute | solution.py:52
  71.7 38.8 %all-to-all-start.2 = ((bf16[8,192,384]{2,1,0:T(8,128)(2,1)}), bf16[8,192,384]{2,1,0:T(8,128)(2,1)S(1)}, u32[]{:S(2)}, u32[]{:S(2)}) async-start(bf16[8,192,384]{2,1,0:T(8,128)(2,1)} %add_convert_fusion), calls=%async_computation.2 | async-start | bytes 2359296 | tf_op jit(solution)/shard_map/all_to_all | solution.py:454
  78.4 3.1 %collective-permute-start.12 = (bf16[8,192,384]{2,1,0:T(8,128)(2,1)S(1)}, bf16[8,192,384]{2,1,0:T(8,128)(2,1)S(1)}, u32[]{:S(2)}, u32[]{:S(2)}) collective-permute-start(bf16[8,192,384]{2,1,0:T(8,128)(2,1)S(1)} %all-to-all-done.mine_ref), channel_id=1, source_target_pairs={{0,64},{64,0},{128,192},{192,128},{1,65},{65,1},{129,193},{193,129... | collective-permute-start | bytes 3538952 | tf_op jit(solution)/shard_map/ppermute | solution.py:52
  92.7 16.5 %collective-permute-start.13 = (bf16[2,128,384]{2,1,0:T(8,128)(2,1)S(1)}, bf16[2,128,384]{2,1,0:T(8,128)(2,1)S(1)}, u32[]{:S(2)}, u32[]{:S(2)}) collective-permute-start(bf16[2,128,384]{2,1,0:T(8,128)(2,1)S(1)} %get-tuple-element.41), channel_id=1, source_target_pairs={{0,15},{1,0},{2,1},{3,2},{4,3},{5,4},{6,5},{7,6},{8,7},{9,8},{10,9... | collective-permute-start | bytes 589832 | tf_op jit(solution)/shard_map/ppermute | solution.py:52
  97.3 17.4 %collective-permute-start.14 = (bf16[2,128,384]{2,1,0:T(8,128)(2,1)}, bf16[2,128,384]{2,1,0:T(8,128)(2,1)S(1)}, u32[]{:S(2)}, u32[]{:S(2)}) collective-permute-start(bf16[2,128,384]{2,1,0:T(8,128)(2,1)} %get-tuple-element.42), channel_id=1, source_target_pairs={{0,63},{1,48},{2,49},{3,50},{4,51},{5,52},{6,53},{7,54},{8,55},{9,... | collective-permute-start | bytes 589832 | tf_op jit(solution)/shard_map/ppermute | solution.py:52
  100.0 17.8 %collective-permute-start.15 = (bf16[2,128,384]{2,1,0:T(8,128)(2,1)}, bf16[2,128,384]{2,1,0:T(8,128)(2,1)S(1)}, u32[]{:S(2)}, u32[]{:S(2)}) collective-permute-start(bf16[2,128,384]{2,1,0:T(8,128)(2,1)} %get-tuple-element.43), channel_id=1, source_target_pairs={{0,47},{1,32},{2,33},{3,34},{4,35},{5,36},{6,37},{7,38},{8,39},{9,... | collective-permute-start | bytes 589832 | tf_op jit(solution)/shard_map/ppermute | solution.py:52
  103.8 18.4 %collective-permute-start.16 = (bf16[2,128,384]{2,1,0:T(8,128)(2,1)}, bf16[2,128,384]{2,1,0:T(8,128)(2,1)S(1)}, u32[]{:S(2)}, u32[]{:S(2)}) collective-permute-start(bf16[2,128,384]{2,1,0:T(8,128)(2,1)} %get-tuple-element.44), channel_id=1, source_target_pairs={{0,31},{1,16},{2,17},{3,18},{4,19},{5,20},{6,21},{7,22},{8,23},{9,... | collective-permute-start | bytes 589832 | tf_op jit(solution)/shard_map/ppermute | solution.py:52
  110.5 28.2 %all-to-all-start.1 = ((bf16[4,3,128,384]{3,2,1,0:T(8,128)(2,1)}), bf16[4,3,128,384]{3,2,1,0:T(8,128)(2,1)S(1)}, u32[]{:S(2)}, u32[]{:S(2)}) async-start(bf16[4,3,128,384]{3,2,1,0:T(8,128)(2,1)} %gate.3), calls=%async_computation.1 | async-start | bytes 2359296 | tf_op jit(solution)/shard_map/all_to_all | solution.py:56
  122.9 5.6 %collective-permute-start.18 = (bf16[96,384]{1,0:T(8,128)(2,1)S(1)}, bf16[96,384]{1,0:T(8,128)(2,1)S(1)}, u32[]{:S(2)}, u32[]{:S(2)}) collective-permute-start(bf16[96,384]{1,0:T(8,128)(2,1)S(1)} %get-tuple-element.50), channel_id=1, source_target_pairs={{0,128},{64,192},{128,0},{192,64},{1,129},{65,193},{129,1},{193,65... | collective-permute-start | bytes 221192 | tf_op jit(solution)/shard_map/ppermute | solution.py:52
  124.2 7.1 %collective-permute-start.19 = (bf16[96,384]{1,0:T(8,128)(2,1)S(1)}, bf16[96,384]{1,0:T(8,128)(2,1)S(1)}, u32[]{:S(2)}, u32[]{:S(2)}) collective-permute-start(bf16[96,384]{1,0:T(8,128)(2,1)S(1)} %get-tuple-element.51), channel_id=1, source_target_pairs={{0,1},{1,0},{2,3},{3,2},{4,5},{5,4},{6,7},{7,6},{8,9},{9,8},{10,11... | collective-permute-start | bytes 221192 | tf_op jit(solution)/shard_map/ppermute | solution.py:52
  128.5 4.7 %collective-permute-start.20 = (bf16[96,384]{1,0:T(8,128)(2,1)S(1)}, bf16[96,384]{1,0:T(8,128)(2,1)S(1)}, u32[]{:S(2)}, u32[]{:S(2)}) collective-permute-start(bf16[96,384]{1,0:T(8,128)(2,1)S(1)} %get-tuple-element.51), channel_id=1, source_target_pairs={{0,129},{1,128},{2,131},{3,130},{4,133},{5,132},{6,135},{7,134},{8... | collective-permute-start | bytes 221192 | tf_op jit(solution)/shard_map/ppermute | solution.py:52
  133.2 4.7 %collective-permute-start.21 = (f32[96,384]{1,0:T(8,128)S(1)}, f32[96,384]{1,0:T(8,128)S(1)}, u32[]{:S(2)}, u32[]{:S(2)}) collective-permute-start(f32[96,384]{1,0:T(8,128)S(1)} %add_add_fusion), channel_id=1, source_target_pairs={{0,64},{64,0},{128,192},{192,128},{1,65},{65,1},{129,193},{193,129... | collective-permute-start | bytes 442376 | tf_op jit(solution)/shard_map/ppermute | solution.py:52
  (10 other events, 20.8 us)

commit v4 on v3

--- a/solution.py
+++ b/solution.py
@@ -363,7 +363,7 @@
 def project(at, scaled, mine, other):
     n, depth = scaled.shape
     steps, rows, width = mine.shape
-    per = CHUNKS
+    per = steps
     w_spec = pl.BlockSpec((per, rows, width), lambda z: (z, 0, 0))
     return pl.pallas_call(
         project_kernel,

time: 141 us -> 141 us (level)
  no operation moved by 1% of the time
where the time goes in v4:
time: 141 us; the launch traced here: 140 us
  starting transfers between devices  70.1 us (50%)
  waiting for transfers between devices  36.5 us (26%)
  Pallas kernels  22.2 us (16%)
  local copies, waits for them, and re-layouts  8.43 us (6%)
  other arithmetic  2.36 us (2%)
    ppermute x11, starting transfers between devices, routed(): return lax.ppermute(x, tuple(axes), pairs)  35.7 us
    ppermute x11, waiting for transfers between devices, routed(): return lax.ppermute(x, tuple(axes), pairs)  22.3 us
    ppermute x11, starting transfers between devices, shift(): return lax.ppermute(x, axis, [(i, (i + distance) % n) for i in range(n)])  16.2 us
    ppermute x11, waiting for transfers between devices, shift(): return lax.ppermute(x, axis, [(i, (i + distance) % n) for i in range(n)])  13 us
    unnamed x34, local copies, waits for them, and re-layouts  7.29 us
    all_to_all x1, starting transfers between devices, shards(): lax.all_to_all(jnp.broadcast_to(w_pair[None], (z_size,) + w_pair.shape),...  7.29 us
    all_to_all x1, starting transfers between devices, shards(): lax.all_to_all(both, 'blk', split_axis=0, concat_axis=0, tiled=True, axis...  6.67 us
    pallas_call x1, Pallas kernels, attention_backward(): pl.pallas_call(backward_kernel, grid=(heads,), in_specs=[SMEM] + piece_sp...  6.16 us
  transfers between devices with their start and end apart: 25, of which 13 were waited for; matrix products, arithmetic and copies ran while one was open for 2% of the time, Pallas kernels for 14%

profile of v4, /device:TPU:1, one launch (start us, length us, event | category | flops | bytes accessed | tf_op | source)
XLA Modules:
  0.0 140.5 jit_solution(10329904529397074025)
XLA Ops:
  4.6 2.2 %collective-permute-start = (bf16[3,128,384]{2,1,0:T(8,128)(2,1)S(1)}, bf16[3,128,384]{2,1,0:T(8,128)(2,1)S(1)}, u32[]{:S(2)}, u32[]{:S(2)}) collective-permute-start(bf16[3,128,384]{2,1,0:T(8,128)(2,1)S(1)} %get-tuple-element.29), channel_id=1, source_target_pairs={{0,16},{16,32},{32,48},{48,0},{1,17},{17,33},{33,49},{49,1},{2,18}... | collective-permute-start | bytes 884744 | tf_op jit(solution)/shard_map/ppermute | solution.py:36
  6.8 2.6 %collective-permute-start.1 = (bf16[3,128,384]{2,1,0:T(8,128)(2,1)S(1)}, bf16[3,128,384]{2,1,0:T(8,128)(2,1)S(1)}, u32[]{:S(2)}, u32[]{:S(2)}) collective-permute-start(bf16[3,128,384]{2,1,0:T(8,128)(2,1)S(1)} %get-tuple-element.30), channel_id=1, source_target_pairs={{0,32},{16,48},{32,0},{48,16},{1,33},{17,49},{33,1},{49,17},{2,34}... | collective-permute-start | bytes 884744 | tf_op jit(solution)/shard_map/ppermute | solution.py:36
  10.5 2.8 %collective-permute-start.11 = (bf16[96,384]{1,0:T(8,128)(2,1)S(1)}, bf16[96,384]{1,0:T(8,128)(2,1)S(1)}, u32[]{:S(2)}, u32[]{:S(2)}) collective-permute-start(bf16[96,384]{1,0:T(8,128)(2,1)S(1)} %constant_dynamic-slice_fusion), channel_id=1, source_target_pairs={{0,1},{1,0},{2,3},{3,2},{4,5},{5,4},{6,7},{7,6},{8,9},{9,8},{10,11... | collective-permute-start | bytes 221192 | tf_op jit(solution)/shard_map/ppermute | solution.py:52
  14.1 1.5 %collective-permute-start.5 = (bf16[64,3072]{1,0:T(8,128)(2,1)S(1)}, bf16[64,3072]{1,0:T(8,128)(2,1)}, u32[]{:S(2)}, u32[]{:S(2)}) collective-permute-start(bf16[64,3072]{1,0:T(8,128)(2,1)S(1)} %get-tuple-element.34.o0), channel_id=1, source_target_pairs={{0,16},{16,32},{32,48},{48,0},{1,17},{17,33},{33,49},{49,1},{2,18}... | collective-permute-start | bytes 1179656 | tf_op jit(solution)/shard_map/ppermute | solution.py:36
  15.6 6.6 %collective-permute-done.1.refs_2_ = bf16[3,128,384]{2,1,0:T(8,128)(2,1)S(1)} collective-permute-done((bf16[3,128,384]{2,1,0:T(8,128)(2,1)S(1)}, bf16[3,128,384]{2,1,0:T(8,128)(2,1)S(1)}, u32[]{:S(2)}, u32[]{:S(2)}) %collective-permute-start.1) | collective-permute-done | bytes 294944 | tf_op jit(solution)/shard_map/ppermute | solution.py:36
  23.1 2.7 %collective-permute-start.3 = (bf16[2,2,128,384]{3,2,1,0:T(8,128)(2,1)}, bf16[2,2,128,384]{3,2,1,0:T(8,128)(2,1)S(1)}, u32[]{:S(2)}, u32[]{:S(2)}) collective-permute-start(bf16[2,2,128,384]{3,2,1,0:T(8,128)(2,1)} %get-tuple-element.32), channel_id=1, source_target_pairs={{0,1},{1,2},{2,3},{3,4},{4,5},{5,6},{6,7},{7,8},{8,9},{9,10},{10,1... | collective-permute-start | bytes 1179656 | tf_op jit(solution)/shard_map/ppermute | solution.py:36
  25.9 1.7 %collective-permute-start.4 = (bf16[2,2,128,384]{3,2,1,0:T(8,128)(2,1)}, bf16[2,2,128,384]{3,2,1,0:T(8,128)(2,1)S(1)}, u32[]{:S(2)}, u32[]{:S(2)}) collective-permute-start(bf16[2,2,128,384]{3,2,1,0:T(8,128)(2,1)} %get-tuple-element.33), channel_id=1, source_target_pairs={{0,1},{1,2},{2,3},{3,4},{4,5},{5,6},{6,7},{7,8},{8,9},{9,10},{10,1... | collective-permute-start | bytes 1179656 | tf_op jit(solution)/shard_map/ppermute | solution.py:36
  28.7 7.3 %all-to-all-start = ((bf16[8,192,384]{2,1,0:T(8,128)(2,1)}), bf16[8,192,384]{2,1,0:T(8,128)(2,1)S(1)}, u32[]{:S(2)}, u32[]{:S(2)}) async-start(bf16[8,192,384]{2,1,0:T(8,128)(2,1)} %broadcast_in_dim.2), calls=%async_computation | async-start | bytes 2359296 | tf_op jit(solution)/shard_map/all_to_all | solution.py:434
  37.3 1.7 %collective-permute-start.8 = (bf16[64,3072]{1,0:T(8,128)(2,1)S(1)}, bf16[64,3072]{1,0:T(8,128)(2,1)S(1)}, u32[]{:S(2)}, u32[]{:S(2)}) collective-permute-start(bf16[64,3072]{1,0:T(8,128)(2,1)S(1)} %get-tuple-element.34.o0), channel_id=1, source_target_pairs={{0,48},{16,0},{32,16},{48,32},{1,49},{17,1},{33,17},{49,33},{2,50}... | collective-permute-start | bytes 1179656 | tf_op jit(solution)/shard_map/ppermute | solution.py:36
  40.5 6.0 %collective-permute-done.4.refs_5_ = bf16[2,2,128,384]{3,2,1,0:T(8,128)(2,1)S(1)} collective-permute-done((bf16[2,2,128,384]{3,2,1,0:T(8,128)(2,1)}, bf16[2,2,128,384]{3,2,1,0:T(8,128)(2,1)S(1)}, u32[]{:S(2)}, u32[]{:S(2)}) %collective-permute-start.4) | collective-permute-done | bytes 393248 | tf_op jit(solution)/shard_map/ppermute | solution.py:36
  46.5 4.1 %forward.1 = (bf16[3,512,512]{2,1,0:T(8,128)(2,1)S(1)}, bf16[3,512,512]{2,1,0:T(8,128)(2,1)S(1)}, bf16[512,384]{1,0:T(8,128)(2,1)S(1)}) custom-call(bf16[3,128,384]{2,1,0:T(8,128)(2,1)S(1)} %get-tuple-element.28.refs_0_, bf16[3,128,384]{2,1,0:T(8,128)(2,1)S(1)} %collective-permute-done.refs_1_, bf16[3,128,384]{2,1,0:T(8,128)(2,1)S(1)} %collective-permute-done.1.refs_2_, ...), custom_call_target="tpu_custom_call" | custom-call | flops 805306368 | bytes 5505024 | tf_op jit(solution)/shard_map/forward/pallas_call | solution.py:202
  53.4 4.2 %weight_term.1 = (bf16[512,3072]{1,0:T(8,128)(2,1)}, bf16[8,192,384]{2,1,0:T(8,128)(2,1)S(1)}, bf16[8,192,384]{2,1,0:T(8,128)(2,1)S(1)}) custom-call(s32[4]{0:T(128)S(1)} %pad_add_fusion.at_ref, bf16[64,3072]{1,0:T(8,128)(2,1)S(1)} %copy-done.11, bf16[64,3072]{1,0:T(8,128)(2,1)} %get-tuple-element.35.o1, bf16[64,3072]{1,0:T(8,128)(2,1)} %collective-permute-done.5.a1, ...), custom_call_target="tpu_custom_call" | custom-call | flops 1207959552 | bytes 8650752 | tf_op jit(solution)/shard_map/weight_term/pallas_call | solution.py:322
  57.5 10.3 %collective-permute-start.17 = (bf16[8,192,384]{2,1,0:T(8,128)(2,1)S(1)}, bf16[8,192,384]{2,1,0:T(8,128)(2,1)S(1)}, u32[]{:S(2)}, u32[]{:S(2)}) collective-permute-start(bf16[8,192,384]{2,1,0:T(8,128)(2,1)S(1)} %get-tuple-element.49), channel_id=1, source_target_pairs={{0,64},{64,0},{128,192},{192,128},{1,65},{65,1},{129,193},{193,129... | collective-permute-start | bytes 3538952 | tf_op jit(solution)/shard_map/ppermute | solution.py:52
  67.8 2.5 %collective-permute-done.17 = bf16[8,192,384]{2,1,0:T(8,128)(2,1)S(1)} collective-permute-done((bf16[8,192,384]{2,1,0:T(8,128)(2,1)S(1)}, bf16[8,192,384]{2,1,0:T(8,128)(2,1)S(1)}, u32[]{:S(2)}, u32[]{:S(2)}) %collective-permute-start.17) | collective-permute-done | bytes 1179680 | tf_op jit(solution)/shard_map/ppermute | solution.py:52
  71.7 6.7 %all-to-all-start.2 = ((bf16[8,192,384]{2,1,0:T(8,128)(2,1)}), bf16[8,192,384]{2,1,0:T(8,128)(2,1)S(1)}, u32[]{:S(2)}, u32[]{:S(2)}) async-start(bf16[8,192,384]{2,1,0:T(8,128)(2,1)} %add_convert_fusion), calls=%async_computation.2 | async-start | bytes 2359296 | tf_op jit(solution)/shard_map/all_to_all | solution.py:454
  79.1 2.5 %collective-permute-done.12.other_ref = bf16[8,192,384]{2,1,0:T(8,128)(2,1)S(1)} collective-permute-done((bf16[8,192,384]{2,1,0:T(8,128)(2,1)S(1)}, bf16[8,192,384]{2,1,0:T(8,128)(2,1)S(1)}, u32[]{:S(2)}, u32[]{:S(2)}) %collective-permute-start.12) | collective-permute-done | bytes 1179680 | tf_op jit(solution)/shard_map/ppermute | solution.py:52
  81.5 1.9 %copy-done = bf16[512,3072]{1,0:T(8,128)(2,1)S(1)} copy-done((bf16[512,3072]{1,0:T(8,128)(2,1)S(1)}, bf16[512,3072]{1,0:T(8,128)(2,1)}, u32[]{:S(2)}) %copy-start) | copy-done | bytes 3145752
  83.4 2.7 %project.1.refs_6_ = bf16[512,384]{1,0:T(8,128)(2,1)S(1)} custom-call(s32[4]{0:T(128)S(1)} %pad_add_fusion.at_ref, bf16[512,3072]{1,0:T(8,128)(2,1)S(1)} %copy-done, bf16[8,192,384]{2,1,0:T(8,128)(2,1)S(1)} %all-to-all-done.mine_ref, bf16[8,192,384]{2,1,0:T(8,128)(2,1)S(1)} %collective-permute-done.12.other_ref), custom_call_target="tpu_custom_call" | custom-call | flops 1207959552 | bytes 5505024 | tf_op jit(solution)/shard_map/project/pallas_call | solution.py:368
  86.1 6.2 %backward.1 = (bf16[4,3,128,384]{3,2,1,0:T(8,128)(2,1)}, bf16[2,128,384]{2,1,0:T(8,128)(2,1)S(1)}, bf16[2,128,384]{2,1,0:T(8,128)(2,1)}, bf16[2,128,384]{2,1,0:T(8,128)(2,1)}, bf16[2,128,384]{2,1,0:T(8,128)(2,1)}) custom-call(s32[4]{0:T(128)S(1)} %pad_add_fusion.at_ref, bf16[3,128,384]{2,1,0:T(8,128)(2,1)S(1)} %get-tuple-element.28.refs_0_, ...), custom_call_target="tpu_custom_call" | custom-call | flops 1610612736 | bytes 7864320 | tf_op jit(solution)/shard_map/backward/pallas_call | solution.py:249
  92.3 4.6 %collective-permute-start.13 = (bf16[2,128,384]{2,1,0:T(8,128)(2,1)S(1)}, bf16[2,128,384]{2,1,0:T(8,128)(2,1)S(1)}, u32[]{:S(2)}, u32[]{:S(2)}) collective-permute-start(bf16[2,128,384]{2,1,0:T(8,128)(2,1)S(1)} %get-tuple-element.41), channel_id=1, source_target_pairs={{0,15},{1,0},{2,1},{3,2},{4,3},{5,4},{6,5},{7,6},{8,7},{9,8},{10,9... | collective-permute-start | bytes 589832 | tf_op jit(solution)/shard_map/ppermute | solution.py:52
  96.9 2.7 %collective-permute-start.14 = (bf16[2,128,384]{2,1,0:T(8,128)(2,1)}, bf16[2,128,384]{2,1,0:T(8,128)(2,1)S(1)}, u32[]{:S(2)}, u32[]{:S(2)}) collective-permute-start(bf16[2,128,384]{2,1,0:T(8,128)(2,1)} %get-tuple-element.42), channel_id=1, source_target_pairs={{0,63},{1,48},{2,49},{3,50},{4,51},{5,52},{6,53},{7,54},{8,55},{9,... | collective-permute-start | bytes 589832 | tf_op jit(solution)/shard_map/ppermute | solution.py:52
  99.6 3.7 %collective-permute-start.15 = (bf16[2,128,384]{2,1,0:T(8,128)(2,1)}, bf16[2,128,384]{2,1,0:T(8,128)(2,1)S(1)}, u32[]{:S(2)}, u32[]{:S(2)}) collective-permute-start(bf16[2,128,384]{2,1,0:T(8,128)(2,1)} %get-tuple-element.43), channel_id=1, source_target_pairs={{0,47},{1,32},{2,33},{3,34},{4,35},{5,36},{6,37},{7,38},{8,39},{9,... | collective-permute-start | bytes 589832 | tf_op jit(solution)/shard_map/ppermute | solution.py:52
  103.3 1.6 %collective-permute-start.16 = (bf16[2,128,384]{2,1,0:T(8,128)(2,1)}, bf16[2,128,384]{2,1,0:T(8,128)(2,1)S(1)}, u32[]{:S(2)}, u32[]{:S(2)}) collective-permute-start(bf16[2,128,384]{2,1,0:T(8,128)(2,1)} %get-tuple-element.44), channel_id=1, source_target_pairs={{0,31},{1,16},{2,17},{3,18},{4,19},{5,20},{6,21},{7,22},{8,23},{9,... | collective-permute-start | bytes 589832 | tf_op jit(solution)/shard_map/ppermute | solution.py:52
  104.9 4.3 %collective-permute-done.13.refs_1_.h0.refs_0_ = bf16[2,128,384]{2,1,0:T(8,128)(2,1)S(1)} collective-permute-done((bf16[2,128,384]{2,1,0:T(8,128)(2,1)S(1)}, bf16[2,128,384]{2,1,0:T(8,128)(2,1)S(1)}, u32[]{:S(2)}, u32[]{:S(2)}) %collective-permute-start.13) | collective-permute-done | bytes 196640 | tf_op jit(solution)/shard_map/ppermute | solution.py:52
  110.5 4.3 %all-to-all-start.1 = ((bf16[4,3,128,384]{3,2,1,0:T(8,128)(2,1)}), bf16[4,3,128,384]{3,2,1,0:T(8,128)(2,1)S(1)}, u32[]{:S(2)}, u32[]{:S(2)}) async-start(bf16[4,3,128,384]{3,2,1,0:T(8,128)(2,1)} %gate.3), calls=%async_computation.1 | async-start | bytes 2359296 | tf_op jit(solution)/shard_map/all_to_all | solution.py:56
  114.8 3.0 %collective-permute-done.15.h2.refs_2_ = bf16[2,128,384]{2,1,0:T(8,128)(2,1)S(1)} collective-permute-done((bf16[2,128,384]{2,1,0:T(8,128)(2,1)}, bf16[2,128,384]{2,1,0:T(8,128)(2,1)S(1)}, u32[]{:S(2)}, u32[]{:S(2)}) %collective-permute-start.15) | collective-permute-done | bytes 196640 | tf_op jit(solution)/shard_map/ppermute | solution.py:52
  117.7 4.3 %collective-permute-done.16.h3.refs_3_ = bf16[2,128,384]{2,1,0:T(8,128)(2,1)S(1)} collective-permute-done((bf16[2,128,384]{2,1,0:T(8,128)(2,1)}, bf16[2,128,384]{2,1,0:T(8,128)(2,1)S(1)}, u32[]{:S(2)}, u32[]{:S(2)}) %collective-permute-start.16) | collective-permute-done | bytes 196640 | tf_op jit(solution)/shard_map/ppermute | solution.py:52
  124.1 4.3 %collective-permute-start.19 = (bf16[96,384]{1,0:T(8,128)(2,1)S(1)}, bf16[96,384]{1,0:T(8,128)(2,1)S(1)}, u32[]{:S(2)}, u32[]{:S(2)}) collective-permute-start(bf16[96,384]{1,0:T(8,128)(2,1)S(1)} %get-tuple-element.51), channel_id=1, source_target_pairs={{0,1},{1,0},{2,3},{3,2},{4,5},{5,4},{6,7},{7,6},{8,9},{9,8},{10,11... | collective-permute-start | bytes 221192 | tf_op jit(solution)/shard_map/ppermute | solution.py:52
  128.5 2.8 %collective-permute-done.19 = bf16[96,384]{1,0:T(8,128)(2,1)S(1)} collective-permute-done((bf16[96,384]{1,0:T(8,128)(2,1)S(1)}, bf16[96,384]{1,0:T(8,128)(2,1)S(1)}, u32[]{:S(2)}, u32[]{:S(2)}) %collective-permute-start.19) | collective-permute-done | bytes 73760 | tf_op jit(solution)/shard_map/ppermute | solution.py:52
  131.3 1.9 %collective-permute-done.20 = bf16[96,384]{1,0:T(8,128)(2,1)S(1)} collective-permute-done((bf16[96,384]{1,0:T(8,128)(2,1)S(1)}, bf16[96,384]{1,0:T(8,128)(2,1)S(1)}, u32[]{:S(2)}, u32[]{:S(2)}) %collective-permute-start.20) | collective-permute-done | bytes 73760 | tf_op jit(solution)/shard_map/ppermute | solution.py:52
  133.2 3.7 %collective-permute-start.21 = (f32[96,384]{1,0:T(8,128)S(1)}, f32[96,384]{1,0:T(8,128)S(1)}, u32[]{:S(2)}, u32[]{:S(2)}) collective-permute-start(f32[96,384]{1,0:T(8,128)S(1)} %add_add_fusion), channel_id=1, source_target_pairs={{0,64},{64,0},{128,192},{192,128},{1,65},{65,1},{129,193},{193,129... | collective-permute-start | bytes 442376 | tf_op jit(solution)/shard_map/ppermute | solution.py:52
  138.7 1.8 %assemble.1 = (bf16[1,128,1536]{2,1,0:T(8,128)(2,1)}, bf16[1,128,1536]{2,1,0:T(8,128)(2,1)}, bf16[1,128,1536]{2,1,0:T(8,128)(2,1)}) custom-call(s32[4]{0:T(128)S(1)} %pad_add_fusion.at_ref, bf16[4,3,128,384]{3,2,1,0:T(8,128)(2,1)S(1)} %all-to-all-done.1.own_ref, bf16[2,128,384]{2,1,0:T(8,128)(2,1)S(1)} %collective-permute-done.13.refs_1_.h0.refs_0_, ...), custom_call_target="tpu_custom_call" | custom-call | flops 393216 | bytes 3145728 | tf_op jit(solution)/shard_map/assemble/pallas_call | solution.py:403
  (72 shorter events, 20.7 us)
Async XLA Ops:
  0.6 12.7 %copy-start.1 = (bf16[1,128,3072]{2,1,0:T(8,128)(2,1)S(1)}, bf16[1,128,3072]{2,1,0:T(8,128)(2,1)}, u32[]{:S(2)}) copy-start(bf16[1,128,3072]{2,1,0:T(8,128)(2,1)} %dy_ref.1) | copy-start | bytes 2359300
  3.8 6.7 %copy-start.16 = (bf16[192,384]{1,0:T(8,128)(2,1)S(1)}, bf16[192,384]{1,0:T(8,128)(2,1)}, u32[]{:S(2)}) copy-start(bf16[192,384]{1,0:T(8,128)(2,1)} %param.11) | copy-start | bytes 442372
  3.8 9.5 %copy-start.5 = (f32[1,3072]{1,0:T(1,128)S(1)}, f32[1,3072]{1,0:T(1,128)}, u32[]{:S(2)}) copy-start(f32[1,3072]{1,0:T(1,128)} %gate_ref.1) | copy-start | bytes 36868
  4.6 9.6 %collective-permute-start = (bf16[3,128,384]{2,1,0:T(8,128)(2,1)S(1)}, bf16[3,128,384]{2,1,0:T(8,128)(2,1)S(1)}, u32[]{:S(2)}, u32[]{:S(2)}) collective-permute-start(bf16[3,128,384]{2,1,0:T(8,128)(2,1)S(1)} %get-tuple-element.29), channel_id=1, source_target_pairs={{0,16},{16,32},{32,48},{48,0},{1,17},{17,33},{33,49},{49,1},{2,18}... | collective-permute-start | bytes 884744 | tf_op jit(solution)/shard_map/ppermute | solution.py:36
  6.8 15.4 %collective-permute-start.1 = (bf16[3,128,384]{2,1,0:T(8,128)(2,1)S(1)}, bf16[3,128,384]{2,1,0:T(8,128)(2,1)S(1)}, u32[]{:S(2)}, u32[]{:S(2)}) collective-permute-start(bf16[3,128,384]{2,1,0:T(8,128)(2,1)S(1)} %get-tuple-element.30), channel_id=1, source_target_pairs={{0,32},{16,48},{32,0},{48,16},{1,33},{17,49},{33,1},{49,17},{2,34}... | collective-permute-start | bytes 884744 | tf_op jit(solution)/shard_map/ppermute | solution.py:36
  9.4 12.8 %collective-permute-start.2 = (bf16[3,128,384]{2,1,0:T(8,128)(2,1)S(1)}, bf16[3,128,384]{2,1,0:T(8,128)(2,1)S(1)}, u32[]{:S(2)}, u32[]{:S(2)}) collective-permute-start(bf16[3,128,384]{2,1,0:T(8,128)(2,1)S(1)} %get-tuple-element.31), channel_id=1, source_target_pairs={{0,48},{16,0},{32,16},{48,32},{1,49},{17,1},{33,17},{49,33},{2,50}... | collective-permute-start | bytes 884744 | tf_op jit(solution)/shard_map/ppermute | solution.py:36
  10.5 15.4 %collective-permute-start.11 = (bf16[96,384]{1,0:T(8,128)(2,1)S(1)}, bf16[96,384]{1,0:T(8,128)(2,1)S(1)}, u32[]{:S(2)}, u32[]{:S(2)}) collective-permute-start(bf16[96,384]{1,0:T(8,128)(2,1)S(1)} %constant_dynamic-slice_fusion), channel_id=1, source_target_pairs={{0,1},{1,0},{2,3},{3,2},{4,5},{5,4},{6,7},{7,6},{8,9},{9,8},{10,11... | collective-permute-start | bytes 221192 | tf_op jit(solution)/shard_map/ppermute | solution.py:52
  14.1 23.2 %copy-start.10 = (bf16[64,3072]{1,0:T(8,128)(2,1)}, bf16[64,3072]{1,0:T(8,128)(2,1)S(1)}, u32[]{:S(2)}) copy-start(bf16[64,3072]{1,0:T(8,128)(2,1)S(1)} %get-tuple-element.34.o0) | copy-start | bytes 1179652
  14.1 23.2 %collective-permute-start.7 = (bf16[64,3072]{1,0:T(8,128)(2,1)}, bf16[64,3072]{1,0:T(8,128)(2,1)}, u32[]{:S(2)}, u32[]{:S(2)}) collective-permute-start(bf16[64,3072]{1,0:T(8,128)(2,1)} %get-tuple-element.35.o1), channel_id=1, source_target_pairs={{0,48},{16,0},{32,16},{48,32},{1,49},{17,1},{33,17},{49,33},{2,50}... | collective-permute-start | bytes 1179656 | tf_op jit(solution)/shard_map/ppermute | solution.py:36
  14.1 24.9 %collective-permute-start.5 = (bf16[64,3072]{1,0:T(8,128)(2,1)S(1)}, bf16[64,3072]{1,0:T(8,128)(2,1)}, u32[]{:S(2)}, u32[]{:S(2)}) collective-permute-start(bf16[64,3072]{1,0:T(8,128)(2,1)S(1)} %get-tuple-element.34.o0), channel_id=1, source_target_pairs={{0,16},{16,32},{32,48},{48,0},{1,17},{17,33},{33,49},{49,1},{2,18}... | collective-permute-start | bytes 1179656 | tf_op jit(solution)/shard_map/ppermute | solution.py:36
  23.1 17.3 %collective-permute-start.3 = (bf16[2,2,128,384]{3,2,1,0:T(8,128)(2,1)}, bf16[2,2,128,384]{3,2,1,0:T(8,128)(2,1)S(1)}, u32[]{:S(2)}, u32[]{:S(2)}) collective-permute-start(bf16[2,2,128,384]{3,2,1,0:T(8,128)(2,1)} %get-tuple-element.32), channel_id=1, source_target_pairs={{0,1},{1,2},{2,3},{3,4},{4,5},{5,6},{6,7},{7,8},{8,9},{9,10},{10,1... | collective-permute-start | bytes 1179656 | tf_op jit(solution)/shard_map/ppermute | solution.py:36
  25.9 20.6 %collective-permute-start.4 = (bf16[2,2,128,384]{3,2,1,0:T(8,128)(2,1)}, bf16[2,2,128,384]{3,2,1,0:T(8,128)(2,1)S(1)}, u32[]{:S(2)}, u32[]{:S(2)}) collective-permute-start(bf16[2,2,128,384]{3,2,1,0:T(8,128)(2,1)} %get-tuple-element.33), channel_id=1, source_target_pairs={{0,1},{1,2},{2,3},{3,4},{4,5},{5,6},{6,7},{7,8},{8,9},{9,10},{10,1... | collective-permute-start | bytes 1179656 | tf_op jit(solution)/shard_map/ppermute | solution.py:36
  28.7 43.0 %all-to-all-start = ((bf16[8,192,384]{2,1,0:T(8,128)(2,1)}), bf16[8,192,384]{2,1,0:T(8,128)(2,1)S(1)}, u32[]{:S(2)}, u32[]{:S(2)}) async-start(bf16[8,192,384]{2,1,0:T(8,128)(2,1)} %broadcast_in_dim.2), calls=%async_computation | async-start | bytes 2359296 | tf_op jit(solution)/shard_map/all_to_all | solution.py:434
  36.0 17.0 %collective-permute-start.6 = (bf16[64,3072]{1,0:T(8,128)(2,1)}, bf16[64,3072]{1,0:T(8,128)(2,1)S(1)}, u32[]{:S(2)}, u32[]{:S(2)}) collective-permute-start(bf16[64,3072]{1,0:T(8,128)(2,1)} %get-tuple-element.35.o1), channel_id=1, source_target_pairs={{0,16},{16,32},{32,48},{48,0},{1,17},{17,33},{33,49},{49,1},{2,18}... | collective-permute-start | bytes 1179656 | tf_op jit(solution)/shard_map/ppermute | solution.py:36
  37.3 15.7 %collective-permute-start.8 = (bf16[64,3072]{1,0:T(8,128)(2,1)S(1)}, bf16[64,3072]{1,0:T(8,128)(2,1)S(1)}, u32[]{:S(2)}, u32[]{:S(2)}) collective-permute-start(bf16[64,3072]{1,0:T(8,128)(2,1)S(1)} %get-tuple-element.34.o0), channel_id=1, source_target_pairs={{0,48},{16,0},{32,16},{48,32},{1,49},{17,1},{33,17},{49,33},{2,50}... | collective-permute-start | bytes 1179656 | tf_op jit(solution)/shard_map/ppermute | solution.py:36
  39.0 14.4 %copy-start.11 = (bf16[64,3072]{1,0:T(8,128)(2,1)S(1)}, bf16[64,3072]{1,0:T(8,128)(2,1)}, u32[]{:S(2)}) copy-start(bf16[64,3072]{1,0:T(8,128)(2,1)} %copy-done.10) | copy-start | bytes 1179652
  39.0 14.3 %collective-permute-start.10 = (bf16[64,3072]{1,0:T(8,128)(2,1)}, bf16[64,3072]{1,0:T(8,128)(2,1)S(1)}, u32[]{:S(2)}, u32[]{:S(2)}) collective-permute-start(bf16[64,3072]{1,0:T(8,128)(2,1)} %collective-permute-done.7.b1), channel_id=1, source_target_pairs={{0,48},{16,0},{32,16},{48,32},{1,49},{17,1},{33,17},{49,33},{2,50}... | collective-permute-start | bytes 1179656 | tf_op jit(solution)/shard_map/ppermute | solution.py:36
  40.4 10.3 %copy-start.6 = (bf16[2,2,128,384]{3,2,1,0:T(8,128)(2,1)}, bf16[2,2,128,384]{3,2,1,0:T(8,128)(2,1)S(1)}, u32[]{:S(2)}) copy-start(bf16[2,2,128,384]{3,2,1,0:T(8,128)(2,1)S(1)} %collective-permute-done.3.refs_4_) | copy-start | bytes 1179652
  40.4 13.0 %collective-permute-start.9 = (bf16[64,3072]{1,0:T(8,128)(2,1)}, bf16[64,3072]{1,0:T(8,128)(2,1)S(1)}, u32[]{:S(2)}, u32[]{:S(2)}) collective-permute-start(bf16[64,3072]{1,0:T(8,128)(2,1)} %collective-permute-done.5.a1), channel_id=1, source_target_pairs={{0,16},{16,32},{32,48},{48,0},{1,17},{17,33},{33,49},{49,1},{2,18}... | collective-permute-start | bytes 1179656 | tf_op jit(solution)/shard_map/ppermute | solution.py:36
  53.0 4.6 %copy-start.14 = (bf16[512,384]{1,0:T(8,128)(2,1)}, bf16[512,384]{1,0:T(8,128)(2,1)S(1)}, u32[]{:S(2)}) copy-start(bf16[512,384]{1,0:T(8,128)(2,1)S(1)} %get-tuple-element.36.att_ref.refs_9_) | copy-start | bytes 1179652
  57.5 12.8 %collective-permute-start.17 = (bf16[8,192,384]{2,1,0:T(8,128)(2,1)S(1)}, bf16[8,192,384]{2,1,0:T(8,128)(2,1)S(1)}, u32[]{:S(2)}, u32[]{:S(2)}) collective-permute-start(bf16[8,192,384]{2,1,0:T(8,128)(2,1)S(1)} %get-tuple-element.49), channel_id=1, source_target_pairs={{0,64},{64,0},{128,192},{192,128},{1,65},{65,1},{129,193},{193,129... | collective-permute-start | bytes 3538952 | tf_op jit(solution)/shard_map/ppermute | solution.py:52
  71.7 38.8 %all-to-all-start.2 = ((bf16[8,192,384]{2,1,0:T(8,128)(2,1)}), bf16[8,192,384]{2,1,0:T(8,128)(2,1)S(1)}, u32[]{:S(2)}, u32[]{:S(2)}) async-start(bf16[8,192,384]{2,1,0:T(8,128)(2,1)} %add_convert_fusion), calls=%async_computation.2 | async-start | bytes 2359296 | tf_op jit(solution)/shard_map/all_to_all | solution.py:454
  78.4 3.1 %collective-permute-start.12 = (bf16[8,192,384]{2,1,0:T(8,128)(2,1)S(1)}, bf16[8,192,384]{2,1,0:T(8,128)(2,1)S(1)}, u32[]{:S(2)}, u32[]{:S(2)}) collective-permute-start(bf16[8,192,384]{2,1,0:T(8,128)(2,1)S(1)} %all-to-all-done.mine_ref), channel_id=1, source_target_pairs={{0,64},{64,0},{128,192},{192,128},{1,65},{65,1},{129,193},{193,129... | collective-permute-start | bytes 3538952 | tf_op jit(solution)/shard_map/ppermute | solution.py:52
  92.3 16.9 %collective-permute-start.13 = (bf16[2,128,384]{2,1,0:T(8,128)(2,1)S(1)}, bf16[2,128,384]{2,1,0:T(8,128)(2,1)S(1)}, u32[]{:S(2)}, u32[]{:S(2)}) collective-permute-start(bf16[2,128,384]{2,1,0:T(8,128)(2,1)S(1)} %get-tuple-element.41), channel_id=1, source_target_pairs={{0,15},{1,0},{2,1},{3,2},{4,3},{5,4},{6,5},{7,6},{8,7},{9,8},{10,9... | collective-permute-start | bytes 589832 | tf_op jit(solution)/shard_map/ppermute | solution.py:52
  96.9 17.9 %collective-permute-start.14 = (bf16[2,128,384]{2,1,0:T(8,128)(2,1)}, bf16[2,128,384]{2,1,0:T(8,128)(2,1)S(1)}, u32[]{:S(2)}, u32[]{:S(2)}) collective-permute-start(bf16[2,128,384]{2,1,0:T(8,128)(2,1)} %get-tuple-element.42), channel_id=1, source_target_pairs={{0,63},{1,48},{2,49},{3,50},{4,51},{5,52},{6,53},{7,54},{8,55},{9,... | collective-permute-start | bytes 589832 | tf_op jit(solution)/shard_map/ppermute | solution.py:52
  99.6 18.2 %collective-permute-start.15 = (bf16[2,128,384]{2,1,0:T(8,128)(2,1)}, bf16[2,128,384]{2,1,0:T(8,128)(2,1)S(1)}, u32[]{:S(2)}, u32[]{:S(2)}) collective-permute-start(bf16[2,128,384]{2,1,0:T(8,128)(2,1)} %get-tuple-element.43), channel_id=1, source_target_pairs={{0,47},{1,32},{2,33},{3,34},{4,35},{5,36},{6,37},{7,38},{8,39},{9,... | collective-permute-start | bytes 589832 | tf_op jit(solution)/shard_map/ppermute | solution.py:52
  103.3 18.7 %collective-permute-start.16 = (bf16[2,128,384]{2,1,0:T(8,128)(2,1)}, bf16[2,128,384]{2,1,0:T(8,128)(2,1)S(1)}, u32[]{:S(2)}, u32[]{:S(2)}) collective-permute-start(bf16[2,128,384]{2,1,0:T(8,128)(2,1)} %get-tuple-element.44), channel_id=1, source_target_pairs={{0,31},{1,16},{2,17},{3,18},{4,19},{5,20},{6,21},{7,22},{8,23},{9,... | collective-permute-start | bytes 589832 | tf_op jit(solution)/shard_map/ppermute | solution.py:52
  110.5 28.2 %all-to-all-start.1 = ((bf16[4,3,128,384]{3,2,1,0:T(8,128)(2,1)}), bf16[4,3,128,384]{3,2,1,0:T(8,128)(2,1)S(1)}, u32[]{:S(2)}, u32[]{:S(2)}) async-start(bf16[4,3,128,384]{3,2,1,0:T(8,128)(2,1)} %gate.3), calls=%async_computation.1 | async-start | bytes 2359296 | tf_op jit(solution)/shard_map/all_to_all | solution.py:56
  122.8 5.6 %collective-permute-start.18 = (bf16[96,384]{1,0:T(8,128)(2,1)S(1)}, bf16[96,384]{1,0:T(8,128)(2,1)S(1)}, u32[]{:S(2)}, u32[]{:S(2)}) collective-permute-start(bf16[96,384]{1,0:T(8,128)(2,1)S(1)} %get-tuple-element.50), channel_id=1, source_target_pairs={{0,128},{64,192},{128,0},{192,64},{1,129},{65,193},{129,1},{193,65... | collective-permute-start | bytes 221192 | tf_op jit(solution)/shard_map/ppermute | solution.py:52
  124.1 7.2 %collective-permute-start.19 = (bf16[96,384]{1,0:T(8,128)(2,1)S(1)}, bf16[96,384]{1,0:T(8,128)(2,1)S(1)}, u32[]{:S(2)}, u32[]{:S(2)}) collective-permute-start(bf16[96,384]{1,0:T(8,128)(2,1)S(1)} %get-tuple-element.51), channel_id=1, source_target_pairs={{0,1},{1,0},{2,3},{3,2},{4,5},{5,4},{6,7},{7,6},{8,9},{9,8},{10,11... | collective-permute-start | bytes 221192 | tf_op jit(solution)/shard_map/ppermute | solution.py:52
  128.5 4.7 %collective-permute-start.20 = (bf16[96,384]{1,0:T(8,128)(2,1)S(1)}, bf16[96,384]{1,0:T(8,128)(2,1)S(1)}, u32[]{:S(2)}, u32[]{:S(2)}) collective-permute-start(bf16[96,384]{1,0:T(8,128)(2,1)S(1)} %get-tuple-element.51), channel_id=1, source_target_pairs={{0,129},{1,128},{2,131},{3,130},{4,133},{5,132},{6,135},{7,134},{8... | collective-permute-start | bytes 221192 | tf_op jit(solution)/shard_map/ppermute | solution.py:52
  133.2 4.7 %collective-permute-start.21 = (f32[96,384]{1,0:T(8,128)S(1)}, f32[96,384]{1,0:T(8,128)S(1)}, u32[]{:S(2)}, u32[]{:S(2)}) collective-permute-start(f32[96,384]{1,0:T(8,128)S(1)} %add_add_fusion), channel_id=1, source_target_pairs={{0,64},{64,0},{128,192},{192,128},{1,65},{65,1},{129,193},{193,129... | collective-permute-start | bytes 442376 | tf_op jit(solution)/shard_map/ppermute | solution.py:52
  (10 other events, 19.4 us)
